TPU v7x, 512 devices: a whole 4x8x8 slice. The times are simulated.
512 devices in a mesh: dp: 32 (over x, y), seq: 16 (over z, core).
Axes of the slice: x: 4, y: 8, z: 8, core: 2. Of those that a mesh axis runs over, the one named last changes fastest.
Arguments:
- queries: bfloat16 [32, 2048, 2048], P('dp', 'seq'), may hold values from -8 to 8
- keys: bfloat16 [32, 2048, 1024], P('dp', 'seq'), may hold values from -8 to 8
- values: bfloat16 [32, 2048, 1024], P('dp', 'seq'), may hold values from -6 to 6
- cotangent: bfloat16 [32, 2048, 2048], P('dp', 'seq'), may hold values from -6 to 6
- out_weight: bfloat16 [2048, 2048], P('seq'), may hold values from -0.125 to 0.125
- segment: int32 [32, 2048], P('dp', 'seq'), may hold values from 0 to 23, as said below
- row_type: int32 [32, 2048], P('dp', 'seq'), may hold values from 0 to 2, as said below
- pair_index: int32 [32, 24], P('dp'), may hold values from 0 to 7, as said below
Outputs:
- query_grad: bfloat16 [32, 2048, 2048], P('dp', 'seq')
- key_grad: bfloat16 [32, 2048, 1024], P('dp', 'seq')
- value_grad: bfloat16 [32, 2048, 1024], P('dp', 'seq')
- weight_grad: float32 [2048, 2048], P('seq', 'dp')
Inputs may be any that keep to these rules, and one draw needn't show every extreme that they name: In each row the segment numbers never fall and each segment holds one or more tokens; segments come in groups of six: the prompts of two pairs, then the chosen and rejected responses of those two pairs in any order; the six segments of group g fill exactly the tokens g * 512 to (g + 1) * 512 - 1. `row_type`: all tokens of a segment have one type. `pair_index`: each pair has one prompt segment, one chosen and one rejected segment, the prompt before both responses.
All inputs are finite; a program needn't handle non-finite values.
Results may differ from a plain program's by a relative error of at most 0.035.
Values may be sent and summed in bfloat16 or wider, within the bound.
No kernel may reach another device: no remote copies, remote signals or barrier semaphores. Data moves between devices by JAX's collectives and lax.ppermute only.
A program may use at most 64 MiB of HBM per device.

v0:
```python
import jax
import jax.numpy as jnp
from jax import lax
from jax.sharding import PartitionSpec as P

HD = 128


def contract_last(left, right):
    return lax.dot_general(
        left, right, (((1,), (1,)), ((), ())), preferred_element_type=jnp.float32
    )


def contract_first(left, right):
    return lax.dot_general(
        left, right, (((0,), (0,)), ((), ())), preferred_element_type=jnp.float32
    )


def local(queries, keys, values, cotangent, out_weight, segment, row_type, pair_index):
    score_scale = HD ** (-0.5)
    tokens_dev = queries.shape[1]
    seq_count = lax.axis_size("seq")
    length = tokens_dev * seq_count
    head_dim = out_weight.shape[0]
    kv_width = keys.shape[2]
    kv_heads = kv_width // head_dim
    segment_all, type_all = (
        lax.all_gather(segment, "seq", axis=1, tiled=True),
        lax.all_gather(row_type, "seq", axis=1, tiled=True),
    )
    segment_all = segment_all[0]
    type_all = type_all[0]
    matches = segment_all[:, None] == jnp.arange(pair_index.shape[1])[None, :]
    pair_all = jnp.sum(jnp.where(matches, pair_index[0][None, :], 0), axis=1)
    key_wide = jnp.repeat(keys.reshape(1, tokens_dev, kv_heads, head_dim), 2, axis=2).reshape(
        1, tokens_dev, 2 * kv_width
    )
    value_wide = jnp.repeat(values.reshape(1, tokens_dev, kv_heads, head_dim), 2, axis=2).reshape(
        1, tokens_dev, 2 * kv_width
    )
    arrived = lax.all_to_all(
        jnp.stack([queries, key_wide, value_wide]), "seq", split_axis=3, concat_axis=2, tiled=True
    )
    query_head = arrived[0, 0]
    key_head = arrived[1, 0]
    value_head = arrived[2, 0]
    piece_rows = lax.all_gather(cotangent, "seq", axis=1, tiled=True)[0]
    projected = contract_last(piece_rows, out_weight).astype(jnp.bfloat16)
    gathered = piece_rows
    grad_head, gathered = (projected, gathered)
    window_count = pair_index.shape[1] // 6
    block_rows = length // window_count
    local_pos = jnp.arange(block_rows)
    causal = local_pos[None, :] <= local_pos[:, None]
    output_parts = []
    query_parts = []
    key_parts = []
    value_parts = []
    for row_block in range(window_count):
        first_row = row_block * block_rows
        finish = first_row + block_rows
        query_block = query_head[first_row:finish]
        key_block = key_head[first_row:finish]
        value_block = value_head[first_row:finish]
        segment_block = segment_all[first_row:finish]
        type_block = type_all[first_row:finish]
        pair_block = pair_all[first_row:finish]
        scores = contract_last(query_block, key_block) * score_scale
        same_segment = segment_block[:, None] == segment_block[None, :]
        from_prompt = (
            (type_block[None, :] == 0)
            & (type_block[:, None] != 0)
            & (pair_block[:, None] == pair_block[None, :])
        )
        allowed = causal & (same_segment | from_prompt)
        row_max = jnp.max(jnp.where(allowed, scores, -jnp.inf), axis=-1, keepdims=True)
        exponent = jnp.where(allowed, jnp.exp(scores - row_max), 0.0)
        attend = exponent / jnp.sum(exponent, axis=-1, keepdims=True)
        attend_low = attend.astype(jnp.bfloat16)
        output_block = jnp.dot(attend_low, value_block, preferred_element_type=jnp.float32).astype(
            jnp.bfloat16
        )
        grad_block = grad_head[first_row:finish]
        row_delta = jnp.sum(
            grad_block.astype(jnp.float32) * output_block.astype(jnp.float32),
            axis=-1,
            keepdims=True,
        )
        grad_attend = contract_last(grad_block, value_block)
        grad_scores = (attend * (grad_attend - row_delta) * score_scale).astype(jnp.bfloat16)
        output_parts.append(output_block)
        query_parts.append(
            jnp.dot(grad_scores, key_block, preferred_element_type=jnp.float32).astype(jnp.bfloat16)
        )
        key_parts.append(contract_first(grad_scores, query_block).astype(jnp.bfloat16))
        value_parts.append(contract_first(attend_low, grad_block).astype(jnp.bfloat16))
    output_head = jnp.concatenate(output_parts, axis=0)
    grad_query = jnp.concatenate(query_parts, axis=0)
    key_part = jnp.concatenate(key_parts, axis=0)
    value_part = jnp.concatenate(value_parts, axis=0)
    weight_total = contract_first(output_head, gathered)
    returned = lax.all_to_all(
        jnp.stack([grad_query, key_part, value_part])[:, None],
        "seq",
        split_axis=2,
        concat_axis=3,
        tiled=True,
    )
    query_grad = returned[0]
    summed = jnp.sum(
        returned[1:].astype(jnp.float32).reshape(2, 1, tokens_dev, kv_heads, 2, head_dim), axis=4
    )
    summed = summed.reshape(2, 1, tokens_dev, kv_width).astype(jnp.bfloat16)
    key_grad = summed[0]
    value_grad = summed[1]
    weight_grad = lax.psum_scatter(
        weight_total.astype(jnp.bfloat16), "dp", scatter_dimension=1, tiled=True
    ).astype(jnp.float32)
    return (query_grad, key_grad, value_grad, weight_grad)


def solution(mesh):
    in_specs = (
        P("dp", "seq", None),
        P("dp", "seq", None),
        P("dp", "seq", None),
        P("dp", "seq", None),
        P("seq", None),
        P("dp", "seq"),
        P("dp", "seq"),
        P("dp", None),
    )
    out_specs = (P("dp", "seq", None), P("dp", "seq", None), P("dp", "seq", None), P("seq", "dp"))
    return jax.shard_map(local, mesh=mesh, in_specs=in_specs, out_specs=out_specs, check_vma=False)
```

profile of v0, /device:TPU:1, one launch (start us, length us, event | category | flops | bytes accessed | tf_op | source)
XLA Modules:
  0.0 401.9 jit_solution(9199330850330098165)
XLA Ops:
  7.2 0.7 all-gather.2.cloned.1.call-update
  7.9 1.1 copy.155
  9.2 0.2 copy.116
  9.4 0.2 copy.156
  9.7 0.2 copy.117
  9.9 1.2 pad_maximum_fusion
  11.1 2.6 copy.118
  13.7 12.0 %all-to-all-start = ((bf16[3,1,128,2048]{2,0,1,3:T(4,128)(2,1)}), bf16[3,1,128,2048]{2,0,1,3:T(4,128)(2,1)S(1)}, u32[]{:S(2)}, u32[]{:S(2)}) async-start(bf16[3,1,128,2048]{2,0,1,3:T(4,128)(2,1)} %copy.118), calls=%async_computation | async-start | bytes 4194304 | tf_op jit(solution)/shard_map/all_to_all | solution.py:43
  25.7 79.3 %all_gather.10 = s32[1,2048]{1,0:T(1,128)S(1)} all-gather(s32[1,128]{1,0:T(1,128)S(1)} %copy-done.23), channel_id=1, replica_groups=mesh['dp'=32,'seq'=16] {'seq'}, dimensions={1}, use_global_device_ids=true | all-gather | bytes 8704 | tf_op jit(solution)/shard_map/all_gather | solution.py:31
  105.0 15.3 %all_gather.9 = s32[1,2048]{1,0:T(1,128)S(1)} all-gather(s32[1,128]{1,0:T(1,128)S(1)} %copy-done.24), channel_id=1, replica_groups=mesh['dp'=32,'seq'=16] {'seq'}, dimensions={1}, use_global_device_ids=true | all-gather | bytes 8704 | tf_op jit(solution)/shard_map/all_gather | solution.py:30
  120.5 0.2 copy.119
  120.8 0.1 copy.135
  121.5 0.1 copy.132
  121.7 0.1 copy.125
  122.4 0.1 copy.122
  122.5 0.4 select_reduce_fusion
  123.0 0.4 fusion.33
  123.4 0.4 select_reduce_fusion.1
  123.8 0.4 fusion.31
  124.2 0.4 select_reduce_fusion.2
  124.7 0.4 fusion.29
  125.1 0.4 select_reduce_fusion.3
  125.5 0.4 fusion.27
  125.9 1.7 fusion.30
  127.6 0.3 convolution_convert_fusion.9
  127.8 0.3 convolution_convert_fusion.11
  128.1 2.3 fusion.26
  130.4 1.1 copy-done.1
  131.5 0.3 convolution_convert_fusion.13
  131.8 6.3 %fusion.4 = bf16[2048,128]{0,1:T(8,128)(2,1)S(1)} fusion(bf16[128,2048]{1,0:T(8,128)(2,1)S(1)} %copy-done, bf16[1,2048,2048]{2,1,0:T(8,128)(2,1)} %all-gather.2.cloned.1.call-done), kind=kOutput, calls=%fused_computation.4 | convolution fusion | flops 1074003968 | bytes 9437184 | tf_op jit(solution)/shard_map/dot_general | solution.py:10
  138.1 1.0 multiply_reduce_fusion.3
  139.1 0.3 fusion.21
  139.4 0.3 convolution_convert_fusion.14
  139.8 0.2 copy-done.18
  140.0 0.3 convolution_convert_fusion.7
  140.4 0.3 fusion.20
  140.7 0.3 convolution_convert_fusion.12
  141.1 0.3 convolution_convert_fusion.6
  141.4 0.3 fusion.19
  141.7 0.4 convolution_convert_fusion.10
  142.1 0.3 convolution_convert_fusion.5
  142.4 0.3 fusion.18
  142.7 0.4 convolution_convert_fusion.8
  143.1 0.3 convolution_convert_fusion.4
  143.3 0.3 convolution_convert_fusion.3
  143.7 0.3 convolution_convert_fusion.2
  144.0 0.3 convolution_convert_fusion
  144.3 0.3 convolution_convert_fusion.1
  144.7 0.2 maximum_bitcast_fusion
  144.9 10.9 %copy.140 = bf16[3,1,2048,128]{3,0,1,2:T(4,128)(2,1)} copy(bf16[3,1,2048,128]{3,2,0,1:T(8,128)(2,1)S(1)} %maximum_bitcast_fusion) | data formatting | bytes 3145728 | tf_op jit(solution)/shard_map/broadcast_in_dim | solution.py:105
  155.8 4.8 %all-to-all-start.1 = ((bf16[3,1,2048,128]{3,0,1,2:T(4,128)(2,1)}), bf16[3,1,2048,128]{3,0,1,2:T(4,128)(2,1)S(1)}, u32[]{:S(2)}, u32[]{:S(2)}) async-start(bf16[3,1,2048,128]{3,0,1,2:T(4,128)(2,1)} %copy.140), calls=%async_computation.1 | async-start | bytes 4194304 | tf_op jit(solution)/shard_map/all_to_all | solution.py:104
  160.7 0.3 reduce-scatter.2.cloned.1.call-start
  161.0 7.5 %fusion.7 = bf16[128,2048]{0,1:T(8,128)(2,1)} fusion(bf16[1,2048,2048]{2,1,0:T(8,128)(2,1)} %all-gather.2.cloned.1.call-done, bf16[512,128]{0,1:T(8,128)(2,1)S(1)} %convolution_convert_fusion.9, bf16[512,128]{0,1:T(8,128)(2,1)S(1)} %convolution_convert_fusion.11, bf16[512,128]{0,1:T(8,128)(2,1)S(1)} %convolution_convert_fusion.13, ...), kind=kOutput, calls=%fused_computation.5 | convolution fusion | flops 1076101120 | bytes 9437184 | tf_op jit(solution)/shard_map/dot_general | solution.py:16
  168.6 214.0 %reduce-scatter.2.cloned.1.call-done = bf16[128,64]{0,1:T(8,128)(2,1)} async-done(((bf16[128,2048]{0,1:T(8,128)(2,1)}), bf16[128,64]{0,1:T(8,128)(2,1)}) %reduce-scatter.2.cloned.1.call-update) | async-done | bytes 16400 | tf_op jit(solution)/shard_map/reduce_scatter | solution.py:118
  382.6 1.3 convert_element_type.172
  383.9 2.3 slice.235
  386.2 1.8 slice.234
  388.0 3.1 reduce.3
  391.3 0.2 copy.143
  391.5 0.9 copy.145
  392.3 0.2 copy.144
  392.5 0.9 copy.146
  393.4 0.6 copy.141
  394.0 1.0 squeeze.18
  (75 shorter events, 2.1 us)
Async XLA Ops:
  7.2 124.6 %copy-start = (bf16[128,2048]{1,0:T(8,128)(2,1)S(1)}, bf16[128,2048]{1,0:T(8,128)(2,1)}, u32[]{:S(2)}) copy-start(bf16[128,2048]{1,0:T(8,128)(2,1)} %param.12) | copy-start | bytes 1572868
  7.2 2.2 copy-start.21
  7.2 124.6 %all-gather.2.cloned.1.call-start = ((), (), s32[]{:S(2)}) async-start(), calls=%async_computation.3 | async-start | bytes 8912896 | tf_op jit(solution)/shard_map/all_gather | solution.py:49
  13.7 12.0 %copy-start.23 = (s32[1,128]{1,0:T(1,128)S(1)}, s32[1,128]{1,0:T(1,128)}, u32[]{:S(2)}) copy-start(s32[1,128]{1,0:T(1,128)} %param.14) | copy-start | bytes 1540
  13.7 91.3 %copy-start.24 = (s32[1,128]{1,0:T(1,128)S(1)}, s32[1,128]{1,0:T(1,128)}, u32[]{:S(2)}) copy-start(s32[1,128]{1,0:T(1,128)} %param.13) | copy-start | bytes 1540
  13.7 106.6 %copy-start.25 = (s32[1,24]{1,0:T(1,128)S(1)}, s32[1,24]{1,0:T(1,128)}, u32[]{:S(2)}) copy-start(s32[1,24]{1,0:T(1,128)} %param.15) | copy-start | bytes 292
  13.7 106.8 %all-to-all-start = ((bf16[3,1,128,2048]{2,0,1,3:T(4,128)(2,1)}), bf16[3,1,128,2048]{2,0,1,3:T(4,128)(2,1)S(1)}, u32[]{:S(2)}, u32[]{:S(2)}) async-start(bf16[3,1,128,2048]{2,0,1,3:T(4,128)(2,1)} %copy.118), calls=%async_computation | async-start | bytes 4194304 | tf_op jit(solution)/shard_map/all_to_all | solution.py:43
  120.9 2.0 copy-start.5
  121.1 1.9 copy-start.7
  121.2 2.1 copy-start.9
  121.4 2.0 copy-start.11
  121.8 2.4 copy-start.13
  122.0 2.3 copy-start.15
  122.1 3.0 copy-start.17
  122.3 2.8 copy-start.19
  130.4 1.1 copy-start.1
  131.8 6.4 %copy-start.3 = (f32[512,512]{0,1:T(8,128)S(1)}, f32[512,512]{0,1:T(8,128)}, u32[]{:S(2)}) copy-start(f32[512,512]{0,1:T(8,128)} %get-tuple-element.55) | copy-start | bytes 3145732
  138.1 1.3 copy-start.20
  139.1 0.9 copy-start.18
  139.1 1.3 copy-start.2
  139.4 1.3 copy-start.16
  140.0 1.1 copy-start.14
  140.7 1.0 copy-start.12
  141.1 1.0 copy-start.10
  141.7 1.0 copy-start.8
  142.1 1.0 copy-start.6
  155.8 5.2 %copy-start.22 = (bf16[512,128]{0,1:T(8,128)(2,1)S(1)}, bf16[512,128]{0,1:T(8,128)(2,1)}, u32[]{:S(2)}) copy-start(bf16[512,128]{0,1:T(8,128)(2,1)} %get-tuple-element.54) | copy-start | bytes 393220
  155.8 228.1 %all-to-all-start.1 = ((bf16[3,1,2048,128]{3,0,1,2:T(4,128)(2,1)}), bf16[3,1,2048,128]{3,0,1,2:T(4,128)(2,1)S(1)}, u32[]{:S(2)}, u32[]{:S(2)}) async-start(bf16[3,1,2048,128]{3,0,1,2:T(4,128)(2,1)} %copy.140), calls=%async_computation.1 | async-start | bytes 4194304 | tf_op jit(solution)/shard_map/all_to_all | solution.py:104
  160.7 221.9 %reduce-scatter.2.cloned.1.call-start = ((), (), s32[]{:S(2)}) async-start(), calls=%async_computation.4 | async-start | bytes 540672 | tf_op jit(solution)/shard_map/reduce_scatter | solution.py:118
  391.2 2.1 copy-start.4
Sparse Core Ops, SparseCore 0:
  10.1 105.7 all-gather.1
  168.7 213.8 reduce-scatter.1
where the time goes:
time: 407 us; the launch traced here: 402 us
  waiting for transfers between devices  215 us (53%)
  blocking collectives  94.6 us (23%)
  local copies, waits for them, and re-layouts  26.8 us (7%)
  matrix products  22.3 us (5%)
  starting transfers between devices  17.1 us (4%)
  between operations  14.7 us (4%)
  other arithmetic  11.6 us (3%)
    reduce_scatter x1, waiting for transfers between devices, local(): lax.psum_scatter(weight_total.astype(jnp.bfloat16), 'dp', scatter_dimensi...  214 us
    all_gather x1, blocking collectives, local(): lax.all_gather(row_type, 'seq', axis=1, tiled=True)  79.3 us
    all_gather x1, blocking collectives, local(): lax.all_gather(segment, 'seq', axis=1, tiled=True)  15.3 us
    all_to_all x1, starting transfers between devices, local(): lax.all_to_all(jnp.stack([queries, key_wide, value_wide]), 'seq', split_a...  12 us
    broadcast_in_dim x1, local copies, waits for them, and re-layouts, local(): jnp.stack([grad_query, key_part, value_part])[:, None]  10.9 us
    dot_general x9, matrix products, contract_first(): lax.dot_general(left, right, (((0,), (0,)), ((), ())), preferred_element_...  9.92 us
    dot_general x9, matrix products, contract_last(): lax.dot_general(left, right, (((1,), (1,)), ((), ())), preferred_element_...  9.19 us
  transfers between devices with their start and end apart: 4, of which 1 were waited for; matrix products, arithmetic and copies ran while one was open for 6% of the time, Pallas kernels for 0%

commit v1 on v0

v1 whole, which is shorter than its diff:
```python
import itertools

import jax
import jax.numpy as jnp
import numpy as np
from jax import lax
from jax.experimental import pallas as pl
from jax.experimental.pallas import tpu as pltpu
from jax.sharding import Mesh
from jax.sharding import PartitionSpec as P

HD = 128
WINDOW = 512
TOK = 128
AXES = ("xh", "xl", "y", "w", "p", "c")
SIZES = (2, 2, 8, 4, 2, 2)
NEAR = ("xl", "p", "c")
FAR = ("xh", "y", "w")
CODE = 16
PAY = 4 * TOK + CODE
NONE = 99
F32 = jnp.float32
BF16 = jnp.bfloat16


def place(*index):
    return int(np.ravel_multi_index(index, SIZES))


def weight_moves(turn):
    moves = []
    for xh, xl, y, w, p, c in itertools.product(*map(range, SIZES)):
        head = 2 * (4 * xl + 2 * p + c) + (w + turn) % 2
        source = place(xh, w // 2, y, head // 4, (head // 2) % 2, head % 2)
        moves.append((source, place(xh, xl, y, w, p, c)))
    return moves


def dot(left, right, dims):
    return lax.dot_general(left, right, (dims, ((), ())), preferred_element_type=F32)


def pack_kernel(q_ref, k_ref, v_ref, seg_ref, type_ref, pair_ref, out_ref):
    for g in range(8):
        out_ref[g, 0:TOK, :] = q_ref[0, :, 2 * g * HD : (2 * g + 1) * HD]
        out_ref[g, TOK : 2 * TOK, :] = q_ref[0, :, (2 * g + 1) * HD : (2 * g + 2) * HD]
        out_ref[g, 2 * TOK : 3 * TOK, :] = k_ref[0, :, g * HD : (g + 1) * HD]
        out_ref[g, 3 * TOK : 4 * TOK, :] = v_ref[0, :, g * HD : (g + 1) * HD]
    seg = seg_ref[...]
    kind = type_ref[...]
    pair = jnp.zeros_like(seg)
    count = pair_ref.shape[1]
    for s in range(count):
        pair = jnp.where(seg == s, pair_ref[0, s], pair)
    as_query = jnp.where(kind != 0, count + pair, NONE)
    as_key = jnp.where(kind == 0, count + pair, NONE)
    row = lax.broadcasted_iota(jnp.int32, (CODE, TOK), 0)
    code = jnp.where(row == 0, seg, jnp.where(row == 1, as_query, jnp.where(row == 2, as_key, 0)))
    code = code.astype(F32).astype(BF16)
    for g in range(8):
        out_ref[g, 4 * TOK :, :] = code


def main_kernel(odd_ref, pay_ref, cot_ref, w0_ref, w1_ref, ret_ref, wg_ref, wbuf, ghbuf, obuf, wacc):
    unit = pl.program_id(0)
    scale = HD ** (-0.5)

    @pl.when(unit == 0)
    def _():
        odd = odd_ref[0]
        wbuf[pl.ds(pl.multiple_of(odd * HD, HD), HD), :] = w0_ref[...]
        wbuf[pl.ds(pl.multiple_of((1 - odd) * HD, HD), HD), :] = w1_ref[...]

    ghbuf[...] = dot(cot_ref[...], wbuf[...], ((1,), (1,))).astype(BF16)

    def rows(first):
        return pay_ref[:, first : first + TOK, :].reshape(WINDOW, HD)

    key = rows(2 * TOK)
    value = rows(3 * TOK)
    code = jnp.concatenate([pay_ref[i, 4 * TOK :, :] for i in range(4)], axis=1)
    code = code.astype(F32)[0:8]
    slot = lax.broadcasted_iota(jnp.int32, (32, WINDOW), 0).astype(F32)
    seg_hot = slot == code[0:1]
    want = jnp.where(seg_hot | (slot == code[1:2]), 1.0, 0.0).astype(BF16)
    have = jnp.where(seg_hot | (slot == code[2:3]), 1.0, 0.0).astype(BF16)

    half = WINDOW // 2
    kparts = [[None, None], [None, None]]
    vparts = [[None, None], [None, None]]
    for block in range(2):
        lo = block * half
        ext = lo + half
        count = dot(want[:, lo:ext], have[:, :ext], ((0,), (0,)))
        t_pos = lax.broadcasted_iota(jnp.int32, (half, ext), 0) + lo
        s_pos = lax.broadcasted_iota(jnp.int32, (half, ext), 1)
        visible = (count > 0.5) & (s_pos <= t_pos)
        for b in range(2):
            query = rows(b * TOK)[lo:ext]
            grad = ghbuf[lo:ext, b * HD : (b + 1) * HD]
            scores = dot(query, key[:ext], ((1,), (1,))) * scale
            scores = jnp.where(visible, scores, -jnp.inf)
            top = jnp.max(scores, axis=-1, keepdims=True)
            exponent = jnp.exp(scores - top)
            attend = exponent * (1.0 / jnp.sum(exponent, axis=-1, keepdims=True))
            low = attend.astype(BF16)
            out = dot(low, value[:ext], ((1,), (0,))).astype(BF16)
            obuf[lo:ext, b * HD : (b + 1) * HD] = out
            delta = jnp.sum(grad.astype(F32) * out.astype(F32), axis=-1, keepdims=True)
            grad_attend = dot(grad, value[:ext], ((1,), (1,)))
            ds = (attend * (grad_attend - delta) * scale).astype(BF16)
            dq = dot(ds, key[:ext], ((1,), (0,))).astype(BF16)
            ret_ref[2 * block : 2 * block + 2, b * TOK : (b + 1) * TOK, :] = dq.reshape(2, TOK, HD)
            dk = dot(ds, query, ((0,), (0,)))
            dv = dot(low, grad, ((0,), (0,)))
            if block == 0:
                kparts[b][0] = dk
                vparts[b][0] = dv
            else:
                kparts[b] = [kparts[b][0] + dk[:half], dk[half:]]
                vparts[b] = [vparts[b][0] + dv[:half], dv[half:]]
    for block in range(2):
        for first, parts in ((2 * TOK, kparts), (3 * TOK, vparts)):
            both = parts[0][block].astype(BF16).astype(F32) + parts[1][block].astype(BF16).astype(F32)
            ret_ref[2 * block : 2 * block + 2, first : first + TOK, :] = both.astype(BF16).reshape(2, TOK, HD)

    part = dot(obuf[...], cot_ref[...], ((0,), (0,)))

    @pl.when(unit == 0)
    def _():
        wacc[...] = part

    @pl.when(unit == 1)
    def _():
        left = lax.broadcasted_iota(jnp.int32, (64, HD), 1) < 64
        total = wacc[...] + part
        for b in range(2):
            for m in range(16):
                upper = total[b * HD : b * HD + 64, m * HD : (m + 1) * HD]
                lower = total[b * HD + 64 : (b + 1) * HD, m * HD : (m + 1) * HD]
                even = jnp.where(left, upper, pltpu.roll(lower, 64, 1))
                odd = jnp.where(left, pltpu.roll(upper, 64, 1), lower)
                for col, piece in ((2 * m, even), (2 * m + 1, odd)):
                    xh, w, y = col // 16, 2 * ((col // 8) % 2) + b, col % 8
                    wg_ref[(xh * 8 + y) * 4 + w] = piece.astype(BF16)


def unpack_kernel(ret_ref, dq_ref, dk_ref, dv_ref):
    for g in range(8):
        dq_ref[0, :, 2 * g * HD : (2 * g + 1) * HD] = ret_ref[g, 0:TOK, :]
        dq_ref[0, :, (2 * g + 1) * HD : (2 * g + 2) * HD] = ret_ref[g, TOK : 2 * TOK, :]
        dk_ref[0, :, g * HD : (g + 1) * HD] = ret_ref[g, 2 * TOK : 3 * TOK, :]
        dv_ref[0, :, g * HD : (g + 1) * HD] = ret_ref[g, 3 * TOK : 4 * TOK, :]


def sum_kernel(got_ref, out_ref):
    out_ref[...] = jnp.sum(got_ref[...].astype(F32), axis=0)


def spread_kernel(sum_ref, out_ref):
    out_ref[0:64, :] = sum_ref[:, 0:64]
    out_ref[64:128, :] = sum_ref[:, 64:128]


VMEM = pl.BlockSpec(memory_space=pltpu.VMEM)
SMEM = pl.BlockSpec(memory_space=pltpu.SMEM)


def call(kernel, out_shape, **kw):
    return pl.pallas_call(
        kernel,
        out_shape=out_shape,
        compiler_params=pltpu.CompilerParams(vmem_limit_bytes=48 << 20),
        **kw,
    )


def shape(dims, dtype=BF16):
    return jax.ShapeDtypeStruct(dims, dtype)


def run_main(odd, arrived, cot, first, second):
    width = cot.shape[1]
    return call(
        main_kernel,
        (shape((8, 4 * TOK, HD)), shape((64, 64, HD))),
        grid=(2,),
        in_specs=[
            SMEM,
            pl.BlockSpec((4, PAY, HD), lambda u: (u, 0, 0)),
            pl.BlockSpec((WINDOW, width), lambda u: (u, 0)),
            pl.BlockSpec((HD, width), lambda u: (0, 0)),
            pl.BlockSpec((HD, width), lambda u: (0, 0)),
        ],
        out_specs=[
            pl.BlockSpec((4, 4 * TOK, HD), lambda u: (u, 0, 0)),
            pl.BlockSpec((64, 64, HD), lambda u: (0, 0, 0)),
        ],
        scratch_shapes=[
            pltpu.VMEM((2 * HD, width), BF16),
            pltpu.VMEM((WINDOW, 2 * HD), BF16),
            pltpu.VMEM((WINDOW, 2 * HD), BF16),
            pltpu.VMEM((2 * HD, width), F32),
        ],
    )(odd, arrived, cot, first, second)


def local(queries, keys, values, cotangent, out_weight, segment, row_type, pair_index):
    first = lax.ppermute(out_weight, AXES, weight_moves(0))
    second = lax.ppermute(out_weight, AXES, weight_moves(1))
    payload = call(
        pack_kernel,
        shape((8, PAY, HD)),
        in_specs=[VMEM] * 5 + [SMEM],
        out_specs=VMEM,
    )(queries, keys, values, segment, row_type, pair_index)
    arrived = lax.all_to_all(payload, NEAR, 0, 0)
    cot = lax.all_gather(cotangent[0], NEAR, axis=0, tiled=True)
    odd = lax.rem(lax.axis_index("w"), 2).astype(jnp.int32).reshape(1)
    back, pieces = run_main(odd, arrived, cot, first, second)
    spread = lax.all_to_all(pieces, FAR, 0, 0)
    home = lax.all_to_all(back, NEAR, 0, 0)
    summed = call(sum_kernel, shape((64, HD), F32), in_specs=[VMEM], out_specs=VMEM)(spread)
    moved = lax.ppermute(summed, AXES, [(b, a) for a, b in weight_moves(0)])
    weight_grad = call(spread_kernel, shape((HD, 64), F32), in_specs=[VMEM], out_specs=VMEM)(moved)
    query_grad, key_grad, value_grad = call(
        unpack_kernel,
        (shape(queries.shape), shape(keys.shape), shape(values.shape)),
        in_specs=[VMEM],
        out_specs=[VMEM] * 3,
    )(home)
    return query_grad, key_grad, value_grad, weight_grad


def solution(mesh):
    fine = Mesh(mesh.devices.reshape(SIZES), AXES)
    dp, seq = AXES[:3], AXES[3:]
    in_specs = (
        P(dp, seq, None),
        P(dp, seq, None),
        P(dp, seq, None),
        P(dp, seq, None),
        P(seq, None),
        P(dp, seq),
        P(dp, seq),
        P(dp, None),
    )
    out_specs = (P(dp, seq, None), P(dp, seq, None), P(dp, seq, None), P(seq, dp))
    return jax.shard_map(local, mesh=fine, in_specs=in_specs, out_specs=out_specs, check_vma=False)
```

time: 407 us -> 177 us (0.43)
  waiting for transfers between devices: 215 us -> 64.7 us
  blocking collectives: 94.6 us -> 48 us
  matrix products: 22.3 us -> 0 us
  local copies, waits for them, and re-layouts: 26.8 us -> 5.6 us
  Pallas kernels: 0 us -> 15.6 us
  other arithmetic: 11.6 us -> 0 us
  starting transfers between devices: 17.1 us -> 26.2 us
    reduce_scatter x1 -> x0, waiting for transfers between devices: 214 us -> none  [local(): lax.psum_scatter(weight_total.astype(jnp.bfloat16), 'dp', scatter_dimensi...]
    all_gather x2 -> x0, blocking collectives: 94.6 us -> none  [the longest x1 79.3 us: local(): lax.all_gather(row_type, 'seq', axis=1, tiled=True)]
    all_to_all x0 -> x1, blocking collectives: none -> 48 us  [local(): spread = lax.all_to_all(pieces, FAR, 0, 0)]
    ppermute x0 -> x3, waiting for transfers between devices: none -> 44.6 us  [the longest x1 36.1 us: local(): second = lax.ppermute(out_weight, AXES, weight_moves(1))]
    dot_general x26 -> x0, matrix products: 22.3 us -> none  [the longest x9 9.92 us: contract_first(): lax.dot_general(left, right, (((0,), (0,)), ((), ())), preferred_element_...]
    pallas_call x0 -> x5, Pallas kernels: none -> 15.6 us  [the longest x1 12.4 us: run_main(): call(main_kernel, (shape((8, 4 * TOK, HD)), shape((64, 64, HD))), grid=(2...]
    broadcast_in_dim x5 -> x0, local copies, waits for them, and re-layouts: 11.6 us -> none  [the longest x1 10.9 us: local(): jnp.stack([grad_query, key_part, value_part])[:, None]]
    all_gather x1, waiting for transfers between devices: 0.02 us -> 10.6 us  [local(): cot = lax.all_gather(cotangent[0], NEAR, axis=0, tiled=True)]
  transfers between devices with their start and end apart: 4 -> 6, of which waited for: 1 -> 4; matrix products, arithmetic and copies ran while one was open for 6% -> 0% of each run, Pallas kernels for 0% -> 2%
where the time goes in v1:
time: 177 us; the launch traced here: 174 us
  waiting for transfers between devices  64.7 us (37%)
  blocking collectives  48 us (27%)
  starting transfers between devices  26.2 us (15%)
  Pallas kernels  15.6 us (9%)
  between operations  14.1 us (8%)
  local copies, waits for them, and re-layouts  5.6 us (3%)
    all_to_all x1, blocking collectives, local(): spread = lax.all_to_all(pieces, FAR, 0, 0)  48 us
    ppermute x1, waiting for transfers between devices, local(): second = lax.ppermute(out_weight, AXES, weight_moves(1))  36.1 us
    pallas_call x1, Pallas kernels, run_main(): call(main_kernel, (shape((8, 4 * TOK, HD)), shape((64, 64, HD))), grid=(2...  12.4 us
    all_gather x1, waiting for transfers between devices, local(): cot = lax.all_gather(cotangent[0], NEAR, axis=0, tiled=True)  10.6 us
    all_to_all x1, starting transfers between devices, local(): arrived = lax.all_to_all(payload, NEAR, 0, 0)  10.5 us
    all_to_all x1, waiting for transfers between devices, local(): home = lax.all_to_all(back, NEAR, 0, 0)  8.77 us
    ppermute x1, waiting for transfers between devices, local(): first = lax.ppermute(out_weight, AXES, weight_moves(0))  8.57 us
    all_to_all x1, starting transfers between devices, local(): home = lax.all_to_all(back, NEAR, 0, 0)  6.84 us
  transfers between devices with their start and end apart: 6, of which 4 were waited for; matrix products, arithmetic and copies ran while one was open for 0% of the time, Pallas kernels for 2%

profile of v1, /device:TPU:1, one launch (start us, length us, event | category | flops | bytes accessed | tf_op | source)
XLA Modules:
  0.0 174.2 jit_solution(18413269615677312108)
XLA Ops:
  7.2 0.0 all-gather.3.cloned.1.call-start
  7.2 0.7 all-gather.3.cloned.1.call-update
  7.9 0.0 copy-start
  7.9 1.0 copy-done
  8.9 0.0 copy-start.1
  8.9 0.9 copy-done.1
  9.9 0.0 copy-start.2
  9.9 0.9 copy-done.2
  10.8 0.0 copy-start.3
  10.8 0.7 copy-done.3
  11.5 0.0 copy-start.4
  11.5 0.7 copy-done.4
  12.2 0.0 copy-start.5
  12.2 0.7 copy-done.5
  12.8 1.7 shard_map.111
  14.5 0.0 copy-start.6
  14.5 10.5 %all-to-all-start = ((bf16[8,528,128]{2,1,0:T(8,128)(2,1)}), bf16[8,528,128]{2,1,0:T(8,128)(2,1)S(1)}, u32[]{:S(2)}, u32[]{:S(2)}) async-start(bf16[8,528,128]{2,1,0:T(8,128)(2,1)} %shard_map.111), calls=%async_computation | async-start | bytes 2162688 | tf_op jit(solution)/shard_map/all_to_all | solution.py:217
  25.0 0.0 copy-done.6
  25.0 2.0 %collective-permute-start.1 = (bf16[128,2048]{1,0:T(8,128)(2,1)S(1)}, bf16[128,2048]{1,0:T(8,128)(2,1)S(1)}, u32[]{:S(2)}, u32[]{:S(2)}) collective-permute-start(bf16[128,2048]{1,0:T(8,128)(2,1)S(1)} %copy-done.6), channel_id=1, source_target_pairs={{1,0},{3,1},{5,2},{7,3},{0,4},{2,5},{4,6},{6,7},{129,8},{131,9},{1... | collective-permute-start | bytes 1572872 | tf_op jit(solution)/shard_map/ppermute | solution.py:210
  27.1 3.3 %collective-permute-start = (bf16[128,2048]{1,0:T(8,128)(2,1)S(1)}, bf16[128,2048]{1,0:T(8,128)(2,1)S(1)}, u32[]{:S(2)}, u32[]{:S(2)}) collective-permute-start(bf16[128,2048]{1,0:T(8,128)(2,1)S(1)} %copy-done.6), channel_id=1, source_target_pairs={{0,0},{2,1},{4,2},{6,3},{1,4},{3,5},{5,6},{7,7},{128,8},{130,9},{1... | collective-permute-start | bytes 1572872 | tf_op jit(solution)/shard_map/ppermute | solution.py:209
  30.4 36.1 %collective-permute-done.1.w1_ref = bf16[128,2048]{1,0:T(8,128)(2,1)S(1)} collective-permute-done((bf16[128,2048]{1,0:T(8,128)(2,1)S(1)}, bf16[128,2048]{1,0:T(8,128)(2,1)S(1)}, u32[]{:S(2)}, u32[]{:S(2)}) %collective-permute-start.1) | collective-permute-done | bytes 524320 | tf_op jit(solution)/shard_map/ppermute | solution.py:210
  66.5 8.6 %collective-permute-done.w0_ref = bf16[128,2048]{1,0:T(8,128)(2,1)S(1)} collective-permute-done((bf16[128,2048]{1,0:T(8,128)(2,1)S(1)}, bf16[128,2048]{1,0:T(8,128)(2,1)S(1)}, u32[]{:S(2)}, u32[]{:S(2)}) %collective-permute-start) | collective-permute-done | bytes 524320 | tf_op jit(solution)/shard_map/ppermute | solution.py:209
  75.0 0.0 all-to-all-done.pay_ref
  75.0 10.6 %all-gather.3.cloned.1.call-done = bf16[1,1024,2048]{2,1,0:T(8,128)(2,1)} async-done(((bf16[1,128,2048]{2,1,0:T(8,128)(2,1)}), bf16[1,1024,2048]{2,1,0:T(8,128)(2,1)}) %all-gather.3.cloned.1.call-update) | async-done | bytes 4194320 | tf_op jit(solution)/shard_map/all_gather | solution.py:218
  85.7 12.4 %shard_map.112 = (bf16[8,512,128]{2,1,0:T(8,128)(2,1)}, bf16[64,64,128]{2,1,0:T(8,128)(2,1)S(1)}) custom-call(s32[1]{0:T(128)} %bitcast.odd_ref, bf16[8,528,128]{2,1,0:T(8,128)(2,1)S(1)} %all-to-all-done.pay_ref, bf16[1024,2048]{1,0:T(8,128)(2,1)} %bitcast.2, bf16[128,2048]{1,0:T(8,128)(2,1)S(1)} %collective-permute-done.w0_ref, ...), custom_call_target="tpu_custom_call" | custom-call | tf_op jit(solution)/shard_map/pallas_call | solution.py:184
  98.0 48.0 %all_to_all.15.got_ref = bf16[64,64,128]{2,1,0:T(8,128)(2,1)S(1)} all-to-all(bf16[64,64,128]{2,1,0:T(8,128)(2,1)S(1)} %get-tuple-element.13), channel_id=1, replica_groups=mesh['xh'=2,'xl'=2,'y'=8,'w'=4,'p'=2,'c'=2] {'xh','y','w'}, dimensions={0} | all-to-all | bytes 2097152 | tf_op jit(solution)/shard_map/all_to_all | solution.py:221
  146.0 6.8 %all-to-all-start.1 = ((bf16[8,512,128]{2,1,0:T(8,128)(2,1)}), bf16[8,512,128]{2,1,0:T(8,128)(2,1)S(1)}, u32[]{:S(2)}, u32[]{:S(2)}) async-start(bf16[8,512,128]{2,1,0:T(8,128)(2,1)} %get-tuple-element.9), calls=%async_computation.1 | async-start | bytes 2097152 | tf_op jit(solution)/shard_map/all_to_all | solution.py:222
  152.8 0.2 shard_map.114
  153.0 3.5 %collective-permute-start.2 = (f32[64,128]{1,0:T(8,128)S(1)}, f32[64,128]{1,0:T(8,128)S(1)}, u32[]{:S(2)}, u32[]{:S(2)}) collective-permute-start(f32[64,128]{1,0:T(8,128)S(1)} %shard_map.114), channel_id=1, source_target_pairs={{0,0},{1,2},{2,4},{3,6},{4,1},{5,3},{6,5},{7,7},{8,128},{9,130},{1... | collective-permute-start | bytes 98312 | tf_op jit(solution)/shard_map/ppermute | solution.py:224
  156.6 8.8 %all-to-all-done.1.ret_ref = bf16[8,512,128]{2,1,0:T(8,128)(2,1)S(1)} async-done(((bf16[8,512,128]{2,1,0:T(8,128)(2,1)}), bf16[8,512,128]{2,1,0:T(8,128)(2,1)S(1)}, u32[]{:S(2)}, u32[]{:S(2)}) %all-to-all-start.1) | async-done | bytes 1048608 | tf_op jit(solution)/shard_map/all_to_all | solution.py:222
  165.3 1.2 shard_map.113
  166.6 0.0 collective-permute-done.2.sum_ref
  166.6 0.1 shard_map.115
  166.6 0.7 copy.12
Async XLA Ops:
  7.2 78.5 %all-gather.3.cloned.1.call-start = ((), (), s32[]{:S(2)}) async-start(), calls=%async_computation.3 | async-start | bytes 4718592 | tf_op jit(solution)/shard_map/all_gather | solution.py:218
  7.9 1.0 copy-start
  8.9 0.9 copy-start.1
  9.9 0.9 copy-start.2
  10.8 0.7 copy-start.3
  11.5 0.7 copy-start.4
  12.2 0.7 copy-start.5
  14.5 10.5 %copy-start.6 = (bf16[128,2048]{1,0:T(8,128)(2,1)S(1)}, bf16[128,2048]{1,0:T(8,128)(2,1)}, u32[]{:S(2)}) copy-start(bf16[128,2048]{1,0:T(8,128)(2,1)} %param.12) | copy-start | bytes 1572868
  14.5 60.5 %all-to-all-start = ((bf16[8,528,128]{2,1,0:T(8,128)(2,1)}), bf16[8,528,128]{2,1,0:T(8,128)(2,1)S(1)}, u32[]{:S(2)}, u32[]{:S(2)}) async-start(bf16[8,528,128]{2,1,0:T(8,128)(2,1)} %shard_map.111), calls=%async_computation | async-start | bytes 2162688 | tf_op jit(solution)/shard_map/all_to_all | solution.py:217
  25.0 41.5 %collective-permute-start.1 = (bf16[128,2048]{1,0:T(8,128)(2,1)S(1)}, bf16[128,2048]{1,0:T(8,128)(2,1)S(1)}, u32[]{:S(2)}, u32[]{:S(2)}) collective-permute-start(bf16[128,2048]{1,0:T(8,128)(2,1)S(1)} %copy-done.6), channel_id=1, source_target_pairs={{1,0},{3,1},{5,2},{7,3},{0,4},{2,5},{4,6},{6,7},{129,8},{131,9},{1... | collective-permute-start | bytes 1572872 | tf_op jit(solution)/shard_map/ppermute | solution.py:210
  27.1 48.0 %collective-permute-start = (bf16[128,2048]{1,0:T(8,128)(2,1)S(1)}, bf16[128,2048]{1,0:T(8,128)(2,1)S(1)}, u32[]{:S(2)}, u32[]{:S(2)}) collective-permute-start(bf16[128,2048]{1,0:T(8,128)(2,1)S(1)} %copy-done.6), channel_id=1, source_target_pairs={{0,0},{2,1},{4,2},{6,3},{1,4},{3,5},{5,6},{7,7},{128,8},{130,9},{1... | collective-permute-start | bytes 1572872 | tf_op jit(solution)/shard_map/ppermute | solution.py:209
  146.0 19.3 %all-to-all-start.1 = ((bf16[8,512,128]{2,1,0:T(8,128)(2,1)}), bf16[8,512,128]{2,1,0:T(8,128)(2,1)S(1)}, u32[]{:S(2)}, u32[]{:S(2)}) async-start(bf16[8,512,128]{2,1,0:T(8,128)(2,1)} %get-tuple-element.9), calls=%async_computation.1 | async-start | bytes 2097152 | tf_op jit(solution)/shard_map/all_to_all | solution.py:222
  153.0 13.5 %collective-permute-start.2 = (f32[64,128]{1,0:T(8,128)S(1)}, f32[64,128]{1,0:T(8,128)S(1)}, u32[]{:S(2)}, u32[]{:S(2)}) collective-permute-start(f32[64,128]{1,0:T(8,128)S(1)} %shard_map.114), channel_id=1, source_target_pairs={{0,0},{1,2},{2,4},{3,6},{4,1},{5,3},{6,5},{7,7},{8,128},{9,130},{1... | collective-permute-start | bytes 98312 | tf_op jit(solution)/shard_map/ppermute | solution.py:224
Sparse Core Ops, SparseCore 0:
  10.1 75.4 all-gather.2

commit v2 on v1

v2 whole, which is shorter than its diff:
```python
import itertools

import jax
import jax.numpy as jnp
import numpy as np
from jax import lax
from jax.experimental import pallas as pl
from jax.experimental.pallas import tpu as pltpu
from jax.sharding import Mesh
from jax.sharding import PartitionSpec as P

HD = 128
WINDOW = 512
HALF = WINDOW // 2
TOK = 128
SCALE = HD ** (-0.5)
AXES = ("x", "yh", "yl", "w", "p", "c")
SIZES = (4, 4, 2, 4, 2, 2)
NEAR = ("yl", "p", "c")
CODE = 16
PAY = 4 * TOK + CODE
NONE = 99
F32 = jnp.float32
BF16 = jnp.bfloat16


def place(*index):
    return int(np.ravel_multi_index(index, SIZES))


def devices():
    return itertools.product(*map(range, SIZES))


def weight_moves():
    moves = []
    for x, yh, yl, w, p, c in devices():
        head = 2 * (4 * yl + 2 * p + c) + x // 2
        source = place(2 * (w // 2) + x % 2, yh, w % 2, head // 4, (head // 2) % 2, head % 2)
        moves.append((source, place(x, yh, yl, w, p, c)))
    return moves


def piece_moves(turn):
    moves = []
    for x, yh, yl, w, p, c in devices():
        piece = (w + turn) % 4
        head = 2 * (4 * yl + 2 * p + c) + piece % 2
        owner = place(x, yh, piece // 2, head // 4, (head // 2) % 2, head % 2)
        moves.append((place(x, yh, yl, w, p, c), owner))
    return moves


def dot(left, right, dims):
    return lax.dot_general(left, right, (dims, ((), ())), preferred_element_type=F32)


def pack_kernel(q_ref, k_ref, v_ref, seg_ref, type_ref, pair_ref, out_ref):
    seg = seg_ref[...]
    kind = type_ref[...]
    pair = jnp.zeros_like(seg)
    count = pair_ref.shape[1]
    for s in range(count):
        pair = jnp.where(seg == s, pair_ref[0, s], pair)
    as_query = jnp.where(kind != 0, count + pair, NONE)
    as_key = jnp.where(kind == 0, count + pair, NONE)
    row = lax.broadcasted_iota(jnp.int32, (CODE, TOK), 0)
    code = jnp.where(row == 0, seg, jnp.where(row == 1, as_query, jnp.where(row == 2, as_key, 0)))
    code = code.astype(F32).astype(BF16)
    for g in range(2):
        out_ref[g, 0:TOK, :] = q_ref[0, :, 2 * g * HD : (2 * g + 1) * HD]
        out_ref[g, TOK : 2 * TOK, :] = q_ref[0, :, (2 * g + 1) * HD : (2 * g + 2) * HD]
        out_ref[g, 2 * TOK : 3 * TOK, :] = k_ref[0, :, g * HD : (g + 1) * HD]
        out_ref[g, 3 * TOK : 4 * TOK, :] = v_ref[0, :, g * HD : (g + 1) * HD]
        out_ref[g, 4 * TOK :, :] = code


def rows(pay_ref, first):
    return pay_ref[:, first : first + TOK, :].reshape(WINDOW, HD)


def hot(pay_ref):
    code = jnp.concatenate([pay_ref[i, 4 * TOK :, :] for i in range(4)], axis=1)
    code = code.astype(F32)[0:8]
    slot = lax.broadcasted_iota(jnp.int32, (32, WINDOW), 0).astype(F32)
    same = slot == code[0:1]
    want = jnp.where(same | (slot == code[1:2]), 1.0, 0.0).astype(BF16)
    have = jnp.where(same | (slot == code[2:3]), 1.0, 0.0).astype(BF16)
    return want, have


def visible_block(want, have, lo, ext):
    count = dot(want[:, lo:ext], have[:, :ext], ((0,), (0,)))
    t_pos = lax.broadcasted_iota(jnp.int32, (ext - lo, ext), 0) + lo
    s_pos = lax.broadcasted_iota(jnp.int32, (ext - lo, ext), 1)
    return (count > 0.5) & (s_pos <= t_pos)


def forward_kernel(pay_ref, after_ref, out_ref, lse_ref):
    del after_ref
    key = rows(pay_ref, 2 * TOK)
    value = rows(pay_ref, 3 * TOK)
    want, have = hot(pay_ref)
    lane = lax.broadcasted_iota(jnp.int32, (HALF, HD), 1)
    for block in range(2):
        lo = block * HALF
        ext = lo + HALF
        visible = visible_block(want, have, lo, ext)
        stats = []
        for b in range(2):
            query = rows(pay_ref, b * TOK)[lo:ext]
            scores = dot(query, key[:ext], ((1,), (1,))) * SCALE
            scores = jnp.where(visible, scores, -jnp.inf)
            top = jnp.max(scores, axis=-1, keepdims=True)
            exponent = jnp.exp(scores - top)
            total = jnp.sum(exponent, axis=-1, keepdims=True)
            low = (exponent * (1.0 / total)).astype(BF16)
            out = dot(low, value[:ext], ((1,), (0,)))
            out_ref[b * HD : (b + 1) * HD, lo:ext] = out.T.astype(BF16)
            stats.append(top + jnp.log(total))
        lse_ref[lo:ext, :] = jnp.where(lane == 0, stats[0], stats[1])


def weight_kernel(out_ref, cot_ref, a_ref, b_ref, c_ref, wg_ref):
    del a_ref, b_ref, c_ref
    total = dot(out_ref[...], cot_ref[...], ((1,), (0,)))
    left = lax.broadcasted_iota(jnp.int32, (64, HD), 1) < 64
    for b in range(2):
        for yh in range(4):
            upper = total[b * HD : b * HD + 64, yh * HD : (yh + 1) * HD]
            lower = total[b * HD + 64 : (b + 1) * HD, yh * HD : (yh + 1) * HD]
            wg_ref[yh, b] = jnp.where(left, upper, pltpu.roll(lower, 64, 1)).astype(BF16)
            wg_ref[yh, 2 + b] = jnp.where(left, pltpu.roll(upper, 64, 1), lower).astype(BF16)


def backward_kernel(x_ref, pay_ref, lse_ref, cot_ref, w0_ref, w1_ref, w2_ref, w3_ref, ret_ref, wbuf, ghbuf):
    @pl.when(pl.program_id(0) == 0)
    def _():
        for turn, quarter in enumerate((w0_ref, w1_ref, w2_ref, w3_ref)):
            first = pl.multiple_of(lax.rem(x_ref[0] + 4 - turn, 4) * 64, 64)
            wbuf[pl.ds(first, 64), :] = quarter[...]

    ghbuf[...] = dot(cot_ref[...], wbuf[...], ((1,), (1,))).astype(BF16)
    key = rows(pay_ref, 2 * TOK)
    value = rows(pay_ref, 3 * TOK)
    want, have = hot(pay_ref)
    kparts = [[None, None], [None, None]]
    vparts = [[None, None], [None, None]]
    for block in range(2):
        lo = block * HALF
        ext = lo + HALF
        visible = visible_block(want, have, lo, ext)
        for b in range(2):
            query = rows(pay_ref, b * TOK)[lo:ext]
            grad = ghbuf[lo:ext, b * HD : (b + 1) * HD]
            scores = dot(query, key[:ext], ((1,), (1,))) * SCALE - lse_ref[lo:ext, b : b + 1]
            attend = jnp.exp(jnp.where(visible, scores, -jnp.inf))
            low = attend.astype(BF16)
            grad_attend = dot(grad, value[:ext], ((1,), (1,)))
            delta = jnp.sum(attend * grad_attend, axis=-1, keepdims=True)
            ds = (attend * (grad_attend - delta) * SCALE).astype(BF16)
            dq = dot(ds, key[:ext], ((1,), (0,))).astype(BF16)
            ret_ref[2 * block : 2 * block + 2, b * TOK : (b + 1) * TOK, :] = dq.reshape(2, TOK, HD)
            dk = dot(ds, query, ((0,), (0,)))
            dv = dot(low, grad, ((0,), (0,)))
            if block == 0:
                kparts[b][0] = dk
                vparts[b][0] = dv
            else:
                kparts[b] = [kparts[b][0] + dk[:HALF], dk[HALF:]]
                vparts[b] = [vparts[b][0] + dv[:HALF], dv[HALF:]]
    for block in range(2):
        for first, parts in ((2 * TOK, kparts), (3 * TOK, vparts)):
            both = parts[0][block].astype(BF16).astype(F32) + parts[1][block].astype(BF16).astype(F32)
            ret_ref[2 * block : 2 * block + 2, first : first + TOK, :] = both.astype(BF16).reshape(2, TOK, HD)


def unpack_kernel(ret_ref, dq_ref, dk_ref, dv_ref):
    for g in range(2):
        dq_ref[0, :, 2 * g * HD : (2 * g + 1) * HD] = ret_ref[g, 0:TOK, :]
        dq_ref[0, :, (2 * g + 1) * HD : (2 * g + 2) * HD] = ret_ref[g, TOK : 2 * TOK, :]
        dk_ref[0, :, g * HD : (g + 1) * HD] = ret_ref[g, 2 * TOK : 3 * TOK, :]
        dv_ref[0, :, g * HD : (g + 1) * HD] = ret_ref[g, 3 * TOK : 4 * TOK, :]


def sum_kernel(w_ref, got_ref, out0_ref, out1_ref, out2_ref, out3_ref, total):
    total[...] = jnp.sum(got_ref[...].astype(F32), axis=0)
    for turn, out_ref in enumerate((out0_ref, out1_ref, out2_ref, out3_ref)):
        out_ref[...] = total[lax.rem(w_ref[0] + turn, 4)].astype(BF16)


def spread_kernel(a_ref, b_ref, c_ref, d_ref, out_ref):
    total = (a_ref[...].astype(F32) + b_ref[...].astype(F32)) + (c_ref[...].astype(F32) + d_ref[...].astype(F32))
    out_ref[:, 0:64] = total[:, 0:64].T
    out_ref[:, 64:128] = total[:, 64:128].T


SMEM = pl.BlockSpec(memory_space=pltpu.SMEM)
ANY = pl.BlockSpec(memory_space=pl.ANY)


def whole(*dims):
    return pl.BlockSpec(dims, lambda *_: (0,) * len(dims))


def call(kernel, out_shape, flops=0, bytes_accessed=0, room=60, **kw):
    return pl.pallas_call(
        kernel,
        out_shape=out_shape,
        compiler_params=pltpu.CompilerParams(vmem_limit_bytes=room << 20),
        cost_estimate=pl.CostEstimate(flops=flops, bytes_accessed=bytes_accessed, transcendentals=0),
        **kw,
    )


def shape(dims, dtype=BF16):
    return jax.ShapeDtypeStruct(dims, dtype)


def run_pack(queries, keys, values, segment, row_type, pair_index):
    return call(
        pack_kernel,
        shape((8, PAY, HD)),
        bytes_accessed=2 << 20,
        grid=(4,),
        in_specs=[
            pl.BlockSpec((1, TOK, 4 * HD), lambda i: (0, 0, i)),
            pl.BlockSpec((1, TOK, 2 * HD), lambda i: (0, 0, i)),
            pl.BlockSpec((1, TOK, 2 * HD), lambda i: (0, 0, i)),
            whole(1, TOK),
            whole(1, TOK),
            SMEM,
        ],
        out_specs=pl.BlockSpec((2, PAY, HD), lambda i: (i, 0, 0)),
    )(queries, keys, values, segment, row_type, pair_index)


def run_forward(arrived, after):
    return call(
        forward_kernel,
        (shape((2 * HD, 2 * WINDOW)), shape((2 * WINDOW, HD), F32)),
        flops=4 << 30,
        bytes_accessed=2 << 20,
        grid=(2,),
        in_specs=[pl.BlockSpec((4, PAY, HD), lambda u: (u, 0, 0)), ANY],
        out_specs=[
            pl.BlockSpec((2 * HD, WINDOW), lambda u: (0, u)),
            pl.BlockSpec((WINDOW, HD), lambda u: (u, 0)),
        ],
    )(arrived, after)


def run_weight(out, cot, after):
    return call(
        weight_kernel,
        shape((16, 4, 64, HD)),
        flops=1 << 30,
        bytes_accessed=6 << 20,
        grid=(4,),
        in_specs=[
            whole(2 * HD, 2 * WINDOW),
            pl.BlockSpec((2 * WINDOW, 512), lambda i: (0, i)),
        ]
        + [ANY] * 3,
        out_specs=pl.BlockSpec((4, 4, 64, HD), lambda i: (i, 0, 0, 0)),
    )(out, cot, *after)


def run_backward(x, arrived, lse, cot, quarters):
    width = cot.shape[1]
    return call(
        backward_kernel,
        shape((8, 4 * TOK, HD)),
        flops=8 << 30,
        bytes_accessed=7 << 20,
        grid=(2,),
        in_specs=[
            SMEM,
            pl.BlockSpec((4, PAY, HD), lambda u: (u, 0, 0)),
            pl.BlockSpec((WINDOW, HD), lambda u: (u, 0)),
            pl.BlockSpec((WINDOW, width), lambda u: (u, 0)),
        ]
        + [whole(64, width)] * 4,
        out_specs=pl.BlockSpec((4, 4 * TOK, HD), lambda u: (u, 0, 0)),
        scratch_shapes=[pltpu.VMEM((2 * HD, width), BF16), pltpu.VMEM((WINDOW, 2 * HD), BF16)],
    )(x, arrived, lse, cot, *quarters)


def run_sum(w, got):
    return call(
        sum_kernel,
        (shape((64, HD)),) * 4,
        room=16,
        bytes_accessed=1 << 20,
        in_specs=[SMEM, pl.BlockSpec(memory_space=pltpu.VMEM)],
        out_specs=[pl.BlockSpec(memory_space=pltpu.VMEM)] * 4,
        scratch_shapes=[pltpu.VMEM((4, 64, HD), F32)],
    )(w, got)


def run_spread(pieces):
    return call(
        spread_kernel,
        shape((64, HD), F32),
        room=16,
        in_specs=[pl.BlockSpec(memory_space=pltpu.VMEM)] * 4,
        out_specs=pl.BlockSpec(memory_space=pltpu.VMEM),
    )(*pieces)


def run_unpack(home, query_shape, key_shape):
    return call(
        unpack_kernel,
        (shape(query_shape), shape(key_shape), shape(key_shape)),
        room=16,
        bytes_accessed=2 << 20,
        grid=(4,),
        in_specs=[pl.BlockSpec((2, 4 * TOK, HD), lambda i: (i, 0, 0))],
        out_specs=[
            pl.BlockSpec((1, TOK, 4 * HD), lambda i: (0, 0, i)),
            pl.BlockSpec((1, TOK, 2 * HD), lambda i: (0, 0, i)),
            pl.BlockSpec((1, TOK, 2 * HD), lambda i: (0, 0, i)),
        ],
    )(home)


def local(queries, keys, values, cotangent, out_weight, segment, row_type, pair_index):
    x = lax.axis_index("x").astype(jnp.int32)
    w = lax.axis_index("w").astype(jnp.int32).reshape(1)
    cot = lax.all_gather(cotangent[0], NEAR, axis=0, tiled=True)
    share = lax.dynamic_slice_in_dim(out_weight, 64 * lax.rem(x, 2), 64, axis=0)
    quarter = lax.ppermute(share, AXES, weight_moves())
    quarters = [quarter] + [
        lax.ppermute(quarter, "x", [(i, (i + turn) % 4) for i in range(4)]) for turn in (1, 2, 3)
    ]
    payload = run_pack(queries, keys, values, segment, row_type, pair_index)
    arrived = lax.all_to_all(payload, NEAR, 0, 0)
    out, lse = run_forward(arrived, quarter)
    pieces = run_weight(out, cot, quarters[1:])
    got = lax.all_to_all(pieces, ("x", "yh"), 0, 0)
    back = run_backward(x.reshape(1), arrived, lse, cot, quarters)
    home = lax.all_to_all(back, NEAR, 0, 0)
    sent = [lax.ppermute(part, AXES, piece_moves(turn)) for turn, part in enumerate(run_sum(w, got))]
    weight_grad = run_spread(sent).T
    query_grad, key_grad, value_grad = run_unpack(home, queries.shape, keys.shape)
    return query_grad, key_grad, value_grad, weight_grad


def solution(mesh):
    fine = Mesh(mesh.devices.reshape(SIZES), AXES)
    dp, seq = AXES[:3], AXES[3:]
    in_specs = (
        P(dp, seq, None),
        P(dp, seq, None),
        P(dp, seq, None),
        P(dp, seq, None),
        P(seq, None),
        P(dp, seq),
        P(dp, seq),
        P(dp, None),
    )
    out_specs = (P(dp, seq, None), P(dp, seq, None), P(dp, seq, None), P(seq, dp))
    return jax.shard_map(local, mesh=fine, in_specs=in_specs, out_specs=out_specs, check_vma=False)
```

time: 177 us -> 153 us (0.86); the launches traced: 174 us -> 153 us
  blocking collectives: 48 us -> 0 us
  starting transfers between devices: 26.2 us -> 63.2 us
  waiting for transfers between devices: 64.7 us -> 46.7 us
  Pallas kernels: 15.6 us -> 27 us
  local copies, waits for them, and re-layouts: 5.6 us -> 1.84 us
    all_to_all x1 -> x0, blocking collectives: 48 us -> none  [local(): spread = lax.all_to_all(pieces, FAR, 0, 0)]
    ppermute x3 -> x8, starting transfers between devices: 8.89 us -> 24.9 us  [the longest x4 15.6 us: local(): lax.ppermute(part, AXES, piece_moves(turn))]
    all_to_all x0 -> x1, starting transfers between devices: none -> 13.2 us  [local(): got = lax.all_to_all(pieces, ('x', 'yh'), 0, 0)]
    all_to_all x0 -> x1, waiting for transfers between devices: none -> 12.7 us  [local(): got = lax.all_to_all(pieces, ('x', 'yh'), 0, 0)]
    ppermute x3 -> x8, waiting for transfers between devices: 44.6 us -> 33.2 us  [the longest x1 25.9 us: local(): quarter = lax.ppermute(share, AXES, weight_moves())]
    pallas_call x5 -> x7, Pallas kernels: 15.6 us -> 27 us  [the longest x1 10.5 us: run_backward(): call(backward_kernel, shape((8, 4 * TOK, HD)), flops=8 << 30, bytes_acces...]
    all_gather x1, waiting for transfers between devices: 10.6 us -> 0.02 us  [local(): cot = lax.all_gather(cotangent[0], NEAR, axis=0, tiled=True)]
    all_to_all x1, waiting for transfers between devices: 8.77 us -> 0.01 us  [local(): home = lax.all_to_all(back, NEAR, 0, 0)]
  transfers between devices with their start and end apart: 6 -> 12, of which waited for: 4 -> 3; matrix products, arithmetic and copies ran while one was open for 0% -> 0% of each run, Pallas kernels for 2% -> 14%
where the time goes in v2:
time: 153 us
  starting transfers between devices  63.2 us (41%)
  waiting for transfers between devices  46.7 us (31%)
  Pallas kernels  27 us (18%)
  between operations  14.2 us (9%)
  local copies, waits for them, and re-layouts  1.84 us (1%)
    ppermute x1, waiting for transfers between devices, local(): quarter = lax.ppermute(share, AXES, weight_moves())  25.9 us
    ppermute x4, starting transfers between devices, local(): lax.ppermute(part, AXES, piece_moves(turn))  15.6 us
    all_to_all x1, starting transfers between devices, local(): home = lax.all_to_all(back, NEAR, 0, 0)  14.7 us
    all_to_all x1, starting transfers between devices, local(): got = lax.all_to_all(pieces, ('x', 'yh'), 0, 0)  13.2 us
    all_to_all x1, waiting for transfers between devices, local(): got = lax.all_to_all(pieces, ('x', 'yh'), 0, 0)  12.7 us
    pallas_call x1, Pallas kernels, run_backward(): call(backward_kernel, shape((8, 4 * TOK, HD)), flops=8 << 30, bytes_acces...  10.5 us
    all_to_all x1, starting transfers between devices, local(): arrived = lax.all_to_all(payload, NEAR, 0, 0)  10.3 us
    ppermute x3, starting transfers between devices, local(): lax.ppermute(quarter, 'x', [(i, (i + turn) % 4) for i in range(4)])  7.44 us
  transfers between devices with their start and end apart: 12, of which 3 were waited for; matrix products, arithmetic and copies ran while one was open for 0% of the time, Pallas kernels for 14%

profile of v2, /device:TPU:1, one launch (start us, length us, event | category | flops | bytes accessed | tf_op | source)
XLA Modules:
  0.0 152.8 jit_solution(9698699086996141133)
XLA Ops:
  7.2 0.0 copy-start
  7.2 0.0 all-gather.3.cloned.1.call-start
  7.2 0.7 all-gather.3.cloned.1.call-update
  7.9 3.5 %shard_map.111 = bf16[8,528,128]{2,1,0:T(8,128)(2,1)} custom-call(bf16[1,128,2048]{2,1,0:T(8,128)(2,1)} %q_ref.1, bf16[1,128,1024]{2,1,0:T(8,128)(2,1)} %k_ref.1, bf16[1,128,1024]{2,1,0:T(8,128)(2,1)} %v_ref.1, s32[1,128]{1,0:T(1,128)} %seg_ref.1, s32[1,128]{1,0:T(1,128)} %type_ref.1, s32[1,24]{1,0:T(1,128)} %pair_ref.1), custom_call_target="tpu_custom_call" | custom-call | bytes 2097152 | tf_op jit(solution)/shard_map/pallas_call | solution.py:221
  11.4 10.3 %all-to-all-start = ((bf16[8,528,128]{2,1,0:T(8,128)(2,1)}), bf16[8,528,128]{2,1,0:T(8,128)(2,1)S(1)}, u32[]{:S(2)}, u32[]{:S(2)}) async-start(bf16[8,528,128]{2,1,0:T(8,128)(2,1)} %shard_map.111), calls=%async_computation | async-start | bytes 2162688 | tf_op jit(solution)/shard_map/all_to_all | solution.py:337
  21.7 0.0 copy-done
  21.8 1.9 %collective-permute-start = (bf16[64,2048]{1,0:T(8,128)(2,1)S(1)}, bf16[64,2048]{1,0:T(8,128)(2,1)S(1)}, u32[]{:S(2)}, u32[]{:S(2)}) collective-permute-start(bf16[64,2048]{1,0:T(8,128)(2,1)S(1)} %constant_dynamic-slice_fusion), channel_id=1, source_target_pairs={{0,0},{2,1},{4,2},{6,3},{16,4},{18,5},{20,6},{22,7},{256,8},{258,9... | collective-permute-start | bytes 786440 | tf_op jit(solution)/shard_map/ppermute | solution.py:332
  23.7 25.9 %collective-permute-done.after_ref.w0_ref = bf16[64,2048]{1,0:T(8,128)(2,1)S(1)} collective-permute-done((bf16[64,2048]{1,0:T(8,128)(2,1)S(1)}, bf16[64,2048]{1,0:T(8,128)(2,1)S(1)}, u32[]{:S(2)}, u32[]{:S(2)}) %collective-permute-start) | collective-permute-done | bytes 262176 | tf_op jit(solution)/shard_map/ppermute | solution.py:332
  49.6 0.0 copy-start.5
  49.6 1.9 %collective-permute-start.3 = (bf16[64,2048]{1,0:T(8,128)(2,1)S(1)}, bf16[64,2048]{1,0:T(8,128)(2,1)S(1)}, u32[]{:S(2)}, u32[]{:S(2)}) collective-permute-start(bf16[64,2048]{1,0:T(8,128)(2,1)S(1)} %collective-permute-done.after_ref.w0_ref), channel_id=1, source_target_pairs={{0,384},{128,0},{256,128},{384,256},{1,385},{129,1},{257,129},{385... | collective-permute-start | bytes 786440 | tf_op jit(solution)/shard_map/ppermute | solution.py:334
  51.5 2.8 %collective-permute-start.2 = (bf16[64,2048]{1,0:T(8,128)(2,1)S(1)}, bf16[64,2048]{1,0:T(8,128)(2,1)S(1)}, u32[]{:S(2)}, u32[]{:S(2)}) collective-permute-start(bf16[64,2048]{1,0:T(8,128)(2,1)S(1)} %collective-permute-done.after_ref.w0_ref), channel_id=1, source_target_pairs={{0,256},{128,384},{256,0},{384,128},{1,257},{129,385},{257,1},{385... | collective-permute-start | bytes 786440 | tf_op jit(solution)/shard_map/ppermute | solution.py:334
  54.3 2.8 %collective-permute-start.1 = (bf16[64,2048]{1,0:T(8,128)(2,1)S(1)}, bf16[64,2048]{1,0:T(8,128)(2,1)S(1)}, u32[]{:S(2)}, u32[]{:S(2)}) collective-permute-start(bf16[64,2048]{1,0:T(8,128)(2,1)S(1)} %collective-permute-done.after_ref.w0_ref), channel_id=1, source_target_pairs={{0,128},{128,256},{256,384},{384,0},{1,129},{129,257},{257,385},{3... | collective-permute-start | bytes 786440 | tf_op jit(solution)/shard_map/ppermute | solution.py:334
  57.1 0.0 all-to-all-done.pay_ref
  57.1 0.0 copy-done.5
  57.1 0.0 copy-start.1
  57.1 1.0 copy-done.1
  58.1 5.2 %shard_map.112 = (bf16[256,1024]{1,0:T(8,128)(2,1)}, f32[1024,128]{1,0:T(8,128)}) custom-call(bf16[8,528,128]{2,1,0:T(8,128)(2,1)} %copy-done.1, bf16[64,2048]{1,0:T(8,128)(2,1)} %copy-done.5), custom_call_target="tpu_custom_call" | custom-call | flops 4294967296 | bytes 2097152 | tf_op jit(solution)/shard_map/pallas_call | solution.py:239
  63.4 0.0 collective-permute-done.3.w3_ref.c_ref
  63.4 0.0 copy-start.2
  63.4 0.0 collective-permute-done.2.w2_ref.b_ref
  63.4 0.0 copy-start.3
  63.4 0.0 collective-permute-done.1.w1_ref.a_ref
  63.4 0.0 copy-start.4
  63.4 0.0 all-gather.3.cloned.1.call-done
  63.4 0.6 copy-done.2
  64.1 0.1 copy-done.3
  64.2 0.0 copy-done.4
  64.2 5.1 %shard_map.115 = bf16[16,4,64,128]{3,2,1,0:T(8,128)(2,1)} custom-call(bf16[256,1024]{1,0:T(8,128)(2,1)} %get-tuple-element.17.out_ref, bf16[1024,2048]{1,0:T(8,128)(2,1)} %bitcast.4, bf16[64,2048]{1,0:T(8,128)(2,1)} %copy-done.4, bf16[64,2048]{1,0:T(8,128)(2,1)} %copy-done.3, bf16[64,2048]{1,0:T(8,128)(2,1)} %copy-done.2), custom_call_target="tpu_custom_call" | custom-call | flops 1073741824 | bytes 6291456 | tf_op jit(solution)/shard_map/pallas_call | solution.py:254
  69.3 13.2 %all-to-all-start.2 = ((bf16[16,4,64,128]{3,2,1,0:T(8,128)(2,1)}), bf16[16,4,64,128]{3,2,1,0:T(8,128)(2,1)S(1)}, u32[]{:S(2)}, u32[]{:S(2)}) async-start(bf16[16,4,64,128]{3,2,1,0:T(8,128)(2,1)} %shard_map.115), calls=%async_computation.2 | async-start | bytes 2097152 | tf_op jit(solution)/shard_map/all_to_all | solution.py:340
  82.5 10.5 %shard_map.113 = bf16[8,512,128]{2,1,0:T(8,128)(2,1)} custom-call(s32[1]{0:T(128)} %bitcast.x_ref, bf16[8,528,128]{2,1,0:T(8,128)(2,1)} %copy-done.1, f32[1024,128]{1,0:T(8,128)} %get-tuple-element.13.lse_ref, bf16[1024,2048]{1,0:T(8,128)(2,1)} %bitcast.5, bf16[64,2048]{1,0:T(8,128)(2,1)} %copy-done.5, bf16[64,2048]{1,0:T(8,128)(2,1)} %copy-done.4, ...), custom_call_target="tpu_custom_call" | custom-call | flops 8589934592 | bytes 7340032 | tf_op jit(solution)/shard_map/pallas_call | solution.py:271
  93.0 12.7 %all-to-all-done.2.got_ref = bf16[16,4,64,128]{3,2,1,0:T(8,128)(2,1)S(1)} async-done(((bf16[16,4,64,128]{3,2,1,0:T(8,128)(2,1)}), bf16[16,4,64,128]{3,2,1,0:T(8,128)(2,1)S(1)}, u32[]{:S(2)}, u32[]{:S(2)}) %all-to-all-start.2) | async-done | bytes 1048608 | tf_op jit(solution)/shard_map/all_to_all | solution.py:340
  105.7 14.7 %all-to-all-start.1 = ((bf16[8,512,128]{2,1,0:T(8,128)(2,1)}), bf16[8,512,128]{2,1,0:T(8,128)(2,1)S(1)}, u32[]{:S(2)}, u32[]{:S(2)}) async-start(bf16[8,512,128]{2,1,0:T(8,128)(2,1)} %shard_map.113), calls=%async_computation.1 | async-start | bytes 2097152 | tf_op jit(solution)/shard_map/all_to_all | solution.py:342
  120.4 0.2 shard_map.116
  120.6 3.5 %collective-permute-start.4 = (bf16[64,128]{1,0:T(8,128)(2,1)S(1)}, bf16[64,128]{1,0:T(8,128)(2,1)S(1)}, u32[]{:S(2)}, u32[]{:S(2)}) collective-permute-start(bf16[64,128]{1,0:T(8,128)(2,1)S(1)} %get-tuple-element.18), channel_id=1, source_target_pairs={{0,0},{1,2},{2,4},{3,6},{4,1},{5,3},{6,5},{7,7},{8,16},{9,18},{10,... | collective-permute-start | bytes 49160 | tf_op jit(solution)/shard_map/ppermute | solution.py:343
  124.2 2.6 %collective-permute-start.5 = (bf16[64,128]{1,0:T(8,128)(2,1)S(1)}, bf16[64,128]{1,0:T(8,128)(2,1)S(1)}, u32[]{:S(2)}, u32[]{:S(2)}) collective-permute-start(bf16[64,128]{1,0:T(8,128)(2,1)S(1)} %get-tuple-element.19), channel_id=1, source_target_pairs={{0,1},{1,3},{2,5},{3,7},{4,16},{5,18},{6,20},{7,22},{8,17},{9,19},... | collective-permute-start | bytes 49160 | tf_op jit(solution)/shard_map/ppermute | solution.py:343
  126.8 7.5 %collective-permute-start.6 = (bf16[64,128]{1,0:T(8,128)(2,1)S(1)}, bf16[64,128]{1,0:T(8,128)(2,1)S(1)}, u32[]{:S(2)}, u32[]{:S(2)}) collective-permute-start(bf16[64,128]{1,0:T(8,128)(2,1)S(1)} %get-tuple-element.20), channel_id=1, source_target_pairs={{0,16},{1,18},{2,20},{3,22},{4,17},{5,19},{6,21},{7,23},{8,0},{9,2... | collective-permute-start | bytes 49160 | tf_op jit(solution)/shard_map/ppermute | solution.py:343
  134.3 1.9 %collective-permute-start.7 = (bf16[64,128]{1,0:T(8,128)(2,1)S(1)}, bf16[64,128]{1,0:T(8,128)(2,1)S(1)}, u32[]{:S(2)}, u32[]{:S(2)}) collective-permute-start(bf16[64,128]{1,0:T(8,128)(2,1)S(1)} %get-tuple-element.21), channel_id=1, source_target_pairs={{0,17},{1,19},{2,21},{3,23},{4,0},{5,2},{6,4},{7,6},{8,1},{9,3},{1... | collective-permute-start | bytes 49160 | tf_op jit(solution)/shard_map/ppermute | solution.py:343
  136.2 0.0 all-to-all-done.1.ret_ref
  136.2 1.6 %shard_map.114 = (bf16[1,128,2048]{2,1,0:T(8,128)(2,1)}, bf16[1,128,1024]{2,1,0:T(8,128)(2,1)}, bf16[1,128,1024]{2,1,0:T(8,128)(2,1)}) custom-call(bf16[8,512,128]{2,1,0:T(8,128)(2,1)S(1)} %all-to-all-done.1.ret_ref), custom_call_target="tpu_custom_call" | custom-call | bytes 2097152 | tf_op jit(solution)/shard_map/pallas_call | solution.py:312
  137.8 0.0 collective-permute-done.4.a_ref
  137.8 0.0 collective-permute-done.5.b_ref
  137.8 0.0 collective-permute-done.6.c_ref
  137.9 7.3 %collective-permute-done.7.d_ref = bf16[64,128]{1,0:T(8,128)(2,1)S(1)} collective-permute-done((bf16[64,128]{1,0:T(8,128)(2,1)S(1)}, bf16[64,128]{1,0:T(8,128)(2,1)S(1)}, u32[]{:S(2)}, u32[]{:S(2)}) %collective-permute-start.7) | collective-permute-done | bytes 16416 | tf_op jit(solution)/shard_map/ppermute | solution.py:343
  145.2 0.8 shard_map.117
  (1 shorter events, 0.0 us)
Async XLA Ops:
  7.2 14.6 %copy-start = (bf16[128,2048]{1,0:T(8,128)(2,1)S(1)}, bf16[128,2048]{1,0:T(8,128)(2,1)}, u32[]{:S(2)}) copy-start(bf16[128,2048]{1,0:T(8,128)(2,1)} %param.12) | copy-start | bytes 1572868
  7.2 56.2 %all-gather.3.cloned.1.call-start = ((), (), s32[]{:S(2)}) async-start(), calls=%async_computation.3 | async-start | bytes 4718592 | tf_op jit(solution)/shard_map/all_gather | solution.py:330
  11.4 45.7 %all-to-all-start = ((bf16[8,528,128]{2,1,0:T(8,128)(2,1)}), bf16[8,528,128]{2,1,0:T(8,128)(2,1)S(1)}, u32[]{:S(2)}, u32[]{:S(2)}) async-start(bf16[8,528,128]{2,1,0:T(8,128)(2,1)} %shard_map.111), calls=%async_computation | async-start | bytes 2162688 | tf_op jit(solution)/shard_map/all_to_all | solution.py:337
  21.8 27.9 %collective-permute-start = (bf16[64,2048]{1,0:T(8,128)(2,1)S(1)}, bf16[64,2048]{1,0:T(8,128)(2,1)S(1)}, u32[]{:S(2)}, u32[]{:S(2)}) collective-permute-start(bf16[64,2048]{1,0:T(8,128)(2,1)S(1)} %constant_dynamic-slice_fusion), channel_id=1, source_target_pairs={{0,0},{2,1},{4,2},{6,3},{16,4},{18,5},{20,6},{22,7},{256,8},{258,9... | collective-permute-start | bytes 786440 | tf_op jit(solution)/shard_map/ppermute | solution.py:332
  49.6 7.5 %copy-start.5 = (bf16[64,2048]{1,0:T(8,128)(2,1)}, bf16[64,2048]{1,0:T(8,128)(2,1)S(1)}, u32[]{:S(2)}) copy-start(bf16[64,2048]{1,0:T(8,128)(2,1)S(1)} %collective-permute-done.after_ref.w0_ref) | copy-start | bytes 786436
  49.6 13.7 %collective-permute-start.3 = (bf16[64,2048]{1,0:T(8,128)(2,1)S(1)}, bf16[64,2048]{1,0:T(8,128)(2,1)S(1)}, u32[]{:S(2)}, u32[]{:S(2)}) collective-permute-start(bf16[64,2048]{1,0:T(8,128)(2,1)S(1)} %collective-permute-done.after_ref.w0_ref), channel_id=1, source_target_pairs={{0,384},{128,0},{256,128},{384,256},{1,385},{129,1},{257,129},{385... | collective-permute-start | bytes 786440 | tf_op jit(solution)/shard_map/ppermute | solution.py:334
  51.5 11.8 %collective-permute-start.2 = (bf16[64,2048]{1,0:T(8,128)(2,1)S(1)}, bf16[64,2048]{1,0:T(8,128)(2,1)S(1)}, u32[]{:S(2)}, u32[]{:S(2)}) collective-permute-start(bf16[64,2048]{1,0:T(8,128)(2,1)S(1)} %collective-permute-done.after_ref.w0_ref), channel_id=1, source_target_pairs={{0,256},{128,384},{256,0},{384,128},{1,257},{129,385},{257,1},{385... | collective-permute-start | bytes 786440 | tf_op jit(solution)/shard_map/ppermute | solution.py:334
  54.3 9.1 %collective-permute-start.1 = (bf16[64,2048]{1,0:T(8,128)(2,1)S(1)}, bf16[64,2048]{1,0:T(8,128)(2,1)S(1)}, u32[]{:S(2)}, u32[]{:S(2)}) collective-permute-start(bf16[64,2048]{1,0:T(8,128)(2,1)S(1)} %collective-permute-done.after_ref.w0_ref), channel_id=1, source_target_pairs={{0,128},{128,256},{256,384},{384,0},{1,129},{129,257},{257,385},{3... | collective-permute-start | bytes 786440 | tf_op jit(solution)/shard_map/ppermute | solution.py:334
  57.1 1.0 copy-start.1
  63.4 0.7 copy-start.2
  63.4 0.8 copy-start.3
  63.4 0.8 copy-start.4
  69.3 36.4 %all-to-all-start.2 = ((bf16[16,4,64,128]{3,2,1,0:T(8,128)(2,1)}), bf16[16,4,64,128]{3,2,1,0:T(8,128)(2,1)S(1)}, u32[]{:S(2)}, u32[]{:S(2)}) async-start(bf16[16,4,64,128]{3,2,1,0:T(8,128)(2,1)} %shard_map.115), calls=%async_computation.2 | async-start | bytes 2097152 | tf_op jit(solution)/shard_map/all_to_all | solution.py:340
  105.7 30.5 %all-to-all-start.1 = ((bf16[8,512,128]{2,1,0:T(8,128)(2,1)}), bf16[8,512,128]{2,1,0:T(8,128)(2,1)S(1)}, u32[]{:S(2)}, u32[]{:S(2)}) async-start(bf16[8,512,128]{2,1,0:T(8,128)(2,1)} %shard_map.113), calls=%async_computation.1 | async-start | bytes 2097152 | tf_op jit(solution)/shard_map/all_to_all | solution.py:342
  120.6 17.2 %collective-permute-start.4 = (bf16[64,128]{1,0:T(8,128)(2,1)S(1)}, bf16[64,128]{1,0:T(8,128)(2,1)S(1)}, u32[]{:S(2)}, u32[]{:S(2)}) collective-permute-start(bf16[64,128]{1,0:T(8,128)(2,1)S(1)} %get-tuple-element.18), channel_id=1, source_target_pairs={{0,0},{1,2},{2,4},{3,6},{4,1},{5,3},{6,5},{7,7},{8,16},{9,18},{10,... | collective-permute-start | bytes 49160 | tf_op jit(solution)/shard_map/ppermute | solution.py:343
  124.2 13.7 %collective-permute-start.5 = (bf16[64,128]{1,0:T(8,128)(2,1)S(1)}, bf16[64,128]{1,0:T(8,128)(2,1)S(1)}, u32[]{:S(2)}, u32[]{:S(2)}) collective-permute-start(bf16[64,128]{1,0:T(8,128)(2,1)S(1)} %get-tuple-element.19), channel_id=1, source_target_pairs={{0,1},{1,3},{2,5},{3,7},{4,16},{5,18},{6,20},{7,22},{8,17},{9,19},... | collective-permute-start | bytes 49160 | tf_op jit(solution)/shard_map/ppermute | solution.py:343
  126.8 11.1 %collective-permute-start.6 = (bf16[64,128]{1,0:T(8,128)(2,1)S(1)}, bf16[64,128]{1,0:T(8,128)(2,1)S(1)}, u32[]{:S(2)}, u32[]{:S(2)}) collective-permute-start(bf16[64,128]{1,0:T(8,128)(2,1)S(1)} %get-tuple-element.20), channel_id=1, source_target_pairs={{0,16},{1,18},{2,20},{3,22},{4,17},{5,19},{6,21},{7,23},{8,0},{9,2... | collective-permute-start | bytes 49160 | tf_op jit(solution)/shard_map/ppermute | solution.py:343
  134.3 10.9 %collective-permute-start.7 = (bf16[64,128]{1,0:T(8,128)(2,1)S(1)}, bf16[64,128]{1,0:T(8,128)(2,1)S(1)}, u32[]{:S(2)}, u32[]{:S(2)}) collective-permute-start(bf16[64,128]{1,0:T(8,128)(2,1)S(1)} %get-tuple-element.21), channel_id=1, source_target_pairs={{0,17},{1,19},{2,21},{3,23},{4,0},{5,2},{6,4},{7,6},{8,1},{9,3},{1... | collective-permute-start | bytes 49160 | tf_op jit(solution)/shard_map/ppermute | solution.py:343
Sparse Core Ops, SparseCore 0:
  10.2 50.2 all-gather.2

commit v3 on v2

--- a/solution.py
+++ b/solution.py
@@ -96,8 +96,11 @@
     return (count > 0.5) & (s_pos <= t_pos)
 
 
-def forward_kernel(pay_ref, after_ref, out_ref, lse_ref):
-    del after_ref
+def forward_kernel(half_ref, pay_ref, w_ref, out_ref, lse_ref, share_ref):
+    @pl.when(pl.program_id(0) == 0)
+    def _():
+        share_ref[...] = w_ref[pl.ds(pl.multiple_of(half_ref[0] * 64, 64), 64), :]
+
     key = rows(pay_ref, 2 * TOK)
     value = rows(pay_ref, 3 * TOK)
     want, have = hot(pay_ref)
@@ -121,16 +124,15 @@
         lse_ref[lo:ext, :] = jnp.where(lane == 0, stats[0], stats[1])
 
 
-def weight_kernel(out_ref, cot_ref, a_ref, b_ref, c_ref, wg_ref):
-    del a_ref, b_ref, c_ref
+def weight_kernel(out_ref, cot_ref, wg_ref):
     total = dot(out_ref[...], cot_ref[...], ((1,), (0,)))
     left = lax.broadcasted_iota(jnp.int32, (64, HD), 1) < 64
     for b in range(2):
         for yh in range(4):
             upper = total[b * HD : b * HD + 64, yh * HD : (yh + 1) * HD]
             lower = total[b * HD + 64 : (b + 1) * HD, yh * HD : (yh + 1) * HD]
-            wg_ref[yh, b] = jnp.where(left, upper, pltpu.roll(lower, 64, 1)).astype(BF16)
-            wg_ref[yh, 2 + b] = jnp.where(left, pltpu.roll(upper, 64, 1), lower).astype(BF16)
+            wg_ref[0, 4 * yh + b] = jnp.where(left, upper, pltpu.roll(lower, 64, 1)).astype(BF16)
+            wg_ref[0, 4 * yh + 2 + b] = jnp.where(left, pltpu.roll(upper, 64, 1), lower).astype(BF16)
 
 
 def backward_kernel(x_ref, pay_ref, lse_ref, cot_ref, w0_ref, w1_ref, w2_ref, w3_ref, ret_ref, wbuf, ghbuf):
@@ -183,10 +185,19 @@
         dv_ref[0, :, g * HD : (g + 1) * HD] = ret_ref[g, 3 * TOK : 4 * TOK, :]
 
 
-def sum_kernel(w_ref, got_ref, out0_ref, out1_ref, out2_ref, out3_ref, total):
-    total[...] = jnp.sum(got_ref[...].astype(F32), axis=0)
-    for turn, out_ref in enumerate((out0_ref, out1_ref, out2_ref, out3_ref)):
-        out_ref[...] = total[lax.rem(w_ref[0] + turn, 4)].astype(BF16)
+def near_sum_kernel(yh_ref, got_ref, *out_refs):
+    for turn, out_ref in enumerate(out_refs):
+        first = pl.multiple_of(lax.rem(yh_ref[0] + turn, 4) * 4, 4)
+        out_ref[...] = jnp.sum(got_ref[:, pl.ds(first, 4)].astype(F32), axis=0).astype(BF16)
+
+
+def far_sum_kernel(w_ref, a_ref, b_ref, c_ref, d_ref, *out_refs):
+    for turn, out_ref in enumerate(out_refs):
+        piece = lax.rem(w_ref[0] + turn, 4)
+        total = (a_ref[piece].astype(F32) + b_ref[piece].astype(F32)) + (
+            c_ref[piece].astype(F32) + d_ref[piece].astype(F32)
+        )
+        out_ref[...] = total.astype(BF16)
 
 
 def spread_kernel(a_ref, b_ref, c_ref, d_ref, out_ref):
@@ -196,7 +207,7 @@
 
 
 SMEM = pl.BlockSpec(memory_space=pltpu.SMEM)
-ANY = pl.BlockSpec(memory_space=pl.ANY)
+VMEM = pl.BlockSpec(memory_space=pltpu.VMEM)
 
 
 def whole(*dims):
@@ -235,35 +246,36 @@
     )(queries, keys, values, segment, row_type, pair_index)
 
 
-def run_forward(arrived, after):
+def run_forward(half, arrived, out_weight):
+    width = out_weight.shape[1]
     return call(
         forward_kernel,
-        (shape((2 * HD, 2 * WINDOW)), shape((2 * WINDOW, HD), F32)),
+        (shape((2 * HD, 2 * WINDOW)), shape((2 * WINDOW, HD), F32), shape((64, width))),
         flops=4 << 30,
         bytes_accessed=2 << 20,
         grid=(2,),
-        in_specs=[pl.BlockSpec((4, PAY, HD), lambda u: (u, 0, 0)), ANY],
+        in_specs=[SMEM, pl.BlockSpec((4, PAY, HD), lambda u: (u, 0, 0)), whole(HD, width)],
         out_specs=[
             pl.BlockSpec((2 * HD, WINDOW), lambda u: (0, u)),
             pl.BlockSpec((WINDOW, HD), lambda u: (u, 0)),
+            whole(64, width),
         ],
-    )(arrived, after)
-
-
-def run_weight(out, cot, after):
+    )(half, arrived, out_weight)
+
+
+def run_weight(out, cot):
     return call(
         weight_kernel,
-        shape((16, 4, 64, HD)),
+        shape((4, 16, 64, HD)),
         flops=1 << 30,
         bytes_accessed=6 << 20,
         grid=(4,),
         in_specs=[
             whole(2 * HD, 2 * WINDOW),
             pl.BlockSpec((2 * WINDOW, 512), lambda i: (0, i)),
-        ]
-        + [ANY] * 3,
-        out_specs=pl.BlockSpec((4, 4, 64, HD), lambda i: (i, 0, 0, 0)),
-    )(out, cot, *after)
+        ],
+        out_specs=pl.BlockSpec((1, 16, 64, HD), lambda i: (i, 0, 0, 0)),
+    )(out, cot)
 
 
 def run_backward(x, arrived, lse, cot, quarters):
@@ -286,16 +298,26 @@
     )(x, arrived, lse, cot, *quarters)
 
 
-def run_sum(w, got):
-    return call(
-        sum_kernel,
+def run_near_sum(yh, got):
+    return call(
+        near_sum_kernel,
+        (shape((4, 64, HD)),) * 4,
+        room=16,
+        bytes_accessed=1 << 20,
+        in_specs=[SMEM, VMEM],
+        out_specs=[VMEM] * 4,
+    )(yh, got)
+
+
+def run_far_sum(w, parts):
+    return call(
+        far_sum_kernel,
         (shape((64, HD)),) * 4,
         room=16,
-        bytes_accessed=1 << 20,
-        in_specs=[SMEM, pl.BlockSpec(memory_space=pltpu.VMEM)],
-        out_specs=[pl.BlockSpec(memory_space=pltpu.VMEM)] * 4,
-        scratch_shapes=[pltpu.VMEM((4, 64, HD), F32)],
-    )(w, got)
+        bytes_accessed=1 << 18,
+        in_specs=[SMEM] + [VMEM] * 4,
+        out_specs=[VMEM] * 4,
+    )(w, *parts)
 
 
 def run_spread(pieces):
@@ -303,8 +325,8 @@
         spread_kernel,
         shape((64, HD), F32),
         room=16,
-        in_specs=[pl.BlockSpec(memory_space=pltpu.VMEM)] * 4,
-        out_specs=pl.BlockSpec(memory_space=pltpu.VMEM),
+        in_specs=[VMEM] * 4,
+        out_specs=VMEM,
     )(*pieces)
 
 
@@ -324,23 +346,30 @@
     )(home)
 
 
+def place_of(axis):
+    return lax.axis_index(axis).astype(jnp.int32).reshape(1)
+
+
+def shifts(count):
+    return [[(i, (i + turn) % count) for i in range(count)] for turn in range(1, count)]
+
+
 def local(queries, keys, values, cotangent, out_weight, segment, row_type, pair_index):
-    x = lax.axis_index("x").astype(jnp.int32)
-    w = lax.axis_index("w").astype(jnp.int32).reshape(1)
+    x = place_of("x")
     cot = lax.all_gather(cotangent[0], NEAR, axis=0, tiled=True)
-    share = lax.dynamic_slice_in_dim(out_weight, 64 * lax.rem(x, 2), 64, axis=0)
-    quarter = lax.ppermute(share, AXES, weight_moves())
-    quarters = [quarter] + [
-        lax.ppermute(quarter, "x", [(i, (i + turn) % 4) for i in range(4)]) for turn in (1, 2, 3)
-    ]
     payload = run_pack(queries, keys, values, segment, row_type, pair_index)
     arrived = lax.all_to_all(payload, NEAR, 0, 0)
-    out, lse = run_forward(arrived, quarter)
-    pieces = run_weight(out, cot, quarters[1:])
-    got = lax.all_to_all(pieces, ("x", "yh"), 0, 0)
-    back = run_backward(x.reshape(1), arrived, lse, cot, quarters)
+    out, lse, share = run_forward(lax.rem(x, 2), arrived, out_weight)
+    quarter = lax.ppermute(share, AXES, weight_moves())
+    quarters = [quarter] + [lax.ppermute(quarter, "x", shift) for shift in shifts(4)]
+    pieces = run_weight(out, cot)
+    got = lax.all_to_all(pieces, "x", 0, 0)
+    back = run_backward(x, arrived, lse, cot, quarters)
     home = lax.all_to_all(back, NEAR, 0, 0)
-    sent = [lax.ppermute(part, AXES, piece_moves(turn)) for turn, part in enumerate(run_sum(w, got))]
+    own, *others = run_near_sum(place_of("yh"), got)
+    parts = [own] + [lax.ppermute(part, "yh", shift) for part, shift in zip(others, shifts(4))]
+    parts = run_far_sum(place_of("w"), parts)
+    sent = [lax.ppermute(part, AXES, piece_moves(turn)) for turn, part in enumerate(parts)]
     weight_grad = run_spread(sent).T
     query_grad, key_grad, value_grad = run_unpack(home, queries.shape, keys.shape)
     return query_grad, key_grad, value_grad, weight_grad

time: 153 us -> 165 us (1.078)
  the two profiles are of different devices: /device:TPU:1 before, /device:TPU:9 now
where the time goes in v3:
time: 165 us; the launch traced here: 164 us
  starting transfers between devices  68.1 us (41%)
  waiting for transfers between devices  53.2 us (32%)
  Pallas kernels  27.1 us (16%)
  between operations  14.2 us (9%)
  local copies, waits for them, and re-layouts  1.74 us (1%)
    ppermute x1, waiting for transfers between devices, local(): quarter = lax.ppermute(share, AXES, weight_moves())  24.8 us
    ppermute x4, starting transfers between devices, local(): lax.ppermute(part, AXES, piece_moves(turn))  20.4 us
    ppermute x3, starting transfers between devices, local(): lax.ppermute(part, 'yh', shift)  15.8 us
    all_to_all x1, waiting for transfers between devices, local(): arrived = lax.all_to_all(payload, NEAR, 0, 0)  14.2 us
    pallas_call x1, Pallas kernels, run_backward(): call(backward_kernel, shape((8, 4 * TOK, HD)), flops=8 << 30, bytes_acces...  10.5 us
    all_to_all x1, starting transfers between devices, local(): arrived = lax.all_to_all(payload, NEAR, 0, 0)  9.62 us
    ppermute x3, starting transfers between devices, local(): lax.ppermute(quarter, 'x', shift)  9.29 us
    ppermute x3, waiting for transfers between devices, local(): lax.ppermute(part, 'yh', shift)  5.99 us
  transfers between devices with their start and end apart: 15, of which 6 were waited for; matrix products, arithmetic and copies ran while one was open for 0% of the time, Pallas kernels for 16%

profile of v3, /device:TPU:9, one launch (start us, length us, event | category | flops | bytes accessed | tf_op | source)
XLA Modules:
  0.0 164.4 jit_solution(15881490370786649917)
XLA Ops:
  7.2 0.0 all-gather.3.cloned.1.call-start
  7.2 0.7 all-gather.3.cloned.1.call-update
  7.9 3.5 %shard_map.111 = bf16[8,528,128]{2,1,0:T(8,128)(2,1)} custom-call(bf16[1,128,2048]{2,1,0:T(8,128)(2,1)} %q_ref.1, bf16[1,128,1024]{2,1,0:T(8,128)(2,1)} %k_ref.1, bf16[1,128,1024]{2,1,0:T(8,128)(2,1)} %v_ref.1, s32[1,128]{1,0:T(1,128)} %seg_ref.1, s32[1,128]{1,0:T(1,128)} %type_ref.1, s32[1,24]{1,0:T(1,128)} %pair_ref.1), custom_call_target="tpu_custom_call" | custom-call | bytes 2097152 | tf_op jit(solution)/shard_map/pallas_call | solution.py:232
  11.4 9.6 %all-to-all-start = ((bf16[8,528,128]{2,1,0:T(8,128)(2,1)}), bf16[8,528,128]{2,1,0:T(8,128)(2,1)S(1)}, u32[]{:S(2)}, u32[]{:S(2)}) async-start(bf16[8,528,128]{2,1,0:T(8,128)(2,1)} %shard_map.111), calls=%async_computation | async-start | bytes 2162688 | tf_op jit(solution)/shard_map/all_to_all | solution.py:361
  21.0 14.2 %all-to-all-done.pay_ref = bf16[8,528,128]{2,1,0:T(8,128)(2,1)S(1)} async-done(((bf16[8,528,128]{2,1,0:T(8,128)(2,1)}), bf16[8,528,128]{2,1,0:T(8,128)(2,1)S(1)}, u32[]{:S(2)}, u32[]{:S(2)}) %all-to-all-start) | async-done | bytes 1081376 | tf_op jit(solution)/shard_map/all_to_all | solution.py:361
  35.2 0.0 copy-start
  35.2 1.0 copy-done
  36.2 5.4 %shard_map.112 = (bf16[256,1024]{1,0:T(8,128)(2,1)}, f32[1024,128]{1,0:T(8,128)}, bf16[64,2048]{1,0:T(8,128)(2,1)}) custom-call(s32[1]{0:T(128)S(6)} %rem.18.half_ref, bf16[8,528,128]{2,1,0:T(8,128)(2,1)} %copy-done, bf16[128,2048]{1,0:T(8,128)(2,1)} %w_ref.1), custom_call_target="tpu_custom_call" | custom-call | flops 4294967296 | bytes 2097152 | tf_op jit(solution)/shard_map/pallas_call | solution.py:251
  41.6 4.4 %collective-permute-start = (bf16[64,2048]{1,0:T(8,128)(2,1)}, bf16[64,2048]{1,0:T(8,128)(2,1)S(1)}, u32[]{:S(2)}, u32[]{:S(2)}) collective-permute-start(bf16[64,2048]{1,0:T(8,128)(2,1)} %get-tuple-element.19), channel_id=1, source_target_pairs={{0,0},{2,1},{4,2},{6,3},{16,4},{18,5},{20,6},{22,7},{256,8},{258,9... | collective-permute-start | bytes 786440 | tf_op jit(solution)/shard_map/ppermute | solution.py:363
  46.0 24.8 %collective-permute-done.w0_ref = bf16[64,2048]{1,0:T(8,128)(2,1)S(1)} collective-permute-done((bf16[64,2048]{1,0:T(8,128)(2,1)}, bf16[64,2048]{1,0:T(8,128)(2,1)S(1)}, u32[]{:S(2)}, u32[]{:S(2)}) %collective-permute-start) | collective-permute-done | bytes 262176 | tf_op jit(solution)/shard_map/ppermute | solution.py:363
  70.8 0.0 copy-start.1
  70.8 3.1 %collective-permute-start.1 = (bf16[64,2048]{1,0:T(8,128)(2,1)S(1)}, bf16[64,2048]{1,0:T(8,128)(2,1)S(1)}, u32[]{:S(2)}, u32[]{:S(2)}) collective-permute-start(bf16[64,2048]{1,0:T(8,128)(2,1)S(1)} %collective-permute-done.w0_ref), channel_id=1, source_target_pairs={{0,128},{128,256},{256,384},{384,0},{1,129},{129,257},{257,385},{3... | collective-permute-start | bytes 786440 | tf_op jit(solution)/shard_map/ppermute | solution.py:364
  73.9 4.3 %collective-permute-start.2 = (bf16[64,2048]{1,0:T(8,128)(2,1)S(1)}, bf16[64,2048]{1,0:T(8,128)(2,1)S(1)}, u32[]{:S(2)}, u32[]{:S(2)}) collective-permute-start(bf16[64,2048]{1,0:T(8,128)(2,1)S(1)} %collective-permute-done.w0_ref), channel_id=1, source_target_pairs={{0,256},{128,384},{256,0},{384,128},{1,257},{129,385},{257,1},{385... | collective-permute-start | bytes 786440 | tf_op jit(solution)/shard_map/ppermute | solution.py:364
  78.2 2.0 %collective-permute-start.3 = (bf16[64,2048]{1,0:T(8,128)(2,1)S(1)}, bf16[64,2048]{1,0:T(8,128)(2,1)S(1)}, u32[]{:S(2)}, u32[]{:S(2)}) collective-permute-start(bf16[64,2048]{1,0:T(8,128)(2,1)S(1)} %collective-permute-done.w0_ref), channel_id=1, source_target_pairs={{0,384},{128,0},{256,128},{384,256},{1,385},{129,1},{257,129},{385... | collective-permute-start | bytes 786440 | tf_op jit(solution)/shard_map/ppermute | solution.py:364
  80.1 0.0 all-gather.3.cloned.1.call-done
  80.2 5.1 %shard_map.115 = bf16[4,16,64,128]{3,2,1,0:T(8,128)(2,1)} custom-call(bf16[256,1024]{1,0:T(8,128)(2,1)} %get-tuple-element.23.out_ref, bf16[1024,2048]{1,0:T(8,128)(2,1)} %bitcast.5), custom_call_target="tpu_custom_call" | custom-call | flops 1073741824 | bytes 6291456 | tf_op jit(solution)/shard_map/pallas_call | solution.py:267
  85.3 0.0 copy-done.1
  85.3 3.5 %all-to-all-start.2 = ((bf16[4,16,64,128]{3,2,1,0:T(8,128)(2,1)}), bf16[4,16,64,128]{3,2,1,0:T(8,128)(2,1)S(1)}, u32[]{:S(2)}, u32[]{:S(2)}) async-start(bf16[4,16,64,128]{3,2,1,0:T(8,128)(2,1)} %shard_map.115), calls=%async_computation.2 | async-start | bytes 2097152 | tf_op jit(solution)/shard_map/all_to_all | solution.py:366
  88.8 0.0 collective-permute-done.1.w1_ref
  88.8 0.0 copy-start.2
  88.8 0.0 collective-permute-done.2.w2_ref
  88.8 0.0 copy-start.3
  88.8 0.4 collective-permute-done.3.w3_ref
  89.3 0.0 copy-start.4
  89.3 0.3 copy-done.2
  89.5 0.1 copy-done.3
  89.6 0.4 copy-done.4
  90.0 10.5 %shard_map.113 = bf16[8,512,128]{2,1,0:T(8,128)(2,1)} custom-call(s32[1]{0:T(128)} %bitcast.x_ref, bf16[8,528,128]{2,1,0:T(8,128)(2,1)} %copy-done, f32[1024,128]{1,0:T(8,128)} %get-tuple-element.18.lse_ref, bf16[1024,2048]{1,0:T(8,128)(2,1)} %bitcast.6, bf16[64,2048]{1,0:T(8,128)(2,1)} %copy-done.1, bf16[64,2048]{1,0:T(8,128)(2,1)} %copy-done.2, ...), custom_call_target="tpu_custom_call" | custom-call | flops 8589934592 | bytes 7340032 | tf_op jit(solution)/shard_map/pallas_call | solution.py:283
  100.5 2.2 %all-to-all-done.2.got_ref = bf16[4,16,64,128]{3,2,1,0:T(8,128)(2,1)S(1)} async-done(((bf16[4,16,64,128]{3,2,1,0:T(8,128)(2,1)}), bf16[4,16,64,128]{3,2,1,0:T(8,128)(2,1)S(1)}, u32[]{:S(2)}, u32[]{:S(2)}) %all-to-all-start.2) | async-done | bytes 1048608 | tf_op jit(solution)/shard_map/all_to_all | solution.py:366
  102.7 5.1 %all-to-all-start.1 = ((bf16[8,512,128]{2,1,0:T(8,128)(2,1)}), bf16[8,512,128]{2,1,0:T(8,128)(2,1)S(1)}, u32[]{:S(2)}, u32[]{:S(2)}) async-start(bf16[8,512,128]{2,1,0:T(8,128)(2,1)} %shard_map.113), calls=%async_computation.1 | async-start | bytes 2097152 | tf_op jit(solution)/shard_map/all_to_all | solution.py:368
  107.8 0.1 shard_map.116
  107.9 4.3 %collective-permute-start.4 = (bf16[4,64,128]{2,1,0:T(8,128)(2,1)S(1)}, bf16[4,64,128]{2,1,0:T(8,128)(2,1)S(1)}, u32[]{:S(2)}, u32[]{:S(2)}) collective-permute-start(bf16[4,64,128]{2,1,0:T(8,128)(2,1)S(1)} %get-tuple-element.25), channel_id=1, source_target_pairs={{0,32},{32,64},{64,96},{96,0},{1,33},{33,65},{65,97},{97,1},{2,34}... | collective-permute-start | bytes 196616 | tf_op jit(solution)/shard_map/ppermute | solution.py:370
  112.2 6.6 %collective-permute-start.5 = (bf16[4,64,128]{2,1,0:T(8,128)(2,1)S(1)}, bf16[4,64,128]{2,1,0:T(8,128)(2,1)S(1)}, u32[]{:S(2)}, u32[]{:S(2)}) collective-permute-start(bf16[4,64,128]{2,1,0:T(8,128)(2,1)S(1)} %get-tuple-element.26), channel_id=1, source_target_pairs={{0,64},{32,96},{64,0},{96,32},{1,65},{33,97},{65,1},{97,33},{2,66}... | collective-permute-start | bytes 196616 | tf_op jit(solution)/shard_map/ppermute | solution.py:370
  118.8 5.0 %collective-permute-start.6 = (bf16[4,64,128]{2,1,0:T(8,128)(2,1)S(1)}, bf16[4,64,128]{2,1,0:T(8,128)(2,1)S(1)}, u32[]{:S(2)}, u32[]{:S(2)}) collective-permute-start(bf16[4,64,128]{2,1,0:T(8,128)(2,1)S(1)} %get-tuple-element.27), channel_id=1, source_target_pairs={{0,96},{32,0},{64,32},{96,64},{1,97},{33,1},{65,33},{97,65},{2,98}... | collective-permute-start | bytes 196616 | tf_op jit(solution)/shard_map/ppermute | solution.py:370
  123.7 0.0 collective-permute-done.4.b_ref
  123.7 6.0 %collective-permute-done.5.c_ref = bf16[4,64,128]{2,1,0:T(8,128)(2,1)S(1)} collective-permute-done((bf16[4,64,128]{2,1,0:T(8,128)(2,1)S(1)}, bf16[4,64,128]{2,1,0:T(8,128)(2,1)S(1)}, u32[]{:S(2)}, u32[]{:S(2)}) %collective-permute-start.5) | collective-permute-done | bytes 65568 | tf_op jit(solution)/shard_map/ppermute | solution.py:370
  129.7 0.0 collective-permute-done.6.d_ref
  129.8 4.8 %collective-permute-start.10 = (bf16[64,128]{1,0:T(8,128)(2,1)S(1)}, bf16[64,128]{1,0:T(8,128)(2,1)S(1)}, u32[]{:S(2)}, u32[]{:S(2)}) collective-permute-start(bf16[64,128]{1,0:T(8,128)(2,1)S(1)} %get-tuple-element.31), channel_id=1, source_target_pairs={{0,17},{1,19},{2,21},{3,23},{4,0},{5,2},{6,4},{7,6},{8,1},{9,3},{1... | collective-permute-start | bytes 49160 | tf_op jit(solution)/shard_map/ppermute | solution.py:372
  134.6 5.0 %collective-permute-start.7 = (bf16[64,128]{1,0:T(8,128)(2,1)S(1)}, bf16[64,128]{1,0:T(8,128)(2,1)S(1)}, u32[]{:S(2)}, u32[]{:S(2)}) collective-permute-start(bf16[64,128]{1,0:T(8,128)(2,1)S(1)} %get-tuple-element.28), channel_id=1, source_target_pairs={{0,0},{1,2},{2,4},{3,6},{4,1},{5,3},{6,5},{7,7},{8,16},{9,18},{10,... | collective-permute-start | bytes 49160 | tf_op jit(solution)/shard_map/ppermute | solution.py:372
  139.6 8.7 %collective-permute-start.8 = (bf16[64,128]{1,0:T(8,128)(2,1)S(1)}, bf16[64,128]{1,0:T(8,128)(2,1)S(1)}, u32[]{:S(2)}, u32[]{:S(2)}) collective-permute-start(bf16[64,128]{1,0:T(8,128)(2,1)S(1)} %get-tuple-element.29), channel_id=1, source_target_pairs={{0,1},{1,3},{2,5},{3,7},{4,16},{5,18},{6,20},{7,22},{8,17},{9,19},... | collective-permute-start | bytes 49160 | tf_op jit(solution)/shard_map/ppermute | solution.py:372
  148.3 1.9 %collective-permute-start.9 = (bf16[64,128]{1,0:T(8,128)(2,1)S(1)}, bf16[64,128]{1,0:T(8,128)(2,1)S(1)}, u32[]{:S(2)}, u32[]{:S(2)}) collective-permute-start(bf16[64,128]{1,0:T(8,128)(2,1)S(1)} %get-tuple-element.30), channel_id=1, source_target_pairs={{0,16},{1,18},{2,20},{3,22},{4,17},{5,19},{6,21},{7,23},{8,0},{9,2... | collective-permute-start | bytes 49160 | tf_op jit(solution)/shard_map/ppermute | solution.py:372
  150.2 0.0 collective-permute-done.10.d_ref
  150.2 0.0 collective-permute-done.7.a_ref
  150.2 0.0 collective-permute-done.8.b_ref
  150.2 4.9 %collective-permute-done.9.c_ref = bf16[64,128]{1,0:T(8,128)(2,1)S(1)} collective-permute-done((bf16[64,128]{1,0:T(8,128)(2,1)S(1)}, bf16[64,128]{1,0:T(8,128)(2,1)S(1)}, u32[]{:S(2)}, u32[]{:S(2)}) %collective-permute-start.9) | collective-permute-done | bytes 16416 | tf_op jit(solution)/shard_map/ppermute | solution.py:372
  155.1 0.8 shard_map.118
  156.0 0.0 all-to-all-done.1.ret_ref
  156.0 1.6 shard_map.114
  (1 shorter events, 0.0 us)
Async XLA Ops:
  7.2 73.0 %all-gather.3.cloned.1.call-start = ((), (), s32[]{:S(2)}) async-start(), calls=%async_computation.3 | async-start | bytes 4718592 | tf_op jit(solution)/shard_map/all_gather | solution.py:359
  11.4 23.8 %all-to-all-start = ((bf16[8,528,128]{2,1,0:T(8,128)(2,1)}), bf16[8,528,128]{2,1,0:T(8,128)(2,1)S(1)}, u32[]{:S(2)}, u32[]{:S(2)}) async-start(bf16[8,528,128]{2,1,0:T(8,128)(2,1)} %shard_map.111), calls=%async_computation | async-start | bytes 2162688 | tf_op jit(solution)/shard_map/all_to_all | solution.py:361
  35.2 1.0 copy-start
  41.6 29.2 %collective-permute-start = (bf16[64,2048]{1,0:T(8,128)(2,1)}, bf16[64,2048]{1,0:T(8,128)(2,1)S(1)}, u32[]{:S(2)}, u32[]{:S(2)}) collective-permute-start(bf16[64,2048]{1,0:T(8,128)(2,1)} %get-tuple-element.19), channel_id=1, source_target_pairs={{0,0},{2,1},{4,2},{6,3},{16,4},{18,5},{20,6},{22,7},{256,8},{258,9... | collective-permute-start | bytes 786440 | tf_op jit(solution)/shard_map/ppermute | solution.py:363
  70.8 14.5 %copy-start.1 = (bf16[64,2048]{1,0:T(8,128)(2,1)}, bf16[64,2048]{1,0:T(8,128)(2,1)S(1)}, u32[]{:S(2)}) copy-start(bf16[64,2048]{1,0:T(8,128)(2,1)S(1)} %collective-permute-done.w0_ref) | copy-start | bytes 786436
  70.8 18.0 %collective-permute-start.1 = (bf16[64,2048]{1,0:T(8,128)(2,1)S(1)}, bf16[64,2048]{1,0:T(8,128)(2,1)S(1)}, u32[]{:S(2)}, u32[]{:S(2)}) collective-permute-start(bf16[64,2048]{1,0:T(8,128)(2,1)S(1)} %collective-permute-done.w0_ref), channel_id=1, source_target_pairs={{0,128},{128,256},{256,384},{384,0},{1,129},{129,257},{257,385},{3... | collective-permute-start | bytes 786440 | tf_op jit(solution)/shard_map/ppermute | solution.py:364
  73.9 14.9 %collective-permute-start.2 = (bf16[64,2048]{1,0:T(8,128)(2,1)S(1)}, bf16[64,2048]{1,0:T(8,128)(2,1)S(1)}, u32[]{:S(2)}, u32[]{:S(2)}) collective-permute-start(bf16[64,2048]{1,0:T(8,128)(2,1)S(1)} %collective-permute-done.w0_ref), channel_id=1, source_target_pairs={{0,256},{128,384},{256,0},{384,128},{1,257},{129,385},{257,1},{385... | collective-permute-start | bytes 786440 | tf_op jit(solution)/shard_map/ppermute | solution.py:364
  78.2 11.1 %collective-permute-start.3 = (bf16[64,2048]{1,0:T(8,128)(2,1)S(1)}, bf16[64,2048]{1,0:T(8,128)(2,1)S(1)}, u32[]{:S(2)}, u32[]{:S(2)}) collective-permute-start(bf16[64,2048]{1,0:T(8,128)(2,1)S(1)} %collective-permute-done.w0_ref), channel_id=1, source_target_pairs={{0,384},{128,0},{256,128},{384,256},{1,385},{129,1},{257,129},{385... | collective-permute-start | bytes 786440 | tf_op jit(solution)/shard_map/ppermute | solution.py:364
  85.3 17.4 %all-to-all-start.2 = ((bf16[4,16,64,128]{3,2,1,0:T(8,128)(2,1)}), bf16[4,16,64,128]{3,2,1,0:T(8,128)(2,1)S(1)}, u32[]{:S(2)}, u32[]{:S(2)}) async-start(bf16[4,16,64,128]{3,2,1,0:T(8,128)(2,1)} %shard_map.115), calls=%async_computation.2 | async-start | bytes 2097152 | tf_op jit(solution)/shard_map/all_to_all | solution.py:366
  88.8 0.7 copy-start.2
  88.8 0.8 copy-start.3
  89.3 0.7 copy-start.4
  102.7 53.3 %all-to-all-start.1 = ((bf16[8,512,128]{2,1,0:T(8,128)(2,1)}), bf16[8,512,128]{2,1,0:T(8,128)(2,1)S(1)}, u32[]{:S(2)}, u32[]{:S(2)}) async-start(bf16[8,512,128]{2,1,0:T(8,128)(2,1)} %shard_map.113), calls=%async_computation.1 | async-start | bytes 2097152 | tf_op jit(solution)/shard_map/all_to_all | solution.py:368
  107.9 15.8 %collective-permute-start.4 = (bf16[4,64,128]{2,1,0:T(8,128)(2,1)S(1)}, bf16[4,64,128]{2,1,0:T(8,128)(2,1)S(1)}, u32[]{:S(2)}, u32[]{:S(2)}) collective-permute-start(bf16[4,64,128]{2,1,0:T(8,128)(2,1)S(1)} %get-tuple-element.25), channel_id=1, source_target_pairs={{0,32},{32,64},{64,96},{96,0},{1,33},{33,65},{65,97},{97,1},{2,34}... | collective-permute-start | bytes 196616 | tf_op jit(solution)/shard_map/ppermute | solution.py:370
  112.2 17.5 %collective-permute-start.5 = (bf16[4,64,128]{2,1,0:T(8,128)(2,1)S(1)}, bf16[4,64,128]{2,1,0:T(8,128)(2,1)S(1)}, u32[]{:S(2)}, u32[]{:S(2)}) collective-permute-start(bf16[4,64,128]{2,1,0:T(8,128)(2,1)S(1)} %get-tuple-element.26), channel_id=1, source_target_pairs={{0,64},{32,96},{64,0},{96,32},{1,65},{33,97},{65,1},{97,33},{2,66}... | collective-permute-start | bytes 196616 | tf_op jit(solution)/shard_map/ppermute | solution.py:370
  118.8 11.0 %collective-permute-start.6 = (bf16[4,64,128]{2,1,0:T(8,128)(2,1)S(1)}, bf16[4,64,128]{2,1,0:T(8,128)(2,1)S(1)}, u32[]{:S(2)}, u32[]{:S(2)}) collective-permute-start(bf16[4,64,128]{2,1,0:T(8,128)(2,1)S(1)} %get-tuple-element.27), channel_id=1, source_target_pairs={{0,96},{32,0},{64,32},{96,64},{1,97},{33,1},{65,33},{97,65},{2,98}... | collective-permute-start | bytes 196616 | tf_op jit(solution)/shard_map/ppermute | solution.py:370
  129.8 20.5 %collective-permute-start.10 = (bf16[64,128]{1,0:T(8,128)(2,1)S(1)}, bf16[64,128]{1,0:T(8,128)(2,1)S(1)}, u32[]{:S(2)}, u32[]{:S(2)}) collective-permute-start(bf16[64,128]{1,0:T(8,128)(2,1)S(1)} %get-tuple-element.31), channel_id=1, source_target_pairs={{0,17},{1,19},{2,21},{3,23},{4,0},{5,2},{6,4},{7,6},{8,1},{9,3},{1... | collective-permute-start | bytes 49160 | tf_op jit(solution)/shard_map/ppermute | solution.py:372
  134.6 15.7 %collective-permute-start.7 = (bf16[64,128]{1,0:T(8,128)(2,1)S(1)}, bf16[64,128]{1,0:T(8,128)(2,1)S(1)}, u32[]{:S(2)}, u32[]{:S(2)}) collective-permute-start(bf16[64,128]{1,0:T(8,128)(2,1)S(1)} %get-tuple-element.28), channel_id=1, source_target_pairs={{0,0},{1,2},{2,4},{3,6},{4,1},{5,3},{6,5},{7,7},{8,16},{9,18},{10,... | collective-permute-start | bytes 49160 | tf_op jit(solution)/shard_map/ppermute | solution.py:372
  139.6 10.7 %collective-permute-start.8 = (bf16[64,128]{1,0:T(8,128)(2,1)S(1)}, bf16[64,128]{1,0:T(8,128)(2,1)S(1)}, u32[]{:S(2)}, u32[]{:S(2)}) collective-permute-start(bf16[64,128]{1,0:T(8,128)(2,1)S(1)} %get-tuple-element.29), channel_id=1, source_target_pairs={{0,1},{1,3},{2,5},{3,7},{4,16},{5,18},{6,20},{7,22},{8,17},{9,19},... | collective-permute-start | bytes 49160 | tf_op jit(solution)/shard_map/ppermute | solution.py:372
  148.3 6.9 %collective-permute-start.9 = (bf16[64,128]{1,0:T(8,128)(2,1)S(1)}, bf16[64,128]{1,0:T(8,128)(2,1)S(1)}, u32[]{:S(2)}, u32[]{:S(2)}) collective-permute-start(bf16[64,128]{1,0:T(8,128)(2,1)S(1)} %get-tuple-element.30), channel_id=1, source_target_pairs={{0,16},{1,18},{2,20},{3,22},{4,17},{5,19},{6,21},{7,23},{8,0},{9,2... | collective-permute-start | bytes 49160 | tf_op jit(solution)/shard_map/ppermute | solution.py:372
Sparse Core Ops, SparseCore 0:
  10.1 43.6 all-gather.2

commit v4 on v2

--- a/solution.py
+++ b/solution.py
@@ -14,9 +14,10 @@
 HALF = WINDOW // 2
 TOK = 128
 SCALE = HD ** (-0.5)
-AXES = ("x", "yh", "yl", "w", "p", "c")
-SIZES = (4, 4, 2, 4, 2, 2)
-NEAR = ("yl", "p", "c")
+AXES = ("xh", "xl", "y", "w", "p", "c")
+SIZES = (2, 2, 8, 4, 2, 2)
+NEAR = ("xl", "p", "c")
+FAR = ("xh", "y")
 CODE = 16
 PAY = 4 * TOK + CODE
 NONE = 99
@@ -34,20 +35,20 @@
 
 def weight_moves():
     moves = []
-    for x, yh, yl, w, p, c in devices():
-        head = 2 * (4 * yl + 2 * p + c) + x // 2
-        source = place(2 * (w // 2) + x % 2, yh, w % 2, head // 4, (head // 2) % 2, head % 2)
-        moves.append((source, place(x, yh, yl, w, p, c)))
+    for xh, xl, y, w, p, c in devices():
+        head = 2 * (4 * xl + 2 * p + c) + y % 2
+        source = place(xh, w // 2, 2 * (y // 2) + w % 2, head // 4, (head // 2) % 2, head % 2)
+        moves.append((source, place(xh, xl, y, w, p, c)))
     return moves
 
 
 def piece_moves(turn):
     moves = []
-    for x, yh, yl, w, p, c in devices():
+    for xh, xl, y, w, p, c in devices():
         piece = (w + turn) % 4
-        head = 2 * (4 * yl + 2 * p + c) + piece % 2
-        owner = place(x, yh, piece // 2, head // 4, (head // 2) % 2, head % 2)
-        moves.append((place(x, yh, yl, w, p, c), owner))
+        head = 2 * (4 * xl + 2 * p + c) + piece % 2
+        owner = place(xh, piece // 2, y, head // 4, (head // 2) % 2, head % 2)
+        moves.append((place(xh, xl, y, w, p, c), owner))
     return moves
 
 
@@ -96,8 +97,7 @@
     return (count > 0.5) & (s_pos <= t_pos)
 
 
-def forward_kernel(pay_ref, after_ref, out_ref, lse_ref):
-    del after_ref
+def forward_kernel(pay_ref, out_ref, lse_ref):
     key = rows(pay_ref, 2 * TOK)
     value = rows(pay_ref, 3 * TOK)
     want, have = hot(pay_ref)
@@ -121,24 +121,24 @@
         lse_ref[lo:ext, :] = jnp.where(lane == 0, stats[0], stats[1])
 
 
-def weight_kernel(out_ref, cot_ref, a_ref, b_ref, c_ref, wg_ref):
-    del a_ref, b_ref, c_ref
+def weight_kernel(out_ref, cot_ref, after_ref, wg_ref):
+    del after_ref
     total = dot(out_ref[...], cot_ref[...], ((1,), (0,)))
     left = lax.broadcasted_iota(jnp.int32, (64, HD), 1) < 64
     for b in range(2):
-        for yh in range(4):
-            upper = total[b * HD : b * HD + 64, yh * HD : (yh + 1) * HD]
-            lower = total[b * HD + 64 : (b + 1) * HD, yh * HD : (yh + 1) * HD]
-            wg_ref[yh, b] = jnp.where(left, upper, pltpu.roll(lower, 64, 1)).astype(BF16)
-            wg_ref[yh, 2 + b] = jnp.where(left, pltpu.roll(upper, 64, 1), lower).astype(BF16)
-
-
-def backward_kernel(x_ref, pay_ref, lse_ref, cot_ref, w0_ref, w1_ref, w2_ref, w3_ref, ret_ref, wbuf, ghbuf):
+        for m in range(4):
+            upper = total[b * HD : b * HD + 64, m * HD : (m + 1) * HD]
+            lower = total[b * HD + 64 : (b + 1) * HD, m * HD : (m + 1) * HD]
+            wg_ref[0, 2 * m, 0, b] = jnp.where(left, upper, pltpu.roll(lower, 64, 1)).astype(BF16)
+            wg_ref[0, 2 * m + 1, 0, b] = jnp.where(left, pltpu.roll(upper, 64, 1), lower).astype(BF16)
+
+
+def backward_kernel(pay_ref, lse_ref, cot_ref, w_ref, ret_ref, wbuf, ghbuf):
     @pl.when(pl.program_id(0) == 0)
     def _():
-        for turn, quarter in enumerate((w0_ref, w1_ref, w2_ref, w3_ref)):
-            first = pl.multiple_of(lax.rem(x_ref[0] + 4 - turn, 4) * 64, 64)
-            wbuf[pl.ds(first, 64), :] = quarter[...]
+        for y in range(8):
+            first = HD * (y % 2) + 32 * (y // 2)
+            wbuf[first : first + 32, :] = w_ref[y]
 
     ghbuf[...] = dot(cot_ref[...], wbuf[...], ((1,), (1,))).astype(BF16)
     key = rows(pay_ref, 2 * TOK)
@@ -235,25 +235,25 @@
     )(queries, keys, values, segment, row_type, pair_index)
 
 
-def run_forward(arrived, after):
+def run_forward(arrived):
     return call(
         forward_kernel,
         (shape((2 * HD, 2 * WINDOW)), shape((2 * WINDOW, HD), F32)),
         flops=4 << 30,
         bytes_accessed=2 << 20,
         grid=(2,),
-        in_specs=[pl.BlockSpec((4, PAY, HD), lambda u: (u, 0, 0)), ANY],
+        in_specs=[pl.BlockSpec((4, PAY, HD), lambda u: (u, 0, 0))],
         out_specs=[
             pl.BlockSpec((2 * HD, WINDOW), lambda u: (0, u)),
             pl.BlockSpec((WINDOW, HD), lambda u: (u, 0)),
         ],
-    )(arrived, after)
+    )(arrived)
 
 
 def run_weight(out, cot, after):
     return call(
         weight_kernel,
-        shape((16, 4, 64, HD)),
+        shape((2, 8, 2, 2, 64, HD)),
         flops=1 << 30,
         bytes_accessed=6 << 20,
         grid=(4,),
@@ -261,12 +261,12 @@
             whole(2 * HD, 2 * WINDOW),
             pl.BlockSpec((2 * WINDOW, 512), lambda i: (0, i)),
         ]
-        + [ANY] * 3,
-        out_specs=pl.BlockSpec((4, 4, 64, HD), lambda i: (i, 0, 0, 0)),
-    )(out, cot, *after)
-
-
-def run_backward(x, arrived, lse, cot, quarters):
+        + [ANY],
+        out_specs=pl.BlockSpec((1, 8, 1, 2, 64, HD), lambda i: (i // 2, 0, i % 2, 0, 0, 0)),
+    )(out, cot, after).reshape(16, 4, 64, HD)
+
+
+def run_backward(arrived, lse, cot, weight):
     width = cot.shape[1]
     return call(
         backward_kernel,
@@ -275,15 +275,14 @@
         bytes_accessed=7 << 20,
         grid=(2,),
         in_specs=[
-            SMEM,
             pl.BlockSpec((4, PAY, HD), lambda u: (u, 0, 0)),
             pl.BlockSpec((WINDOW, HD), lambda u: (u, 0)),
             pl.BlockSpec((WINDOW, width), lambda u: (u, 0)),
-        ]
-        + [whole(64, width)] * 4,
+            whole(8, 32, width),
+        ],
         out_specs=pl.BlockSpec((4, 4 * TOK, HD), lambda u: (u, 0, 0)),
         scratch_shapes=[pltpu.VMEM((2 * HD, width), BF16), pltpu.VMEM((WINDOW, 2 * HD), BF16)],
-    )(x, arrived, lse, cot, *quarters)
+    )(arrived, lse, cot, weight)
 
 
 def run_sum(w, got):
@@ -325,20 +324,19 @@
 
 
 def local(queries, keys, values, cotangent, out_weight, segment, row_type, pair_index):
-    x = lax.axis_index("x").astype(jnp.int32)
+    width = out_weight.shape[1]
+    y = lax.axis_index("y").astype(jnp.int32)
     w = lax.axis_index("w").astype(jnp.int32).reshape(1)
+    share = lax.dynamic_slice_in_dim(out_weight, 32 * lax.div(y, 2), 32, axis=0)
+    eighth = lax.ppermute(share, AXES, weight_moves())
     cot = lax.all_gather(cotangent[0], NEAR, axis=0, tiled=True)
-    share = lax.dynamic_slice_in_dim(out_weight, 64 * lax.rem(x, 2), 64, axis=0)
-    quarter = lax.ppermute(share, AXES, weight_moves())
-    quarters = [quarter] + [
-        lax.ppermute(quarter, "x", [(i, (i + turn) % 4) for i in range(4)]) for turn in (1, 2, 3)
-    ]
     payload = run_pack(queries, keys, values, segment, row_type, pair_index)
     arrived = lax.all_to_all(payload, NEAR, 0, 0)
-    out, lse = run_forward(arrived, quarter)
-    pieces = run_weight(out, cot, quarters[1:])
-    got = lax.all_to_all(pieces, ("x", "yh"), 0, 0)
-    back = run_backward(x.reshape(1), arrived, lse, cot, quarters)
+    weight = lax.all_to_all(jnp.broadcast_to(eighth[None], (8, 32, width)), "y", 0, 0)
+    out, lse = run_forward(arrived)
+    pieces = run_weight(out, cot, weight)
+    got = lax.all_to_all(pieces, FAR, 0, 0)
+    back = run_backward(arrived, lse, cot, weight)
     home = lax.all_to_all(back, NEAR, 0, 0)
     sent = [lax.ppermute(part, AXES, piece_moves(turn)) for turn, part in enumerate(run_sum(w, got))]
     weight_grad = run_spread(sent).T

time: 153 us -> 149 us (0.974)
  starting transfers between devices: 63.2 us -> 51.9 us
  waiting for transfers between devices: 46.7 us -> 53 us
    all_to_all x1 -> x2, waiting for transfers between devices: 12.7 us -> 32.7 us  [the longest x1 20.3 us: local(): lax.all_to_all(jnp.broadcast_to(eighth[None], (8, 32, width)), 'y', 0, 0)]
    ppermute x4 -> x1, starting transfers between devices: 9.36 us -> 1.92 us  [local(): eighth = lax.ppermute(share, AXES, weight_moves())]
    ppermute x4 -> x1, waiting for transfers between devices: 25.9 us -> 19 us  [local(): eighth = lax.ppermute(share, AXES, weight_moves())]
    ppermute x4, starting transfers between devices: 15.6 us -> 22.3 us  [local(): lax.ppermute(part, AXES, piece_moves(turn))]
    ppermute x4, waiting for transfers between devices: 7.32 us -> 0.59 us  [local(): lax.ppermute(part, AXES, piece_moves(turn))]
    all_to_all x1 -> x2, starting transfers between devices: 13.2 us -> 7.36 us  [the longest x1 3.8 us: local(): got = lax.all_to_all(pieces, FAR, 0, 0)]
    all_to_all x1, starting transfers between devices: 14.7 us -> 9.94 us  [local(): home = lax.all_to_all(back, NEAR, 0, 0)]
  transfers between devices with their start and end apart: 12 -> 10, of which waited for: 3 -> 4; matrix products, arithmetic and copies ran while one was open for 0% -> 1% of each run, Pallas kernels for 14% -> 14%
where the time goes in v4:
time: 149 us; the launch traced here: 148 us
  waiting for transfers between devices  53 us (36%)
  starting transfers between devices  51.9 us (35%)
  Pallas kernels  27 us (18%)
  between operations  14.1 us (9%)
  local copies, waits for them, and re-layouts  2.34 us (2%)
    ppermute x4, starting transfers between devices, local(): lax.ppermute(part, AXES, piece_moves(turn))  22.3 us
    all_to_all x1, waiting for transfers between devices, local(): lax.all_to_all(jnp.broadcast_to(eighth[None], (8, 32, width)), 'y', 0, 0)  20.3 us
    ppermute x1, waiting for transfers between devices, local(): eighth = lax.ppermute(share, AXES, weight_moves())  19 us
    all_to_all x1, waiting for transfers between devices, local(): got = lax.all_to_all(pieces, FAR, 0, 0)  12.3 us
    pallas_call x1, Pallas kernels, run_backward(): call(backward_kernel, shape((8, 4 * TOK, HD)), flops=8 << 30, bytes_acces...  10.5 us
    all_to_all x1, starting transfers between devices, local(): arrived = lax.all_to_all(payload, NEAR, 0, 0)  10.3 us
    all_to_all x1, starting transfers between devices, local(): home = lax.all_to_all(back, NEAR, 0, 0)  9.94 us
    pallas_call x1, Pallas kernels, run_forward(): call(forward_kernel, (shape((2 * HD, 2 * WINDOW)), shape((2 * WINDOW, HD)...  5.25 us
  transfers between devices with their start and end apart: 10, of which 4 were waited for; matrix products, arithmetic and copies ran while one was open for 1% of the time, Pallas kernels for 14%

profile of v4, /device:TPU:1, one launch (start us, length us, event | category | flops | bytes accessed | tf_op | source)
XLA Modules:
  0.0 148.4 jit_solution(11127940008946971106)
XLA Ops:
  7.2 0.0 copy-start
  7.2 0.0 all-gather.3.cloned.1.call-start
  7.2 0.7 all-gather.3.cloned.1.call-update
  7.9 3.5 %shard_map.111 = bf16[8,528,128]{2,1,0:T(8,128)(2,1)} custom-call(bf16[1,128,2048]{2,1,0:T(8,128)(2,1)} %q_ref.1, bf16[1,128,1024]{2,1,0:T(8,128)(2,1)} %k_ref.1, bf16[1,128,1024]{2,1,0:T(8,128)(2,1)} %v_ref.1, s32[1,128]{1,0:T(1,128)} %seg_ref.1, s32[1,128]{1,0:T(1,128)} %type_ref.1, s32[1,24]{1,0:T(1,128)} %pair_ref.1), custom_call_target="tpu_custom_call" | custom-call | bytes 2097152 | tf_op jit(solution)/shard_map/pallas_call | solution.py:221
  11.4 10.3 %all-to-all-start = ((bf16[8,528,128]{2,1,0:T(8,128)(2,1)}), bf16[8,528,128]{2,1,0:T(8,128)(2,1)S(1)}, u32[]{:S(2)}, u32[]{:S(2)}) async-start(bf16[8,528,128]{2,1,0:T(8,128)(2,1)} %shard_map.111), calls=%async_computation | async-start | bytes 2162688 | tf_op jit(solution)/shard_map/all_to_all | solution.py:334
  21.7 0.0 copy-done
  21.8 1.9 %collective-permute-start = (bf16[32,2048]{1,0:T(8,128)(2,1)S(1)}, bf16[32,2048]{1,0:T(8,128)(2,1)S(1)}, u32[]{:S(2)}, u32[]{:S(2)}) collective-permute-start(bf16[32,2048]{1,0:T(8,128)(2,1)S(1)} %constant_dynamic-slice_fusion), channel_id=1, source_target_pairs={{0,0},{2,1},{4,2},{6,3},{16,4},{18,5},{20,6},{22,7},{128,8},{130,9... | collective-permute-start | bytes 393224 | tf_op jit(solution)/shard_map/ppermute | solution.py:331
  23.7 19.0 %collective-permute-done = bf16[32,2048]{1,0:T(8,128)(2,1)S(1)} collective-permute-done((bf16[32,2048]{1,0:T(8,128)(2,1)S(1)}, bf16[32,2048]{1,0:T(8,128)(2,1)S(1)}, u32[]{:S(2)}, u32[]{:S(2)}) %collective-permute-start) | collective-permute-done | bytes 131104 | tf_op jit(solution)/shard_map/ppermute | solution.py:331
  42.7 0.0 all-to-all-done.pay_ref
  42.7 0.0 copy-start.2
  42.7 1.2 broadcast_in_dim.2
  43.9 0.1 copy-done.2
  44.0 3.6 %all-to-all-start.1 = ((bf16[8,32,2048]{2,1,0:T(8,128)(2,1)}), bf16[8,32,2048]{2,1,0:T(8,128)(2,1)S(1)}, u32[]{:S(2)}, u32[]{:S(2)}) async-start(bf16[8,32,2048]{2,1,0:T(8,128)(2,1)} %broadcast_in_dim.2), calls=%async_computation.1 | async-start | bytes 2097152 | tf_op jit(solution)/shard_map/all_to_all | solution.py:335
  47.6 5.3 %shard_map.112 = (bf16[256,1024]{1,0:T(8,128)(2,1)}, f32[1024,128]{1,0:T(8,128)}) custom-call(bf16[8,528,128]{2,1,0:T(8,128)(2,1)} %copy-done.2), custom_call_target="tpu_custom_call" | custom-call | flops 4294967296 | bytes 2097152 | tf_op jit(solution)/shard_map/pallas_call | solution.py:239
  52.8 20.3 %all-to-all-done.1.w_ref.after_ref = bf16[8,32,2048]{2,1,0:T(8,128)(2,1)S(1)} async-done(((bf16[8,32,2048]{2,1,0:T(8,128)(2,1)}), bf16[8,32,2048]{2,1,0:T(8,128)(2,1)S(1)}, u32[]{:S(2)}, u32[]{:S(2)}) %all-to-all-start.1) | async-done | bytes 1048608 | tf_op jit(solution)/shard_map/all_to_all | solution.py:335
  73.2 0.0 copy-start.1
  73.2 0.0 all-gather.3.cloned.1.call-done
  73.2 1.0 copy-done.1
  74.2 5.1 %shard_map.115 = bf16[2,8,2,2,64,128]{5,4,3,2,1,0:T(8,128)(2,1)} custom-call(bf16[256,1024]{1,0:T(8,128)(2,1)} %get-tuple-element.17.out_ref, bf16[1024,2048]{1,0:T(8,128)(2,1)} %bitcast.4, bf16[8,32,2048]{2,1,0:T(8,128)(2,1)} %copy-done.1), custom_call_target="tpu_custom_call" | custom-call | flops 1073741824 | bytes 6291456 | tf_op jit(solution)/shard_map/pallas_call | solution.py:254
  79.3 3.8 %all-to-all-start.3 = ((bf16[16,4,64,128]{3,2,1,0:T(8,128)(2,1)}), bf16[16,4,64,128]{3,2,1,0:T(8,128)(2,1)S(1)}, u32[]{:S(2)}, u32[]{:S(2)}) async-start(bf16[16,4,64,128]{3,2,1,0:T(8,128)(2,1)} %bitcast.6), calls=%async_computation.3 | async-start | bytes 2097152 | tf_op jit(solution)/shard_map/all_to_all | solution.py:338
  83.1 10.5 %shard_map.113 = bf16[8,512,128]{2,1,0:T(8,128)(2,1)} custom-call(bf16[8,528,128]{2,1,0:T(8,128)(2,1)} %copy-done.2, f32[1024,128]{1,0:T(8,128)} %get-tuple-element.13.lse_ref, bf16[1024,2048]{1,0:T(8,128)(2,1)} %bitcast.5, bf16[8,32,2048]{2,1,0:T(8,128)(2,1)} %copy-done.1), custom_call_target="tpu_custom_call" | custom-call | flops 8589934592 | bytes 7340032 | tf_op jit(solution)/shard_map/pallas_call | solution.py:271
  93.6 12.3 %all-to-all-done.3.got_ref = bf16[16,4,64,128]{3,2,1,0:T(8,128)(2,1)S(1)} async-done(((bf16[16,4,64,128]{3,2,1,0:T(8,128)(2,1)}), bf16[16,4,64,128]{3,2,1,0:T(8,128)(2,1)S(1)}, u32[]{:S(2)}, u32[]{:S(2)}) %all-to-all-start.3) | async-done | bytes 1048608 | tf_op jit(solution)/shard_map/all_to_all | solution.py:338
  106.0 9.9 %all-to-all-start.2 = ((bf16[8,512,128]{2,1,0:T(8,128)(2,1)}), bf16[8,512,128]{2,1,0:T(8,128)(2,1)S(1)}, u32[]{:S(2)}, u32[]{:S(2)}) async-start(bf16[8,512,128]{2,1,0:T(8,128)(2,1)} %shard_map.113), calls=%async_computation.2 | async-start | bytes 2097152 | tf_op jit(solution)/shard_map/all_to_all | solution.py:340
  115.9 0.2 shard_map.116
  116.1 3.5 %collective-permute-start.1 = (bf16[64,128]{1,0:T(8,128)(2,1)S(1)}, bf16[64,128]{1,0:T(8,128)(2,1)S(1)}, u32[]{:S(2)}, u32[]{:S(2)}) collective-permute-start(bf16[64,128]{1,0:T(8,128)(2,1)S(1)} %get-tuple-element.18), channel_id=1, source_target_pairs={{0,0},{1,2},{2,4},{3,6},{4,1},{5,3},{6,5},{7,7},{8,128},{9,130},{1... | collective-permute-start | bytes 49160 | tf_op jit(solution)/shard_map/ppermute | solution.py:341
  119.7 10.1 %collective-permute-start.2 = (bf16[64,128]{1,0:T(8,128)(2,1)S(1)}, bf16[64,128]{1,0:T(8,128)(2,1)S(1)}, u32[]{:S(2)}, u32[]{:S(2)}) collective-permute-start(bf16[64,128]{1,0:T(8,128)(2,1)S(1)} %get-tuple-element.19), channel_id=1, source_target_pairs={{0,1},{1,3},{2,5},{3,7},{4,128},{5,130},{6,132},{7,134},{8,129},{9... | collective-permute-start | bytes 49160 | tf_op jit(solution)/shard_map/ppermute | solution.py:341
  129.8 1.9 %collective-permute-start.3 = (bf16[64,128]{1,0:T(8,128)(2,1)S(1)}, bf16[64,128]{1,0:T(8,128)(2,1)S(1)}, u32[]{:S(2)}, u32[]{:S(2)}) collective-permute-start(bf16[64,128]{1,0:T(8,128)(2,1)S(1)} %get-tuple-element.20), channel_id=1, source_target_pairs={{0,128},{1,130},{2,132},{3,134},{4,129},{5,131},{6,133},{7,135},{8... | collective-permute-start | bytes 49160 | tf_op jit(solution)/shard_map/ppermute | solution.py:341
  131.7 6.8 %collective-permute-start.4 = (bf16[64,128]{1,0:T(8,128)(2,1)S(1)}, bf16[64,128]{1,0:T(8,128)(2,1)S(1)}, u32[]{:S(2)}, u32[]{:S(2)}) collective-permute-start(bf16[64,128]{1,0:T(8,128)(2,1)S(1)} %get-tuple-element.21), channel_id=1, source_target_pairs={{0,129},{1,131},{2,133},{3,135},{4,0},{5,2},{6,4},{7,6},{8,1},{9,3... | collective-permute-start | bytes 49160 | tf_op jit(solution)/shard_map/ppermute | solution.py:341
  138.5 0.0 all-to-all-done.2.ret_ref
  138.5 1.6 %shard_map.114 = (bf16[1,128,2048]{2,1,0:T(8,128)(2,1)}, bf16[1,128,1024]{2,1,0:T(8,128)(2,1)}, bf16[1,128,1024]{2,1,0:T(8,128)(2,1)}) custom-call(bf16[8,512,128]{2,1,0:T(8,128)(2,1)S(1)} %all-to-all-done.2.ret_ref), custom_call_target="tpu_custom_call" | custom-call | bytes 2097152 | tf_op jit(solution)/shard_map/pallas_call | solution.py:311
  140.1 0.0 collective-permute-done.1.a_ref
  140.1 0.0 collective-permute-done.2.b_ref
  140.1 0.0 collective-permute-done.3.c_ref
  140.1 0.6 collective-permute-done.4.d_ref
  140.7 0.8 shard_map.117
  (1 shorter events, 0.0 us)
Async XLA Ops:
  7.2 14.6 %copy-start = (bf16[128,2048]{1,0:T(8,128)(2,1)S(1)}, bf16[128,2048]{1,0:T(8,128)(2,1)}, u32[]{:S(2)}) copy-start(bf16[128,2048]{1,0:T(8,128)(2,1)} %param.12) | copy-start | bytes 1572868
  7.2 66.0 %all-gather.3.cloned.1.call-start = ((), (), s32[]{:S(2)}) async-start(), calls=%async_computation.4 | async-start | bytes 4718592 | tf_op jit(solution)/shard_map/all_gather | solution.py:332
  11.4 31.3 %all-to-all-start = ((bf16[8,528,128]{2,1,0:T(8,128)(2,1)}), bf16[8,528,128]{2,1,0:T(8,128)(2,1)S(1)}, u32[]{:S(2)}, u32[]{:S(2)}) async-start(bf16[8,528,128]{2,1,0:T(8,128)(2,1)} %shard_map.111), calls=%async_computation | async-start | bytes 2162688 | tf_op jit(solution)/shard_map/all_to_all | solution.py:334
  21.8 20.9 %collective-permute-start = (bf16[32,2048]{1,0:T(8,128)(2,1)S(1)}, bf16[32,2048]{1,0:T(8,128)(2,1)S(1)}, u32[]{:S(2)}, u32[]{:S(2)}) collective-permute-start(bf16[32,2048]{1,0:T(8,128)(2,1)S(1)} %constant_dynamic-slice_fusion), channel_id=1, source_target_pairs={{0,0},{2,1},{4,2},{6,3},{16,4},{18,5},{20,6},{22,7},{128,8},{130,9... | collective-permute-start | bytes 393224 | tf_op jit(solution)/shard_map/ppermute | solution.py:331
  42.7 1.3 copy-start.2
  44.0 29.1 %all-to-all-start.1 = ((bf16[8,32,2048]{2,1,0:T(8,128)(2,1)}), bf16[8,32,2048]{2,1,0:T(8,128)(2,1)S(1)}, u32[]{:S(2)}, u32[]{:S(2)}) async-start(bf16[8,32,2048]{2,1,0:T(8,128)(2,1)} %broadcast_in_dim.2), calls=%async_computation.1 | async-start | bytes 2097152 | tf_op jit(solution)/shard_map/all_to_all | solution.py:335
  73.2 1.0 copy-start.1
  79.3 26.7 %all-to-all-start.3 = ((bf16[16,4,64,128]{3,2,1,0:T(8,128)(2,1)}), bf16[16,4,64,128]{3,2,1,0:T(8,128)(2,1)S(1)}, u32[]{:S(2)}, u32[]{:S(2)}) async-start(bf16[16,4,64,128]{3,2,1,0:T(8,128)(2,1)} %bitcast.6), calls=%async_computation.3 | async-start | bytes 2097152 | tf_op jit(solution)/shard_map/all_to_all | solution.py:338
  106.0 32.5 %all-to-all-start.2 = ((bf16[8,512,128]{2,1,0:T(8,128)(2,1)}), bf16[8,512,128]{2,1,0:T(8,128)(2,1)S(1)}, u32[]{:S(2)}, u32[]{:S(2)}) async-start(bf16[8,512,128]{2,1,0:T(8,128)(2,1)} %shard_map.113), calls=%async_computation.2 | async-start | bytes 2097152 | tf_op jit(solution)/shard_map/all_to_all | solution.py:340
  116.1 24.0 %collective-permute-start.1 = (bf16[64,128]{1,0:T(8,128)(2,1)S(1)}, bf16[64,128]{1,0:T(8,128)(2,1)S(1)}, u32[]{:S(2)}, u32[]{:S(2)}) collective-permute-start(bf16[64,128]{1,0:T(8,128)(2,1)S(1)} %get-tuple-element.18), channel_id=1, source_target_pairs={{0,0},{1,2},{2,4},{3,6},{4,1},{5,3},{6,5},{7,7},{8,128},{9,130},{1... | collective-permute-start | bytes 49160 | tf_op jit(solution)/shard_map/ppermute | solution.py:341
  119.7 20.4 %collective-permute-start.2 = (bf16[64,128]{1,0:T(8,128)(2,1)S(1)}, bf16[64,128]{1,0:T(8,128)(2,1)S(1)}, u32[]{:S(2)}, u32[]{:S(2)}) collective-permute-start(bf16[64,128]{1,0:T(8,128)(2,1)S(1)} %get-tuple-element.19), channel_id=1, source_target_pairs={{0,1},{1,3},{2,5},{3,7},{4,128},{5,130},{6,132},{7,134},{8,129},{9... | collective-permute-start | bytes 49160 | tf_op jit(solution)/shard_map/ppermute | solution.py:341
  129.8 10.3 %collective-permute-start.3 = (bf16[64,128]{1,0:T(8,128)(2,1)S(1)}, bf16[64,128]{1,0:T(8,128)(2,1)S(1)}, u32[]{:S(2)}, u32[]{:S(2)}) collective-permute-start(bf16[64,128]{1,0:T(8,128)(2,1)S(1)} %get-tuple-element.20), channel_id=1, source_target_pairs={{0,128},{1,130},{2,132},{3,134},{4,129},{5,131},{6,133},{7,135},{8... | collective-permute-start | bytes 49160 | tf_op jit(solution)/shard_map/ppermute | solution.py:341
  131.7 9.0 %collective-permute-start.4 = (bf16[64,128]{1,0:T(8,128)(2,1)S(1)}, bf16[64,128]{1,0:T(8,128)(2,1)S(1)}, u32[]{:S(2)}, u32[]{:S(2)}) collective-permute-start(bf16[64,128]{1,0:T(8,128)(2,1)S(1)} %get-tuple-element.21), channel_id=1, source_target_pairs={{0,129},{1,131},{2,133},{3,135},{4,0},{5,2},{6,4},{7,6},{8,1},{9,3... | collective-permute-start | bytes 49160 | tf_op jit(solution)/shard_map/ppermute | solution.py:341
Sparse Core Ops, SparseCore 0:
  10.2 47.4 all-gather.2

commit v5 on v2

--- a/solution.py
+++ b/solution.py
@@ -17,6 +17,7 @@
 AXES = ("x", "yh", "yl", "w", "p", "c")
 SIZES = (4, 4, 2, 4, 2, 2)
 NEAR = ("yl", "p", "c")
+FAR = ("x", "yh")
 CODE = 16
 PAY = 4 * TOK + CODE
 NONE = 99
@@ -32,11 +33,15 @@
     return itertools.product(*map(range, SIZES))
 
 
+def key_head(yl, p, c):
+    return yl + 2 * p + 4 * c
+
+
 def weight_moves():
     moves = []
     for x, yh, yl, w, p, c in devices():
-        head = 2 * (4 * yl + 2 * p + c) + x // 2
-        source = place(2 * (w // 2) + x % 2, yh, w % 2, head // 4, (head // 2) % 2, head % 2)
+        head = 2 * key_head(yl, p, c) + x // 2
+        source = place(2 * (w // 2) + x % 2, yh, (w + head) % 2, head // 4, (head // 2) % 2, head % 2)
         moves.append((source, place(x, yh, yl, w, p, c)))
     return moves
 
@@ -45,7 +50,7 @@
     moves = []
     for x, yh, yl, w, p, c in devices():
         piece = (w + turn) % 4
-        head = 2 * (4 * yl + 2 * p + c) + piece % 2
+        head = 2 * key_head(yl, p, c) + piece % 2
         owner = place(x, yh, piece // 2, head // 4, (head // 2) % 2, head % 2)
         moves.append((place(x, yh, yl, w, p, c), owner))
     return moves
@@ -68,11 +73,11 @@
     code = jnp.where(row == 0, seg, jnp.where(row == 1, as_query, jnp.where(row == 2, as_key, 0)))
     code = code.astype(F32).astype(BF16)
     for g in range(2):
-        out_ref[g, 0:TOK, :] = q_ref[0, :, 2 * g * HD : (2 * g + 1) * HD]
-        out_ref[g, TOK : 2 * TOK, :] = q_ref[0, :, (2 * g + 1) * HD : (2 * g + 2) * HD]
-        out_ref[g, 2 * TOK : 3 * TOK, :] = k_ref[0, :, g * HD : (g + 1) * HD]
-        out_ref[g, 3 * TOK : 4 * TOK, :] = v_ref[0, :, g * HD : (g + 1) * HD]
-        out_ref[g, 4 * TOK :, :] = code
+        out_ref[g, 0, 0:TOK, :] = q_ref[0, :, 2 * g * HD : (2 * g + 1) * HD]
+        out_ref[g, 0, TOK : 2 * TOK, :] = q_ref[0, :, (2 * g + 1) * HD : (2 * g + 2) * HD]
+        out_ref[g, 0, 2 * TOK : 3 * TOK, :] = k_ref[0, :, g * HD : (g + 1) * HD]
+        out_ref[g, 0, 3 * TOK : 4 * TOK, :] = v_ref[0, :, g * HD : (g + 1) * HD]
+        out_ref[g, 0, 4 * TOK :, :] = code
 
 
 def rows(pay_ref, first):
@@ -96,8 +101,7 @@
     return (count > 0.5) & (s_pos <= t_pos)
 
 
-def forward_kernel(pay_ref, after_ref, out_ref, lse_ref):
-    del after_ref
+def forward_kernel(pay_ref, out_ref, lse_ref):
     key = rows(pay_ref, 2 * TOK)
     value = rows(pay_ref, 3 * TOK)
     want, have = hot(pay_ref)
@@ -121,8 +125,7 @@
         lse_ref[lo:ext, :] = jnp.where(lane == 0, stats[0], stats[1])
 
 
-def weight_kernel(out_ref, cot_ref, a_ref, b_ref, c_ref, wg_ref):
-    del a_ref, b_ref, c_ref
+def weight_kernel(out_ref, cot_ref, wg_ref):
     total = dot(out_ref[...], cot_ref[...], ((1,), (0,)))
     left = lax.broadcasted_iota(jnp.int32, (64, HD), 1) < 64
     for b in range(2):
@@ -133,14 +136,8 @@
             wg_ref[yh, 2 + b] = jnp.where(left, pltpu.roll(upper, 64, 1), lower).astype(BF16)
 
 
-def backward_kernel(x_ref, pay_ref, lse_ref, cot_ref, w0_ref, w1_ref, w2_ref, w3_ref, ret_ref, wbuf, ghbuf):
-    @pl.when(pl.program_id(0) == 0)
-    def _():
-        for turn, quarter in enumerate((w0_ref, w1_ref, w2_ref, w3_ref)):
-            first = pl.multiple_of(lax.rem(x_ref[0] + 4 - turn, 4) * 64, 64)
-            wbuf[pl.ds(first, 64), :] = quarter[...]
-
-    ghbuf[...] = dot(cot_ref[...], wbuf[...], ((1,), (1,))).astype(BF16)
+def backward_kernel(pay_ref, lse_ref, cot_ref, w_ref, ret_ref, ghbuf):
+    ghbuf[...] = dot(cot_ref[...], w_ref[...], ((1,), (1,))).astype(BF16)
     key = rows(pay_ref, 2 * TOK)
     value = rows(pay_ref, 3 * TOK)
     want, have = hot(pay_ref)
@@ -177,10 +174,10 @@
 
 def unpack_kernel(ret_ref, dq_ref, dk_ref, dv_ref):
     for g in range(2):
-        dq_ref[0, :, 2 * g * HD : (2 * g + 1) * HD] = ret_ref[g, 0:TOK, :]
-        dq_ref[0, :, (2 * g + 1) * HD : (2 * g + 2) * HD] = ret_ref[g, TOK : 2 * TOK, :]
-        dk_ref[0, :, g * HD : (g + 1) * HD] = ret_ref[g, 2 * TOK : 3 * TOK, :]
-        dv_ref[0, :, g * HD : (g + 1) * HD] = ret_ref[g, 3 * TOK : 4 * TOK, :]
+        dq_ref[0, :, 2 * g * HD : (2 * g + 1) * HD] = ret_ref[g, 0, 0:TOK, :]
+        dq_ref[0, :, (2 * g + 1) * HD : (2 * g + 2) * HD] = ret_ref[g, 0, TOK : 2 * TOK, :]
+        dk_ref[0, :, g * HD : (g + 1) * HD] = ret_ref[g, 0, 2 * TOK : 3 * TOK, :]
+        dv_ref[0, :, g * HD : (g + 1) * HD] = ret_ref[g, 0, 3 * TOK : 4 * TOK, :]
 
 
 def sum_kernel(w_ref, got_ref, out0_ref, out1_ref, out2_ref, out3_ref, total):
@@ -196,11 +193,14 @@
 
 
 SMEM = pl.BlockSpec(memory_space=pltpu.SMEM)
-ANY = pl.BlockSpec(memory_space=pl.ANY)
 
 
 def whole(*dims):
     return pl.BlockSpec(dims, lambda *_: (0,) * len(dims))
+
+
+def pair_of_heads(i):
+    return 0, 2 * (i % 2) + i // 2, 0, 0
 
 
 def call(kernel, out_shape, flops=0, bytes_accessed=0, room=60, **kw):
@@ -220,7 +220,7 @@
 def run_pack(queries, keys, values, segment, row_type, pair_index):
     return call(
         pack_kernel,
-        shape((8, PAY, HD)),
+        shape((2, 4, PAY, HD)),
         bytes_accessed=2 << 20,
         grid=(4,),
         in_specs=[
@@ -231,26 +231,26 @@
             whole(1, TOK),
             SMEM,
         ],
-        out_specs=pl.BlockSpec((2, PAY, HD), lambda i: (i, 0, 0)),
-    )(queries, keys, values, segment, row_type, pair_index)
-
-
-def run_forward(arrived, after):
+        out_specs=pl.BlockSpec((2, 1, PAY, HD), pair_of_heads),
+    )(queries, keys, values, segment, row_type, pair_index).reshape(8, PAY, HD)
+
+
+def run_forward(arrived):
     return call(
         forward_kernel,
         (shape((2 * HD, 2 * WINDOW)), shape((2 * WINDOW, HD), F32)),
         flops=4 << 30,
         bytes_accessed=2 << 20,
         grid=(2,),
-        in_specs=[pl.BlockSpec((4, PAY, HD), lambda u: (u, 0, 0)), ANY],
+        in_specs=[pl.BlockSpec((4, PAY, HD), lambda u: (u, 0, 0))],
         out_specs=[
             pl.BlockSpec((2 * HD, WINDOW), lambda u: (0, u)),
             pl.BlockSpec((WINDOW, HD), lambda u: (u, 0)),
         ],
-    )(arrived, after)
-
-
-def run_weight(out, cot, after):
+    )(arrived)
+
+
+def run_weight(out, cot):
     return call(
         weight_kernel,
         shape((16, 4, 64, HD)),
@@ -260,13 +260,12 @@
         in_specs=[
             whole(2 * HD, 2 * WINDOW),
             pl.BlockSpec((2 * WINDOW, 512), lambda i: (0, i)),
-        ]
-        + [ANY] * 3,
+        ],
         out_specs=pl.BlockSpec((4, 4, 64, HD), lambda i: (i, 0, 0, 0)),
-    )(out, cot, *after)
-
-
-def run_backward(x, arrived, lse, cot, quarters):
+    )(out, cot)
+
+
+def run_backward(arrived, lse, cot, weight):
     width = cot.shape[1]
     return call(
         backward_kernel,
@@ -275,15 +274,14 @@
         bytes_accessed=7 << 20,
         grid=(2,),
         in_specs=[
-            SMEM,
             pl.BlockSpec((4, PAY, HD), lambda u: (u, 0, 0)),
             pl.BlockSpec((WINDOW, HD), lambda u: (u, 0)),
             pl.BlockSpec((WINDOW, width), lambda u: (u, 0)),
-        ]
-        + [whole(64, width)] * 4,
+            whole(2 * HD, width),
+        ],
         out_specs=pl.BlockSpec((4, 4 * TOK, HD), lambda u: (u, 0, 0)),
-        scratch_shapes=[pltpu.VMEM((2 * HD, width), BF16), pltpu.VMEM((WINDOW, 2 * HD), BF16)],
-    )(x, arrived, lse, cot, *quarters)
+        scratch_shapes=[pltpu.VMEM((WINDOW, 2 * HD), BF16)],
+    )(arrived, lse, cot, weight)
 
 
 def run_sum(w, got):
@@ -315,30 +313,28 @@
         room=16,
         bytes_accessed=2 << 20,
         grid=(4,),
-        in_specs=[pl.BlockSpec((2, 4 * TOK, HD), lambda i: (i, 0, 0))],
+        in_specs=[pl.BlockSpec((2, 1, 4 * TOK, HD), pair_of_heads)],
         out_specs=[
             pl.BlockSpec((1, TOK, 4 * HD), lambda i: (0, 0, i)),
             pl.BlockSpec((1, TOK, 2 * HD), lambda i: (0, 0, i)),
             pl.BlockSpec((1, TOK, 2 * HD), lambda i: (0, 0, i)),
         ],
-    )(home)
+    )(home.reshape(2, 4, 4 * TOK, HD))
 
 
 def local(queries, keys, values, cotangent, out_weight, segment, row_type, pair_index):
     x = lax.axis_index("x").astype(jnp.int32)
     w = lax.axis_index("w").astype(jnp.int32).reshape(1)
-    cot = lax.all_gather(cotangent[0], NEAR, axis=0, tiled=True)
     share = lax.dynamic_slice_in_dim(out_weight, 64 * lax.rem(x, 2), 64, axis=0)
     quarter = lax.ppermute(share, AXES, weight_moves())
-    quarters = [quarter] + [
-        lax.ppermute(quarter, "x", [(i, (i + turn) % 4) for i in range(4)]) for turn in (1, 2, 3)
-    ]
+    cot = lax.all_gather(cotangent[0], NEAR, axis=0, tiled=True)
     payload = run_pack(queries, keys, values, segment, row_type, pair_index)
     arrived = lax.all_to_all(payload, NEAR, 0, 0)
-    out, lse = run_forward(arrived, quarter)
-    pieces = run_weight(out, cot, quarters[1:])
-    got = lax.all_to_all(pieces, ("x", "yh"), 0, 0)
-    back = run_backward(x.reshape(1), arrived, lse, cot, quarters)
+    weight = lax.all_gather(quarter, "x", axis=0, tiled=True)
+    out, lse = run_forward(arrived)
+    pieces = run_weight(out, cot)
+    got = lax.all_to_all(pieces, FAR, 0, 0)
+    back = run_backward(arrived, lse, cot, weight)
     home = lax.all_to_all(back, NEAR, 0, 0)
     sent = [lax.ppermute(part, AXES, piece_moves(turn)) for turn, part in enumerate(run_sum(w, got))]
     weight_grad = run_spread(sent).T

time: 153 us -> 152 us (level)
  starting transfers between devices: 63.2 us -> 49.6 us
  waiting for transfers between devices: 46.7 us -> 59.4 us
    all_gather x0 -> x1, waiting for transfers between devices: none -> 25.4 us  [local(): weight = lax.all_gather(quarter, 'x', axis=0, tiled=True)]
    all_to_all x1, waiting for transfers between devices: 12.7 us -> 0.01 us  [local(): got = lax.all_to_all(pieces, FAR, 0, 0)]
    all_to_all x1, starting transfers between devices: 14.7 us -> 7.05 us  [local(): home = lax.all_to_all(back, NEAR, 0, 0)]
    ppermute x3 -> x0, starting transfers between devices: 7.44 us -> none  [local(): lax.ppermute(quarter, 'x', [(i, (i + turn) % 4) for i in range(4)])]
    all_to_all x1, starting transfers between devices: 13.2 us -> 6.36 us  [local(): got = lax.all_to_all(pieces, FAR, 0, 0)]
    ppermute x4, starting transfers between devices: 15.6 us -> 21.7 us  [local(): lax.ppermute(part, AXES, piece_moves(turn))]
    all_gather x1, waiting for transfers between devices: 0.02 us -> 6.11 us  [local(): cot = lax.all_gather(cotangent[0], NEAR, axis=0, tiled=True)]
    ppermute x4, waiting for transfers between devices: 7.32 us -> 3.66 us  [local(): lax.ppermute(part, AXES, piece_moves(turn))]
  transfers between devices with their start and end apart: 12 -> 10, of which waited for: 3 -> 4; matrix products, arithmetic and copies ran while one was open for 0% -> 0% of each run, Pallas kernels for 14% -> 17%
where the time goes in v5:
time: 152 us
  waiting for transfers between devices  59.4 us (39%)
  starting transfers between devices  49.6 us (33%)
  Pallas kernels  27 us (18%)
  between operations  14.1 us (9%)
  local copies, waits for them, and re-layouts  1.75 us (1%)
    all_gather x1, waiting for transfers between devices, local(): weight = lax.all_gather(quarter, 'x', axis=0, tiled=True)  25.4 us
    ppermute x1, waiting for transfers between devices, local(): quarter = lax.ppermute(share, AXES, weight_moves())  23.6 us
    ppermute x4, starting transfers between devices, local(): lax.ppermute(part, AXES, piece_moves(turn))  21.7 us
    pallas_call x1, Pallas kernels, run_backward(): call(backward_kernel, shape((8, 4 * TOK, HD)), flops=8 << 30, bytes_acces...  10.4 us
    all_to_all x1, starting transfers between devices, local(): arrived = lax.all_to_all(payload, NEAR, 0, 0)  10.3 us
    all_to_all x1, starting transfers between devices, local(): home = lax.all_to_all(back, NEAR, 0, 0)  7.05 us
    all_to_all x1, starting transfers between devices, local(): got = lax.all_to_all(pieces, FAR, 0, 0)  6.36 us
    all_gather x1, waiting for transfers between devices, local(): cot = lax.all_gather(cotangent[0], NEAR, axis=0, tiled=True)  6.11 us
  transfers between devices with their start and end apart: 10, of which 4 were waited for; matrix products, arithmetic and copies ran while one was open for 0% of the time, Pallas kernels for 17%

profile of v5, /device:TPU:1, one launch (start us, length us, event | category | flops | bytes accessed | tf_op | source)
XLA Modules:
  0.0 151.9 jit_solution(18441162577972358125)
XLA Ops:
  7.2 0.0 copy-start
  7.2 0.0 all-gather.6.cloned.1.call-start
  7.2 0.7 all-gather.6.cloned.1.call-update
  7.9 3.5 %shard_map.111 = bf16[2,4,528,128]{3,2,1,0:T(8,128)(2,1)} custom-call(bf16[1,128,2048]{2,1,0:T(8,128)(2,1)} %q_ref.1, bf16[1,128,1024]{2,1,0:T(8,128)(2,1)} %k_ref.1, bf16[1,128,1024]{2,1,0:T(8,128)(2,1)} %v_ref.1, s32[1,128]{1,0:T(1,128)} %seg_ref.1, s32[1,128]{1,0:T(1,128)} %type_ref.1, s32[1,24]{1,0:T(1,128)} %pair_ref.1), custom_call_target="tpu_custom_call" | custom-call | bytes 2097152 | tf_op jit(solution)/shard_map/pallas_call | solution.py:221
  11.5 10.3 %all-to-all-start = ((bf16[8,528,128]{2,1,0:T(8,128)(2,1)}), bf16[8,528,128]{2,1,0:T(8,128)(2,1)S(1)}, u32[]{:S(2)}, u32[]{:S(2)}) async-start(bf16[8,528,128]{2,1,0:T(8,128)(2,1)} %bitcast.6), calls=%async_computation | async-start | bytes 2162688 | tf_op jit(solution)/shard_map/all_to_all | solution.py:332
  21.8 0.0 all-gather.4.cloned.1.call-start
  21.8 0.0 copy-done
  21.8 4.0 %collective-permute-start = (bf16[64,2048]{1,0:T(8,128)(2,1)S(1)}, bf16[64,2048]{1,0:T(8,128)(2,1)S(1)}, u32[]{:S(2)}, u32[]{:S(2)}) collective-permute-start(bf16[64,2048]{1,0:T(8,128)(2,1)S(1)} %constant_dynamic-slice_fusion), channel_id=1, source_target_pairs={{0,0},{8,1},{4,2},{12,3},{16,4},{24,5},{20,6},{28,7},{256,8},{264,... | collective-permute-start | bytes 786440 | tf_op jit(solution)/shard_map/ppermute | solution.py:329
  25.9 23.6 %collective-permute-done = bf16[64,2048]{1,0:T(8,128)(2,1)S(1)} collective-permute-done((bf16[64,2048]{1,0:T(8,128)(2,1)S(1)}, bf16[64,2048]{1,0:T(8,128)(2,1)S(1)}, u32[]{:S(2)}, u32[]{:S(2)}) %collective-permute-start) | collective-permute-done | bytes 262176 | tf_op jit(solution)/shard_map/ppermute | solution.py:329
  49.4 0.0 copy-start.2
  49.4 0.7 copy-done.2
  50.1 0.0 all-gather.4.cloned.1.call-update
  50.2 0.0 all-to-all-done.pay_ref
  50.2 0.0 copy-start.1
  50.2 1.0 copy-done.1
  51.2 5.3 %shard_map.112 = (bf16[256,1024]{1,0:T(8,128)(2,1)}, f32[1024,128]{1,0:T(8,128)}) custom-call(bf16[8,528,128]{2,1,0:T(8,128)(2,1)} %copy-done.1), custom_call_target="tpu_custom_call" | custom-call | flops 4294967296 | bytes 2097152 | tf_op jit(solution)/shard_map/pallas_call | solution.py:239
  56.4 6.1 %all-gather.6.cloned.1.call-done = bf16[1,1024,2048]{2,1,0:T(8,128)(2,1)} async-done(((bf16[1,128,2048]{2,1,0:T(8,128)(2,1)}), bf16[1,1024,2048]{2,1,0:T(8,128)(2,1)}) %all-gather.6.cloned.1.call-update) | async-done | bytes 4194320 | tf_op jit(solution)/shard_map/all_gather | solution.py:330
  62.6 5.1 %shard_map.115 = bf16[16,4,64,128]{3,2,1,0:T(8,128)(2,1)} custom-call(bf16[256,1024]{1,0:T(8,128)(2,1)} %get-tuple-element.17.out_ref, bf16[1024,2048]{1,0:T(8,128)(2,1)} %bitcast.7), custom_call_target="tpu_custom_call" | custom-call | flops 1073741824 | bytes 6291456 | tf_op jit(solution)/shard_map/pallas_call | solution.py:254
  67.7 6.4 %all-to-all-start.2 = ((bf16[16,4,64,128]{3,2,1,0:T(8,128)(2,1)}), bf16[16,4,64,128]{3,2,1,0:T(8,128)(2,1)S(1)}, u32[]{:S(2)}, u32[]{:S(2)}) async-start(bf16[16,4,64,128]{3,2,1,0:T(8,128)(2,1)} %shard_map.115), calls=%async_computation.2 | async-start | bytes 2097152 | tf_op jit(solution)/shard_map/all_to_all | solution.py:336
  74.0 25.4 %all-gather.4.cloned.1.call-done.w_ref = bf16[256,2048]{1,0:T(8,128)(2,1)} async-done(((bf16[64,2048]{1,0:T(8,128)(2,1)}), bf16[256,2048]{1,0:T(8,128)(2,1)}) %all-gather.4.cloned.1.call-update) | async-done | bytes 1048592 | tf_op jit(solution)/shard_map/all_gather | solution.py:333
  99.4 10.4 %shard_map.113 = bf16[8,512,128]{2,1,0:T(8,128)(2,1)} custom-call(bf16[8,528,128]{2,1,0:T(8,128)(2,1)} %copy-done.1, f32[1024,128]{1,0:T(8,128)} %get-tuple-element.13.lse_ref, bf16[1024,2048]{1,0:T(8,128)(2,1)} %bitcast.8, bf16[256,2048]{1,0:T(8,128)(2,1)} %all-gather.4.cloned.1.call-done.w_ref), custom_call_target="tpu_custom_call" | custom-call | flops 8589934592 | bytes 7340032 | tf_op jit(solution)/shard_map/pallas_call | solution.py:270
  109.8 0.0 all-to-all-done.2.got_ref
  109.8 7.1 %all-to-all-start.1 = ((bf16[8,512,128]{2,1,0:T(8,128)(2,1)}), bf16[8,512,128]{2,1,0:T(8,128)(2,1)S(1)}, u32[]{:S(2)}, u32[]{:S(2)}) async-start(bf16[8,512,128]{2,1,0:T(8,128)(2,1)} %shard_map.113), calls=%async_computation.1 | async-start | bytes 2097152 | tf_op jit(solution)/shard_map/all_to_all | solution.py:338
  116.9 0.2 shard_map.116
  117.1 8.0 %collective-permute-start.1 = (bf16[64,128]{1,0:T(8,128)(2,1)S(1)}, bf16[64,128]{1,0:T(8,128)(2,1)S(1)}, u32[]{:S(2)}, u32[]{:S(2)}) collective-permute-start(bf16[64,128]{1,0:T(8,128)(2,1)S(1)} %get-tuple-element.18), channel_id=1, source_target_pairs={{0,0},{1,8},{2,4},{3,12},{4,1},{5,9},{6,5},{7,13},{8,16},{9,24},{1... | collective-permute-start | bytes 49160 | tf_op jit(solution)/shard_map/ppermute | solution.py:339
  125.1 3.7 %collective-permute-start.2 = (bf16[64,128]{1,0:T(8,128)(2,1)S(1)}, bf16[64,128]{1,0:T(8,128)(2,1)S(1)}, u32[]{:S(2)}, u32[]{:S(2)}) collective-permute-start(bf16[64,128]{1,0:T(8,128)(2,1)S(1)} %get-tuple-element.19), channel_id=1, source_target_pairs={{0,1},{1,9},{2,5},{3,13},{4,16},{5,24},{6,20},{7,28},{8,17},{9,25}... | collective-permute-start | bytes 49160 | tf_op jit(solution)/shard_map/ppermute | solution.py:339
  128.7 6.5 %collective-permute-start.3 = (bf16[64,128]{1,0:T(8,128)(2,1)S(1)}, bf16[64,128]{1,0:T(8,128)(2,1)S(1)}, u32[]{:S(2)}, u32[]{:S(2)}) collective-permute-start(bf16[64,128]{1,0:T(8,128)(2,1)S(1)} %get-tuple-element.20), channel_id=1, source_target_pairs={{0,16},{1,24},{2,20},{3,28},{4,17},{5,25},{6,21},{7,29},{8,0},{9,8... | collective-permute-start | bytes 49160 | tf_op jit(solution)/shard_map/ppermute | solution.py:339
  135.3 3.6 %collective-permute-start.4 = (bf16[64,128]{1,0:T(8,128)(2,1)S(1)}, bf16[64,128]{1,0:T(8,128)(2,1)S(1)}, u32[]{:S(2)}, u32[]{:S(2)}) collective-permute-start(bf16[64,128]{1,0:T(8,128)(2,1)S(1)} %get-tuple-element.21), channel_id=1, source_target_pairs={{0,17},{1,25},{2,21},{3,29},{4,0},{5,8},{6,4},{7,12},{8,1},{9,9},{... | collective-permute-start | bytes 49160 | tf_op jit(solution)/shard_map/ppermute | solution.py:339
  138.9 0.0 all-to-all-done.1
  138.9 1.7 %shard_map.114 = (bf16[1,128,2048]{2,1,0:T(8,128)(2,1)}, bf16[1,128,1024]{2,1,0:T(8,128)(2,1)}, bf16[1,128,1024]{2,1,0:T(8,128)(2,1)}) custom-call(bf16[2,4,512,128]{3,2,1,0:T(8,128)(2,1)S(1)} %bitcast.5), custom_call_target="tpu_custom_call" | custom-call | bytes 2097152 | tf_op jit(solution)/shard_map/pallas_call | solution.py:310
  140.6 0.0 collective-permute-done.1.a_ref
  140.6 0.0 collective-permute-done.2.b_ref
  140.6 0.0 collective-permute-done.3.c_ref
  140.6 3.6 %collective-permute-done.4.d_ref = bf16[64,128]{1,0:T(8,128)(2,1)S(1)} collective-permute-done((bf16[64,128]{1,0:T(8,128)(2,1)S(1)}, bf16[64,128]{1,0:T(8,128)(2,1)S(1)}, u32[]{:S(2)}, u32[]{:S(2)}) %collective-permute-start.4) | collective-permute-done | bytes 16416 | tf_op jit(solution)/shard_map/ppermute | solution.py:339
  144.2 0.8 shard_map.117
  (1 shorter events, 0.0 us)
Async XLA Ops:
  7.2 14.6 %copy-start = (bf16[128,2048]{1,0:T(8,128)(2,1)S(1)}, bf16[128,2048]{1,0:T(8,128)(2,1)}, u32[]{:S(2)}) copy-start(bf16[128,2048]{1,0:T(8,128)(2,1)} %param.12) | copy-start | bytes 1572868
  7.2 55.4 %all-gather.6.cloned.1.call-start = ((), (), s32[]{:S(2)}) async-start(), calls=%async_computation.4 | async-start | bytes 4718592 | tf_op jit(solution)/shard_map/all_gather | solution.py:330
  11.5 38.7 %all-to-all-start = ((bf16[8,528,128]{2,1,0:T(8,128)(2,1)}), bf16[8,528,128]{2,1,0:T(8,128)(2,1)S(1)}, u32[]{:S(2)}, u32[]{:S(2)}) async-start(bf16[8,528,128]{2,1,0:T(8,128)(2,1)} %bitcast.6), calls=%async_computation | async-start | bytes 2162688 | tf_op jit(solution)/shard_map/all_to_all | solution.py:332
  21.8 77.6 %all-gather.4.cloned.1.call-start = ((), (), s32[]{:S(2)}) async-start(), calls=%async_computation.3 | async-start | bytes 1310720 | tf_op jit(solution)/shard_map/all_gather | solution.py:333
  21.8 27.6 %collective-permute-start = (bf16[64,2048]{1,0:T(8,128)(2,1)S(1)}, bf16[64,2048]{1,0:T(8,128)(2,1)S(1)}, u32[]{:S(2)}, u32[]{:S(2)}) collective-permute-start(bf16[64,2048]{1,0:T(8,128)(2,1)S(1)} %constant_dynamic-slice_fusion), channel_id=1, source_target_pairs={{0,0},{8,1},{4,2},{12,3},{16,4},{24,5},{20,6},{28,7},{256,8},{264,... | collective-permute-start | bytes 786440 | tf_op jit(solution)/shard_map/ppermute | solution.py:329
  49.4 0.7 copy-start.2
  50.2 1.0 copy-start.1
  67.7 42.2 %all-to-all-start.2 = ((bf16[16,4,64,128]{3,2,1,0:T(8,128)(2,1)}), bf16[16,4,64,128]{3,2,1,0:T(8,128)(2,1)S(1)}, u32[]{:S(2)}, u32[]{:S(2)}) async-start(bf16[16,4,64,128]{3,2,1,0:T(8,128)(2,1)} %shard_map.115), calls=%async_computation.2 | async-start | bytes 2097152 | tf_op jit(solution)/shard_map/all_to_all | solution.py:336
  109.8 29.0 %all-to-all-start.1 = ((bf16[8,512,128]{2,1,0:T(8,128)(2,1)}), bf16[8,512,128]{2,1,0:T(8,128)(2,1)S(1)}, u32[]{:S(2)}, u32[]{:S(2)}) async-start(bf16[8,512,128]{2,1,0:T(8,128)(2,1)} %shard_map.113), calls=%async_computation.1 | async-start | bytes 2097152 | tf_op jit(solution)/shard_map/all_to_all | solution.py:338
  117.1 23.5 %collective-permute-start.1 = (bf16[64,128]{1,0:T(8,128)(2,1)S(1)}, bf16[64,128]{1,0:T(8,128)(2,1)S(1)}, u32[]{:S(2)}, u32[]{:S(2)}) collective-permute-start(bf16[64,128]{1,0:T(8,128)(2,1)S(1)} %get-tuple-element.18), channel_id=1, source_target_pairs={{0,0},{1,8},{2,4},{3,12},{4,1},{5,9},{6,5},{7,13},{8,16},{9,24},{1... | collective-permute-start | bytes 49160 | tf_op jit(solution)/shard_map/ppermute | solution.py:339
  125.1 15.5 %collective-permute-start.2 = (bf16[64,128]{1,0:T(8,128)(2,1)S(1)}, bf16[64,128]{1,0:T(8,128)(2,1)S(1)}, u32[]{:S(2)}, u32[]{:S(2)}) collective-permute-start(bf16[64,128]{1,0:T(8,128)(2,1)S(1)} %get-tuple-element.19), channel_id=1, source_target_pairs={{0,1},{1,9},{2,5},{3,13},{4,16},{5,24},{6,20},{7,28},{8,17},{9,25}... | collective-permute-start | bytes 49160 | tf_op jit(solution)/shard_map/ppermute | solution.py:339
  128.7 11.9 %collective-permute-start.3 = (bf16[64,128]{1,0:T(8,128)(2,1)S(1)}, bf16[64,128]{1,0:T(8,128)(2,1)S(1)}, u32[]{:S(2)}, u32[]{:S(2)}) collective-permute-start(bf16[64,128]{1,0:T(8,128)(2,1)S(1)} %get-tuple-element.20), channel_id=1, source_target_pairs={{0,16},{1,24},{2,20},{3,28},{4,17},{5,25},{6,21},{7,29},{8,0},{9,8... | collective-permute-start | bytes 49160 | tf_op jit(solution)/shard_map/ppermute | solution.py:339
  135.3 9.0 %collective-permute-start.4 = (bf16[64,128]{1,0:T(8,128)(2,1)S(1)}, bf16[64,128]{1,0:T(8,128)(2,1)S(1)}, u32[]{:S(2)}, u32[]{:S(2)}) collective-permute-start(bf16[64,128]{1,0:T(8,128)(2,1)S(1)} %get-tuple-element.21), channel_id=1, source_target_pairs={{0,17},{1,25},{2,21},{3,29},{4,0},{5,8},{6,4},{7,12},{8,1},{9,9},{... | collective-permute-start | bytes 49160 | tf_op jit(solution)/shard_map/ppermute | solution.py:339
Sparse Core Ops, SparseCore 0:
  10.2 52.3 all-gather.5
  65.2 34.1 all-gather.3

commit v6 on v5

--- a/solution.py
+++ b/solution.py
@@ -14,10 +14,11 @@
 HALF = WINDOW // 2
 TOK = 128
 SCALE = HD ** (-0.5)
-AXES = ("x", "yh", "yl", "w", "p", "c")
-SIZES = (4, 4, 2, 4, 2, 2)
+AXES = ("x", "ya", "yb", "yl", "w", "p", "c")
+SIZES = (4, 2, 2, 2, 4, 2, 2)
 NEAR = ("yl", "p", "c")
-FAR = ("x", "yh")
+FAR = ("x", "ya", "yb")
+SHARE = ("x", "yb")
 CODE = 16
 PAY = 4 * TOK + CODE
 NONE = 99
@@ -39,20 +40,20 @@
 
 def weight_moves():
     moves = []
-    for x, yh, yl, w, p, c in devices():
+    for x, ya, yb, yl, w, p, c in devices():
         head = 2 * key_head(yl, p, c) + x // 2
-        source = place(2 * (w // 2) + x % 2, yh, (w + head) % 2, head // 4, (head // 2) % 2, head % 2)
-        moves.append((source, place(x, yh, yl, w, p, c)))
+        source = place(2 * (w // 2) + x % 2, ya, yb, (w + head) % 2, head // 4, (head // 2) % 2, head % 2)
+        moves.append((source, place(x, ya, yb, yl, w, p, c)))
     return moves
 
 
 def piece_moves(turn):
     moves = []
-    for x, yh, yl, w, p, c in devices():
+    for x, ya, yb, yl, w, p, c in devices():
         piece = (w + turn) % 4
         head = 2 * key_head(yl, p, c) + piece % 2
-        owner = place(x, yh, piece // 2, head // 4, (head // 2) % 2, head % 2)
-        moves.append((place(x, yh, yl, w, p, c), owner))
+        owner = place(x, ya, yb, piece // 2, head // 4, (head // 2) % 2, head % 2)
+        moves.append((place(x, ya, yb, yl, w, p, c), owner))
     return moves
 
 
@@ -125,15 +126,16 @@
         lse_ref[lo:ext, :] = jnp.where(lane == 0, stats[0], stats[1])
 
 
-def weight_kernel(out_ref, cot_ref, wg_ref):
+def weight_kernel(out_ref, cot_ref, after_ref, wg_ref):
+    del after_ref
     total = dot(out_ref[...], cot_ref[...], ((1,), (0,)))
     left = lax.broadcasted_iota(jnp.int32, (64, HD), 1) < 64
     for b in range(2):
-        for yh in range(4):
-            upper = total[b * HD : b * HD + 64, yh * HD : (yh + 1) * HD]
-            lower = total[b * HD + 64 : (b + 1) * HD, yh * HD : (yh + 1) * HD]
-            wg_ref[yh, b] = jnp.where(left, upper, pltpu.roll(lower, 64, 1)).astype(BF16)
-            wg_ref[yh, 2 + b] = jnp.where(left, pltpu.roll(upper, 64, 1), lower).astype(BF16)
+        for m in range(8):
+            upper = total[b * HD : b * HD + 64, m * HD : (m + 1) * HD]
+            lower = total[b * HD + 64 : (b + 1) * HD, m * HD : (m + 1) * HD]
+            wg_ref[m, b] = jnp.where(left, upper, pltpu.roll(lower, 64, 1)).astype(BF16)
+            wg_ref[m, 2 + b] = jnp.where(left, pltpu.roll(upper, 64, 1), lower).astype(BF16)
 
 
 def backward_kernel(pay_ref, lse_ref, cot_ref, w_ref, ret_ref, ghbuf):
@@ -250,19 +252,20 @@
     )(arrived)
 
 
-def run_weight(out, cot):
+def run_weight(out, cot, after):
     return call(
         weight_kernel,
         shape((16, 4, 64, HD)),
         flops=1 << 30,
         bytes_accessed=6 << 20,
-        grid=(4,),
+        grid=(2,),
         in_specs=[
             whole(2 * HD, 2 * WINDOW),
-            pl.BlockSpec((2 * WINDOW, 512), lambda i: (0, i)),
-        ],
-        out_specs=pl.BlockSpec((4, 4, 64, HD), lambda i: (i, 0, 0, 0)),
-    )(out, cot)
+            pl.BlockSpec((2 * WINDOW, 1024), lambda i: (0, i)),
+            pl.BlockSpec(memory_space=pl.ANY),
+        ],
+        out_specs=pl.BlockSpec((8, 4, 64, HD), lambda i: (i, 0, 0, 0)),
+    )(out, cot, after)
 
 
 def run_backward(arrived, lse, cot, weight):
@@ -325,16 +328,16 @@
 def local(queries, keys, values, cotangent, out_weight, segment, row_type, pair_index):
     x = lax.axis_index("x").astype(jnp.int32)
     w = lax.axis_index("w").astype(jnp.int32).reshape(1)
-    share = lax.dynamic_slice_in_dim(out_weight, 64 * lax.rem(x, 2), 64, axis=0)
-    quarter = lax.ppermute(share, AXES, weight_moves())
+    first = 32 * (2 * lax.rem(x, 2) + lax.axis_index("yb").astype(jnp.int32))
+    eighth = lax.ppermute(lax.dynamic_slice_in_dim(out_weight, first, 32, axis=0), AXES, weight_moves())
     cot = lax.all_gather(cotangent[0], NEAR, axis=0, tiled=True)
     payload = run_pack(queries, keys, values, segment, row_type, pair_index)
     arrived = lax.all_to_all(payload, NEAR, 0, 0)
-    weight = lax.all_gather(quarter, "x", axis=0, tiled=True)
+    weight = lax.all_to_all(jnp.broadcast_to(eighth[None], (8, *eighth.shape)), SHARE, 0, 0)
     out, lse = run_forward(arrived)
-    pieces = run_weight(out, cot)
+    pieces = run_weight(out, cot, weight)
     got = lax.all_to_all(pieces, FAR, 0, 0)
-    back = run_backward(arrived, lse, cot, weight)
+    back = run_backward(arrived, lse, cot, weight.reshape(-1, weight.shape[2]))
     home = lax.all_to_all(back, NEAR, 0, 0)
     sent = [lax.ppermute(part, AXES, piece_moves(turn)) for turn, part in enumerate(run_sum(w, got))]
     weight_grad = run_spread(sent).T
@@ -344,7 +347,7 @@
 
 def solution(mesh):
     fine = Mesh(mesh.devices.reshape(SIZES), AXES)
-    dp, seq = AXES[:3], AXES[3:]
+    dp, seq = AXES[:4], AXES[4:]
     in_specs = (
         P(dp, seq, None),
         P(dp, seq, None),

time: 152 us -> 157 us (1.033)
  starting transfers between devices: 49.6 us -> 52.4 us
  waiting for transfers between devices: 59.4 us -> 61.6 us
    all_gather x1 -> x0, waiting for transfers between devices: 25.4 us -> none  [local(): weight = lax.all_gather(quarter, 'x', axis=0, tiled=True)]
    all_to_all x0 -> x1, waiting for transfers between devices: none -> 20.3 us  [local(): lax.all_to_all(jnp.broadcast_to(eighth[None], (8, *eighth.shape)), SHARE,...]
    all_to_all x1, waiting for transfers between devices: 0.01 us -> 19.1 us  [local(): got = lax.all_to_all(pieces, FAR, 0, 0)]
    all_to_all x0 -> x1, starting transfers between devices: none -> 8.11 us  [local(): lax.all_to_all(jnp.broadcast_to(eighth[None], (8, *eighth.shape)), SHARE,...]
    ppermute x1, waiting for transfers between devices: 23.6 us -> 16.2 us  [local(): lax.ppermute(lax.dynamic_slice_in_dim(out_weight, first, 32, axis=0), AXE...]
    all_gather x1, waiting for transfers between devices: 6.11 us -> 0.01 us  [local(): cot = lax.all_gather(cotangent[0], NEAR, axis=0, tiled=True)]
    all_to_all x1, starting transfers between devices: 7.05 us -> 3.51 us  [local(): home = lax.all_to_all(back, NEAR, 0, 0)]
    all_to_all x1, starting transfers between devices: 6.36 us -> 3.65 us  [local(): got = lax.all_to_all(pieces, FAR, 0, 0)]
  transfers between devices with their start and end apart: 10 -> 10, of which waited for: 4 -> 4; matrix products, arithmetic and copies ran while one was open for 0% -> 1% of each run, Pallas kernels for 17% -> 13%
where the time goes in v6:
time: 157 us
  waiting for transfers between devices  61.6 us (39%)
  starting transfers between devices  52.4 us (33%)
  Pallas kernels  26 us (17%)
  between operations  14.1 us (9%)
  local copies, waits for them, and re-layouts  2.34 us (1%)
    ppermute x4, starting transfers between devices, local(): lax.ppermute(part, AXES, piece_moves(turn))  22.8 us
    all_to_all x1, waiting for transfers between devices, local(): lax.all_to_all(jnp.broadcast_to(eighth[None], (8, *eighth.shape)), SHARE,...  20.3 us
    all_to_all x1, waiting for transfers between devices, local(): got = lax.all_to_all(pieces, FAR, 0, 0)  19.1 us
    ppermute x1, waiting for transfers between devices, local(): lax.ppermute(lax.dynamic_slice_in_dim(out_weight, first, 32, axis=0), AXE...  16.2 us
    pallas_call x1, Pallas kernels, run_backward(): call(backward_kernel, shape((8, 4 * TOK, HD)), flops=8 << 30, bytes_acces...  10.4 us
    all_to_all x1, starting transfers between devices, local(): arrived = lax.all_to_all(payload, NEAR, 0, 0)  10.3 us
    all_to_all x1, starting transfers between devices, local(): lax.all_to_all(jnp.broadcast_to(eighth[None], (8, *eighth.shape)), SHARE,...  8.11 us
    ppermute x4, waiting for transfers between devices, local(): lax.ppermute(part, AXES, piece_moves(turn))  5.32 us
  transfers between devices with their start and end apart: 10, of which 4 were waited for; matrix products, arithmetic and copies ran while one was open for 1% of the time, Pallas kernels for 13%

profile of v6, /device:TPU:1, one launch (start us, length us, event | category | flops | bytes accessed | tf_op | source)
XLA Modules:
  0.0 156.6 jit_solution(3545831529173346298)
XLA Ops:
  7.2 0.0 copy-start
  7.2 0.0 all-gather.3.cloned.1.call-start
  7.2 0.7 all-gather.3.cloned.1.call-update
  7.9 3.5 %shard_map.111 = bf16[2,4,528,128]{3,2,1,0:T(8,128)(2,1)} custom-call(bf16[1,128,2048]{2,1,0:T(8,128)(2,1)} %q_ref.1, bf16[1,128,1024]{2,1,0:T(8,128)(2,1)} %k_ref.1, bf16[1,128,1024]{2,1,0:T(8,128)(2,1)} %v_ref.1, s32[1,128]{1,0:T(1,128)} %seg_ref.1, s32[1,128]{1,0:T(1,128)} %type_ref.1, s32[1,24]{1,0:T(1,128)} %pair_ref.1), custom_call_target="tpu_custom_call" | custom-call | bytes 2097152 | tf_op jit(solution)/shard_map/pallas_call | solution.py:223
  11.4 10.3 %all-to-all-start = ((bf16[8,528,128]{2,1,0:T(8,128)(2,1)}), bf16[8,528,128]{2,1,0:T(8,128)(2,1)S(1)}, u32[]{:S(2)}, u32[]{:S(2)}) async-start(bf16[8,528,128]{2,1,0:T(8,128)(2,1)} %bitcast.7), calls=%async_computation | async-start | bytes 2162688 | tf_op jit(solution)/shard_map/all_to_all | solution.py:335
  21.8 0.0 copy-done
  21.8 4.0 %collective-permute-start = (bf16[32,2048]{1,0:T(8,128)(2,1)S(1)}, bf16[32,2048]{1,0:T(8,128)(2,1)S(1)}, u32[]{:S(2)}, u32[]{:S(2)}) collective-permute-start(bf16[32,2048]{1,0:T(8,128)(2,1)S(1)} %constant_dynamic-slice_fusion), channel_id=1, source_target_pairs={{0,0},{8,1},{4,2},{12,3},{16,4},{24,5},{20,6},{28,7},{256,8},{264,... | collective-permute-start | bytes 393224 | tf_op jit(solution)/shard_map/ppermute | solution.py:332
  25.8 16.2 %collective-permute-done = bf16[32,2048]{1,0:T(8,128)(2,1)S(1)} collective-permute-done((bf16[32,2048]{1,0:T(8,128)(2,1)S(1)}, bf16[32,2048]{1,0:T(8,128)(2,1)S(1)}, u32[]{:S(2)}, u32[]{:S(2)}) %collective-permute-start) | collective-permute-done | bytes 131104 | tf_op jit(solution)/shard_map/ppermute | solution.py:332
  42.0 0.0 all-to-all-done.pay_ref
  42.0 0.0 copy-start.2
  42.0 1.2 broadcast_in_dim.2
  43.2 0.1 copy-done.2
  43.3 8.1 %all-to-all-start.1 = ((bf16[8,32,2048]{2,1,0:T(8,128)(2,1)}), bf16[8,32,2048]{2,1,0:T(8,128)(2,1)S(1)}, u32[]{:S(2)}, u32[]{:S(2)}) async-start(bf16[8,32,2048]{2,1,0:T(8,128)(2,1)} %broadcast_in_dim.2), calls=%async_computation.1 | async-start | bytes 2097152 | tf_op jit(solution)/shard_map/all_to_all | solution.py:336
  51.4 5.2 %shard_map.112 = (bf16[256,1024]{1,0:T(8,128)(2,1)}, f32[1024,128]{1,0:T(8,128)}) custom-call(bf16[8,528,128]{2,1,0:T(8,128)(2,1)} %copy-done.2), custom_call_target="tpu_custom_call" | custom-call | flops 4294967296 | bytes 2097152 | tf_op jit(solution)/shard_map/pallas_call | solution.py:241
  56.7 20.3 %all-to-all-done.1.after_ref = bf16[8,32,2048]{2,1,0:T(8,128)(2,1)S(1)} async-done(((bf16[8,32,2048]{2,1,0:T(8,128)(2,1)}), bf16[8,32,2048]{2,1,0:T(8,128)(2,1)S(1)}, u32[]{:S(2)}, u32[]{:S(2)}) %all-to-all-start.1) | async-done | bytes 1048608 | tf_op jit(solution)/shard_map/all_to_all | solution.py:336
  77.0 0.0 copy-start.1
  77.0 0.0 all-gather.3.cloned.1.call-done
  77.0 1.0 copy-done.1
  78.0 4.1 %shard_map.115 = bf16[16,4,64,128]{3,2,1,0:T(8,128)(2,1)} custom-call(bf16[256,1024]{1,0:T(8,128)(2,1)} %get-tuple-element.17.out_ref, bf16[1024,2048]{1,0:T(8,128)(2,1)} %bitcast.8, bf16[8,32,2048]{2,1,0:T(8,128)(2,1)} %copy-done.1), custom_call_target="tpu_custom_call" | custom-call | flops 1073741824 | bytes 6291456 | tf_op jit(solution)/shard_map/pallas_call | solution.py:256
  82.1 3.7 %all-to-all-start.3 = ((bf16[16,4,64,128]{3,2,1,0:T(8,128)(2,1)}), bf16[16,4,64,128]{3,2,1,0:T(8,128)(2,1)S(1)}, u32[]{:S(2)}, u32[]{:S(2)}) async-start(bf16[16,4,64,128]{3,2,1,0:T(8,128)(2,1)} %shard_map.115), calls=%async_computation.3 | async-start | bytes 2097152 | tf_op jit(solution)/shard_map/all_to_all | solution.py:339
  85.7 10.4 %shard_map.113 = bf16[8,512,128]{2,1,0:T(8,128)(2,1)} custom-call(bf16[8,528,128]{2,1,0:T(8,128)(2,1)} %copy-done.2, f32[1024,128]{1,0:T(8,128)} %get-tuple-element.13.lse_ref, bf16[1024,2048]{1,0:T(8,128)(2,1)} %bitcast.9, bf16[256,2048]{1,0:T(8,128)(2,1)} %bitcast.10), custom_call_target="tpu_custom_call" | custom-call | flops 8589934592 | bytes 7340032 | tf_op jit(solution)/shard_map/pallas_call | solution.py:273
  96.2 19.1 %all-to-all-done.3.got_ref = bf16[16,4,64,128]{3,2,1,0:T(8,128)(2,1)S(1)} async-done(((bf16[16,4,64,128]{3,2,1,0:T(8,128)(2,1)}), bf16[16,4,64,128]{3,2,1,0:T(8,128)(2,1)S(1)}, u32[]{:S(2)}, u32[]{:S(2)}) %all-to-all-start.3) | async-done | bytes 1048608 | tf_op jit(solution)/shard_map/all_to_all | solution.py:339
  115.3 3.5 %all-to-all-start.2 = ((bf16[8,512,128]{2,1,0:T(8,128)(2,1)}), bf16[8,512,128]{2,1,0:T(8,128)(2,1)S(1)}, u32[]{:S(2)}, u32[]{:S(2)}) async-start(bf16[8,512,128]{2,1,0:T(8,128)(2,1)} %shard_map.113), calls=%async_computation.2 | async-start | bytes 2097152 | tf_op jit(solution)/shard_map/all_to_all | solution.py:341
  118.8 0.2 shard_map.116
  119.0 6.9 %collective-permute-start.1 = (bf16[64,128]{1,0:T(8,128)(2,1)S(1)}, bf16[64,128]{1,0:T(8,128)(2,1)S(1)}, u32[]{:S(2)}, u32[]{:S(2)}) collective-permute-start(bf16[64,128]{1,0:T(8,128)(2,1)S(1)} %get-tuple-element.18), channel_id=1, source_target_pairs={{0,0},{1,8},{2,4},{3,12},{4,1},{5,9},{6,5},{7,13},{8,16},{9,24},{1... | collective-permute-start | bytes 49160 | tf_op jit(solution)/shard_map/ppermute | solution.py:342
  125.9 3.7 %collective-permute-start.2 = (bf16[64,128]{1,0:T(8,128)(2,1)S(1)}, bf16[64,128]{1,0:T(8,128)(2,1)S(1)}, u32[]{:S(2)}, u32[]{:S(2)}) collective-permute-start(bf16[64,128]{1,0:T(8,128)(2,1)S(1)} %get-tuple-element.19), channel_id=1, source_target_pairs={{0,1},{1,9},{2,5},{3,13},{4,16},{5,24},{6,20},{7,28},{8,17},{9,25}... | collective-permute-start | bytes 49160 | tf_op jit(solution)/shard_map/ppermute | solution.py:342
  129.6 10.3 %collective-permute-start.3 = (bf16[64,128]{1,0:T(8,128)(2,1)S(1)}, bf16[64,128]{1,0:T(8,128)(2,1)S(1)}, u32[]{:S(2)}, u32[]{:S(2)}) collective-permute-start(bf16[64,128]{1,0:T(8,128)(2,1)S(1)} %get-tuple-element.20), channel_id=1, source_target_pairs={{0,16},{1,24},{2,20},{3,28},{4,17},{5,25},{6,21},{7,29},{8,0},{9,8... | collective-permute-start | bytes 49160 | tf_op jit(solution)/shard_map/ppermute | solution.py:342
  139.9 1.9 %collective-permute-start.4 = (bf16[64,128]{1,0:T(8,128)(2,1)S(1)}, bf16[64,128]{1,0:T(8,128)(2,1)S(1)}, u32[]{:S(2)}, u32[]{:S(2)}) collective-permute-start(bf16[64,128]{1,0:T(8,128)(2,1)S(1)} %get-tuple-element.21), channel_id=1, source_target_pairs={{0,17},{1,25},{2,21},{3,29},{4,0},{5,8},{6,4},{7,12},{8,1},{9,9},{... | collective-permute-start | bytes 49160 | tf_op jit(solution)/shard_map/ppermute | solution.py:342
  141.9 0.0 all-to-all-done.2
  141.9 1.7 %shard_map.114 = (bf16[1,128,2048]{2,1,0:T(8,128)(2,1)}, bf16[1,128,1024]{2,1,0:T(8,128)(2,1)}, bf16[1,128,1024]{2,1,0:T(8,128)(2,1)}) custom-call(bf16[2,4,512,128]{3,2,1,0:T(8,128)(2,1)S(1)} %bitcast.6), custom_call_target="tpu_custom_call" | custom-call | bytes 2097152 | tf_op jit(solution)/shard_map/pallas_call | solution.py:313
  143.6 0.0 collective-permute-done.1.a_ref
  143.6 0.0 collective-permute-done.2.b_ref
  143.6 0.0 collective-permute-done.3.c_ref
  143.6 5.3 %collective-permute-done.4.d_ref = bf16[64,128]{1,0:T(8,128)(2,1)S(1)} collective-permute-done((bf16[64,128]{1,0:T(8,128)(2,1)S(1)}, bf16[64,128]{1,0:T(8,128)(2,1)S(1)}, u32[]{:S(2)}, u32[]{:S(2)}) %collective-permute-start.4) | collective-permute-done | bytes 16416 | tf_op jit(solution)/shard_map/ppermute | solution.py:342
  148.9 0.8 shard_map.117
  (1 shorter events, 0.0 us)
Async XLA Ops:
  7.2 14.6 %copy-start = (bf16[128,2048]{1,0:T(8,128)(2,1)S(1)}, bf16[128,2048]{1,0:T(8,128)(2,1)}, u32[]{:S(2)}) copy-start(bf16[128,2048]{1,0:T(8,128)(2,1)} %param.12) | copy-start | bytes 1572868
  7.2 69.8 %all-gather.3.cloned.1.call-start = ((), (), s32[]{:S(2)}) async-start(), calls=%async_computation.4 | async-start | bytes 4718592 | tf_op jit(solution)/shard_map/all_gather | solution.py:333
  11.4 30.6 %all-to-all-start = ((bf16[8,528,128]{2,1,0:T(8,128)(2,1)}), bf16[8,528,128]{2,1,0:T(8,128)(2,1)S(1)}, u32[]{:S(2)}, u32[]{:S(2)}) async-start(bf16[8,528,128]{2,1,0:T(8,128)(2,1)} %bitcast.7), calls=%async_computation | async-start | bytes 2162688 | tf_op jit(solution)/shard_map/all_to_all | solution.py:335
  21.8 20.2 %collective-permute-start = (bf16[32,2048]{1,0:T(8,128)(2,1)S(1)}, bf16[32,2048]{1,0:T(8,128)(2,1)S(1)}, u32[]{:S(2)}, u32[]{:S(2)}) collective-permute-start(bf16[32,2048]{1,0:T(8,128)(2,1)S(1)} %constant_dynamic-slice_fusion), channel_id=1, source_target_pairs={{0,0},{8,1},{4,2},{12,3},{16,4},{24,5},{20,6},{28,7},{256,8},{264,... | collective-permute-start | bytes 393224 | tf_op jit(solution)/shard_map/ppermute | solution.py:332
  42.0 1.3 copy-start.2
  43.3 33.7 %all-to-all-start.1 = ((bf16[8,32,2048]{2,1,0:T(8,128)(2,1)}), bf16[8,32,2048]{2,1,0:T(8,128)(2,1)S(1)}, u32[]{:S(2)}, u32[]{:S(2)}) async-start(bf16[8,32,2048]{2,1,0:T(8,128)(2,1)} %broadcast_in_dim.2), calls=%async_computation.1 | async-start | bytes 2097152 | tf_op jit(solution)/shard_map/all_to_all | solution.py:336
  77.0 1.0 copy-start.1
  82.1 33.2 %all-to-all-start.3 = ((bf16[16,4,64,128]{3,2,1,0:T(8,128)(2,1)}), bf16[16,4,64,128]{3,2,1,0:T(8,128)(2,1)S(1)}, u32[]{:S(2)}, u32[]{:S(2)}) async-start(bf16[16,4,64,128]{3,2,1,0:T(8,128)(2,1)} %shard_map.115), calls=%async_computation.3 | async-start | bytes 2097152 | tf_op jit(solution)/shard_map/all_to_all | solution.py:339
  115.3 26.6 %all-to-all-start.2 = ((bf16[8,512,128]{2,1,0:T(8,128)(2,1)}), bf16[8,512,128]{2,1,0:T(8,128)(2,1)S(1)}, u32[]{:S(2)}, u32[]{:S(2)}) async-start(bf16[8,512,128]{2,1,0:T(8,128)(2,1)} %shard_map.113), calls=%async_computation.2 | async-start | bytes 2097152 | tf_op jit(solution)/shard_map/all_to_all | solution.py:341
  119.0 24.5 %collective-permute-start.1 = (bf16[64,128]{1,0:T(8,128)(2,1)S(1)}, bf16[64,128]{1,0:T(8,128)(2,1)S(1)}, u32[]{:S(2)}, u32[]{:S(2)}) collective-permute-start(bf16[64,128]{1,0:T(8,128)(2,1)S(1)} %get-tuple-element.18), channel_id=1, source_target_pairs={{0,0},{1,8},{2,4},{3,12},{4,1},{5,9},{6,5},{7,13},{8,16},{9,24},{1... | collective-permute-start | bytes 49160 | tf_op jit(solution)/shard_map/ppermute | solution.py:342
  125.9 17.7 %collective-permute-start.2 = (bf16[64,128]{1,0:T(8,128)(2,1)S(1)}, bf16[64,128]{1,0:T(8,128)(2,1)S(1)}, u32[]{:S(2)}, u32[]{:S(2)}) collective-permute-start(bf16[64,128]{1,0:T(8,128)(2,1)S(1)} %get-tuple-element.19), channel_id=1, source_target_pairs={{0,1},{1,9},{2,5},{3,13},{4,16},{5,24},{6,20},{7,28},{8,17},{9,25}... | collective-permute-start | bytes 49160 | tf_op jit(solution)/shard_map/ppermute | solution.py:342
  129.6 14.0 %collective-permute-start.3 = (bf16[64,128]{1,0:T(8,128)(2,1)S(1)}, bf16[64,128]{1,0:T(8,128)(2,1)S(1)}, u32[]{:S(2)}, u32[]{:S(2)}) collective-permute-start(bf16[64,128]{1,0:T(8,128)(2,1)S(1)} %get-tuple-element.20), channel_id=1, source_target_pairs={{0,16},{1,24},{2,20},{3,28},{4,17},{5,25},{6,21},{7,29},{8,0},{9,8... | collective-permute-start | bytes 49160 | tf_op jit(solution)/shard_map/ppermute | solution.py:342
  139.9 9.0 %collective-permute-start.4 = (bf16[64,128]{1,0:T(8,128)(2,1)S(1)}, bf16[64,128]{1,0:T(8,128)(2,1)S(1)}, u32[]{:S(2)}, u32[]{:S(2)}) collective-permute-start(bf16[64,128]{1,0:T(8,128)(2,1)S(1)} %get-tuple-element.21), channel_id=1, source_target_pairs={{0,17},{1,25},{2,21},{3,29},{4,0},{5,8},{6,4},{7,12},{8,1},{9,9},{... | collective-permute-start | bytes 49160 | tf_op jit(solution)/shard_map/ppermute | solution.py:342
Sparse Core Ops, SparseCore 0:
  10.2 48.7 all-gather.2

commit v7 on v5

--- a/solution.py
+++ b/solution.py
@@ -125,19 +125,29 @@
         lse_ref[lo:ext, :] = jnp.where(lane == 0, stats[0], stats[1])
 
 
-def weight_kernel(out_ref, cot_ref, wg_ref):
+def weight_kernel(out_ref, cot_ref, w_ref, wg_ref, share_ref):
+    @pl.when(pl.program_id(0) == 0)
+    def _():
+        share_ref[...] = w_ref[...]
+
     total = dot(out_ref[...], cot_ref[...], ((1,), (0,)))
     left = lax.broadcasted_iota(jnp.int32, (64, HD), 1) < 64
     for b in range(2):
-        for yh in range(4):
-            upper = total[b * HD : b * HD + 64, yh * HD : (yh + 1) * HD]
-            lower = total[b * HD + 64 : (b + 1) * HD, yh * HD : (yh + 1) * HD]
-            wg_ref[yh, b] = jnp.where(left, upper, pltpu.roll(lower, 64, 1)).astype(BF16)
-            wg_ref[yh, 2 + b] = jnp.where(left, pltpu.roll(upper, 64, 1), lower).astype(BF16)
-
-
-def backward_kernel(pay_ref, lse_ref, cot_ref, w_ref, ret_ref, ghbuf):
-    ghbuf[...] = dot(cot_ref[...], w_ref[...], ((1,), (1,))).astype(BF16)
+        for m in range(8):
+            upper = total[b * HD : b * HD + 64, m * HD : (m + 1) * HD]
+            lower = total[b * HD + 64 : (b + 1) * HD, m * HD : (m + 1) * HD]
+            wg_ref[m, b] = jnp.where(left, upper, pltpu.roll(lower, 64, 1)).astype(BF16)
+            wg_ref[m, 2 + b] = jnp.where(left, pltpu.roll(upper, 64, 1), lower).astype(BF16)
+
+
+def backward_kernel(x_ref, pay_ref, lse_ref, cot_ref, w0_ref, w1_ref, w2_ref, w3_ref, ret_ref, wbuf, ghbuf):
+    @pl.when(pl.program_id(0) == 0)
+    def _():
+        for turn, quarter in enumerate((w0_ref, w1_ref, w2_ref, w3_ref)):
+            first = pl.multiple_of(lax.rem(x_ref[0] + 4 - turn, 4) * 64, 64)
+            wbuf[pl.ds(first, 64), :] = quarter[...]
+
+    ghbuf[...] = dot(cot_ref[...], wbuf[...], ((1,), (1,))).astype(BF16)
     key = rows(pay_ref, 2 * TOK)
     value = rows(pay_ref, 3 * TOK)
     want, have = hot(pay_ref)
@@ -250,22 +260,23 @@
     )(arrived)
 
 
-def run_weight(out, cot):
+def run_weight(out, cot, quarter):
     return call(
         weight_kernel,
-        shape((16, 4, 64, HD)),
+        (shape((16, 4, 64, HD)), shape(quarter.shape)),
         flops=1 << 30,
         bytes_accessed=6 << 20,
-        grid=(4,),
+        grid=(2,),
         in_specs=[
             whole(2 * HD, 2 * WINDOW),
-            pl.BlockSpec((2 * WINDOW, 512), lambda i: (0, i)),
+            pl.BlockSpec((2 * WINDOW, 1024), lambda i: (0, i)),
+            whole(*quarter.shape),
         ],
-        out_specs=pl.BlockSpec((4, 4, 64, HD), lambda i: (i, 0, 0, 0)),
-    )(out, cot)
-
-
-def run_backward(arrived, lse, cot, weight):
+        out_specs=[pl.BlockSpec((8, 4, 64, HD), lambda i: (i, 0, 0, 0)), whole(*quarter.shape)],
+    )(out, cot, quarter)
+
+
+def run_backward(x, arrived, lse, cot, quarters):
     width = cot.shape[1]
     return call(
         backward_kernel,
@@ -274,14 +285,15 @@
         bytes_accessed=7 << 20,
         grid=(2,),
         in_specs=[
+            SMEM,
             pl.BlockSpec((4, PAY, HD), lambda u: (u, 0, 0)),
             pl.BlockSpec((WINDOW, HD), lambda u: (u, 0)),
             pl.BlockSpec((WINDOW, width), lambda u: (u, 0)),
-            whole(2 * HD, width),
-        ],
+        ]
+        + [whole(64, width)] * 4,
         out_specs=pl.BlockSpec((4, 4 * TOK, HD), lambda u: (u, 0, 0)),
-        scratch_shapes=[pltpu.VMEM((WINDOW, 2 * HD), BF16)],
-    )(arrived, lse, cot, weight)
+        scratch_shapes=[pltpu.VMEM((2 * HD, width), BF16), pltpu.VMEM((WINDOW, 2 * HD), BF16)],
+    )(x, arrived, lse, cot, *quarters)
 
 
 def run_sum(w, got):
@@ -330,11 +342,13 @@
     cot = lax.all_gather(cotangent[0], NEAR, axis=0, tiled=True)
     payload = run_pack(queries, keys, values, segment, row_type, pair_index)
     arrived = lax.all_to_all(payload, NEAR, 0, 0)
-    weight = lax.all_gather(quarter, "x", axis=0, tiled=True)
     out, lse = run_forward(arrived)
-    pieces = run_weight(out, cot)
+    pieces, share = run_weight(out, cot, quarter)
     got = lax.all_to_all(pieces, FAR, 0, 0)
-    back = run_backward(arrived, lse, cot, weight)
+    quarters = [share] + [
+        lax.ppermute(share, "x", [(i, (i + turn) % 4) for i in range(4)]) for turn in (1, 2, 3)
+    ]
+    back = run_backward(x.reshape(1), arrived, lse, cot, quarters)
     home = lax.all_to_all(back, NEAR, 0, 0)
     sent = [lax.ppermute(part, AXES, piece_moves(turn)) for turn, part in enumerate(run_sum(w, got))]
     weight_grad = run_spread(sent).T

time: 152 us -> 159 us (1.046)
  starting transfers between devices: 49.6 us -> 61.1 us
  waiting for transfers between devices: 59.4 us -> 55.5 us
    all_gather x1 -> x0, waiting for transfers between devices: 25.4 us -> none  [local(): weight = lax.all_gather(quarter, 'x', axis=0, tiled=True)]
    ppermute x1, waiting for transfers between devices: 23.6 us -> 6.21 us  [local(): quarter = lax.ppermute(share, AXES, weight_moves())]
    ppermute x0 -> x3, waiting for transfers between devices: none -> 17.3 us  [local(): lax.ppermute(share, 'x', [(i, (i + turn) % 4) for i in range(4)])]
    all_to_all x1, waiting for transfers between devices: 0.01 us -> 11.1 us  [local(): arrived = lax.all_to_all(payload, NEAR, 0, 0)]
    ppermute x0 -> x3, starting transfers between devices: none -> 9.45 us  [local(): lax.ppermute(share, 'x', [(i, (i + turn) % 4) for i in range(4)])]
    all_gather x1, waiting for transfers between devices: 6.11 us -> 13.1 us  [local(): cot = lax.all_gather(cotangent[0], NEAR, axis=0, tiled=True)]
    ppermute x4, waiting for transfers between devices: 3.66 us -> 7.01 us  [local(): lax.ppermute(part, AXES, piece_moves(turn))]
  transfers between devices with their start and end apart: 10 -> 12, of which waited for: 4 -> 7; matrix products, arithmetic and copies ran while one was open for 0% -> 0% of each run, Pallas kernels for 17% -> 13%
where the time goes in v7:
time: 159 us
  starting transfers between devices  61.1 us (38%)
  waiting for transfers between devices  55.5 us (35%)
  Pallas kernels  26.2 us (16%)
  between operations  14.2 us (9%)
  local copies, waits for them, and re-layouts  1.76 us (1%)
    ppermute x4, starting transfers between devices, local(): lax.ppermute(part, AXES, piece_moves(turn))  23.1 us
    ppermute x3, waiting for transfers between devices, local(): lax.ppermute(share, 'x', [(i, (i + turn) % 4) for i in range(4)])  17.3 us
    all_gather x1, waiting for transfers between devices, local(): cot = lax.all_gather(cotangent[0], NEAR, axis=0, tiled=True)  13.1 us
    all_to_all x1, waiting for transfers between devices, local(): arrived = lax.all_to_all(payload, NEAR, 0, 0)  11.1 us
    pallas_call x1, Pallas kernels, run_backward(): call(backward_kernel, shape((8, 4 * TOK, HD)), flops=8 << 30, bytes_acces...  10.5 us
    all_to_all x1, starting transfers between devices, local(): arrived = lax.all_to_all(payload, NEAR, 0, 0)  10.3 us
    ppermute x3, starting transfers between devices, local(): lax.ppermute(share, 'x', [(i, (i + turn) % 4) for i in range(4)])  9.45 us
    all_to_all x1, starting transfers between devices, local(): home = lax.all_to_all(back, NEAR, 0, 0)  7.68 us
  transfers between devices with their start and end apart: 12, of which 7 were waited for; matrix products, arithmetic and copies ran while one was open for 0% of the time, Pallas kernels for 13%

profile of v7, /device:TPU:1, one launch (start us, length us, event | category | flops | bytes accessed | tf_op | source)
XLA Modules:
  0.0 158.7 jit_solution(3478012987227656904)
XLA Ops:
  7.2 0.0 copy-start
  7.2 0.0 all-gather.3.cloned.1.call-start
  7.2 0.7 all-gather.3.cloned.1.call-update
  7.9 3.5 %shard_map.111 = bf16[2,4,528,128]{3,2,1,0:T(8,128)(2,1)} custom-call(bf16[1,128,2048]{2,1,0:T(8,128)(2,1)} %q_ref.1, bf16[1,128,1024]{2,1,0:T(8,128)(2,1)} %k_ref.1, bf16[1,128,1024]{2,1,0:T(8,128)(2,1)} %v_ref.1, s32[1,128]{1,0:T(1,128)} %seg_ref.1, s32[1,128]{1,0:T(1,128)} %type_ref.1, s32[1,24]{1,0:T(1,128)} %pair_ref.1), custom_call_target="tpu_custom_call" | custom-call | bytes 2097152 | tf_op jit(solution)/shard_map/pallas_call | solution.py:231
  11.4 10.3 %all-to-all-start = ((bf16[8,528,128]{2,1,0:T(8,128)(2,1)}), bf16[8,528,128]{2,1,0:T(8,128)(2,1)S(1)}, u32[]{:S(2)}, u32[]{:S(2)}) async-start(bf16[8,528,128]{2,1,0:T(8,128)(2,1)} %bitcast.7), calls=%async_computation | async-start | bytes 2162688 | tf_op jit(solution)/shard_map/all_to_all | solution.py:344
  21.8 0.0 copy-done
  21.8 4.0 %collective-permute-start = (bf16[64,2048]{1,0:T(8,128)(2,1)S(1)}, bf16[64,2048]{1,0:T(8,128)(2,1)S(1)}, u32[]{:S(2)}, u32[]{:S(2)}) collective-permute-start(bf16[64,2048]{1,0:T(8,128)(2,1)S(1)} %constant_dynamic-slice_fusion), channel_id=1, source_target_pairs={{0,0},{8,1},{4,2},{12,3},{16,4},{24,5},{20,6},{28,7},{256,8},{264,... | collective-permute-start | bytes 786440 | tf_op jit(solution)/shard_map/ppermute | solution.py:341
  25.8 11.1 %all-to-all-done.pay_ref = bf16[8,528,128]{2,1,0:T(8,128)(2,1)S(1)} async-done(((bf16[8,528,128]{2,1,0:T(8,128)(2,1)}), bf16[8,528,128]{2,1,0:T(8,128)(2,1)S(1)}, u32[]{:S(2)}, u32[]{:S(2)}) %all-to-all-start) | async-done | bytes 1081376 | tf_op jit(solution)/shard_map/all_to_all | solution.py:344
  36.9 0.0 copy-start.1
  36.9 1.0 copy-done.1
  38.0 5.3 %shard_map.112 = (bf16[256,1024]{1,0:T(8,128)(2,1)}, f32[1024,128]{1,0:T(8,128)}) custom-call(bf16[8,528,128]{2,1,0:T(8,128)(2,1)} %copy-done.1), custom_call_target="tpu_custom_call" | custom-call | flops 4294967296 | bytes 2097152 | tf_op jit(solution)/shard_map/pallas_call | solution.py:249
  43.2 6.2 %collective-permute-done.w_ref = bf16[64,2048]{1,0:T(8,128)(2,1)S(1)} collective-permute-done((bf16[64,2048]{1,0:T(8,128)(2,1)S(1)}, bf16[64,2048]{1,0:T(8,128)(2,1)S(1)}, u32[]{:S(2)}, u32[]{:S(2)}) %collective-permute-start) | collective-permute-done | bytes 262176 | tf_op jit(solution)/shard_map/ppermute | solution.py:341
  49.4 0.0 copy-start.2
  49.4 13.1 %all-gather.3.cloned.1.call-done = bf16[1,1024,2048]{2,1,0:T(8,128)(2,1)} async-done(((bf16[1,128,2048]{2,1,0:T(8,128)(2,1)}), bf16[1,1024,2048]{2,1,0:T(8,128)(2,1)}) %all-gather.3.cloned.1.call-update) | async-done | bytes 4194320 | tf_op jit(solution)/shard_map/all_gather | solution.py:342
  62.5 0.0 copy-done.2
  62.5 4.2 %shard_map.113 = (bf16[16,4,64,128]{3,2,1,0:T(8,128)(2,1)}, bf16[64,2048]{1,0:T(8,128)(2,1)}) custom-call(bf16[256,1024]{1,0:T(8,128)(2,1)} %get-tuple-element.16.out_ref, bf16[1024,2048]{1,0:T(8,128)(2,1)} %bitcast.8, bf16[64,2048]{1,0:T(8,128)(2,1)} %copy-done.2), custom_call_target="tpu_custom_call" | custom-call | flops 1073741824 | bytes 6291456 | tf_op jit(solution)/shard_map/pallas_call | solution.py:264
  66.7 0.0 copy-start.3
  66.7 6.5 %all-to-all-start.2 = ((bf16[16,4,64,128]{3,2,1,0:T(8,128)(2,1)}), bf16[16,4,64,128]{3,2,1,0:T(8,128)(2,1)S(1)}, u32[]{:S(2)}, u32[]{:S(2)}) async-start(bf16[16,4,64,128]{3,2,1,0:T(8,128)(2,1)} %get-tuple-element.21), calls=%async_computation.2 | async-start | bytes 2097152 | tf_op jit(solution)/shard_map/all_to_all | solution.py:347
  73.2 0.0 copy-done.3
  73.2 4.5 %collective-permute-start.3 = (bf16[64,2048]{1,0:T(8,128)(2,1)S(1)}, bf16[64,2048]{1,0:T(8,128)(2,1)S(1)}, u32[]{:S(2)}, u32[]{:S(2)}) collective-permute-start(bf16[64,2048]{1,0:T(8,128)(2,1)S(1)} %copy-done.3), channel_id=1, source_target_pairs={{0,384},{128,0},{256,128},{384,256},{1,385},{129,1},{257,129},{385... | collective-permute-start | bytes 786440 | tf_op jit(solution)/shard_map/ppermute | solution.py:349
  77.7 2.5 %collective-permute-start.2 = (bf16[64,2048]{1,0:T(8,128)(2,1)S(1)}, bf16[64,2048]{1,0:T(8,128)(2,1)S(1)}, u32[]{:S(2)}, u32[]{:S(2)}) collective-permute-start(bf16[64,2048]{1,0:T(8,128)(2,1)S(1)} %copy-done.3), channel_id=1, source_target_pairs={{0,256},{128,384},{256,0},{384,128},{1,257},{129,385},{257,1},{385... | collective-permute-start | bytes 786440 | tf_op jit(solution)/shard_map/ppermute | solution.py:349
  80.2 2.5 %collective-permute-start.1 = (bf16[64,2048]{1,0:T(8,128)(2,1)S(1)}, bf16[64,2048]{1,0:T(8,128)(2,1)S(1)}, u32[]{:S(2)}, u32[]{:S(2)}) collective-permute-start(bf16[64,2048]{1,0:T(8,128)(2,1)S(1)} %copy-done.3), channel_id=1, source_target_pairs={{0,128},{128,256},{256,384},{384,0},{1,129},{129,257},{257,385},{3... | collective-permute-start | bytes 786440 | tf_op jit(solution)/shard_map/ppermute | solution.py:349
  82.7 7.4 %collective-permute-done.3.w3_ref = bf16[64,2048]{1,0:T(8,128)(2,1)S(1)} collective-permute-done((bf16[64,2048]{1,0:T(8,128)(2,1)S(1)}, bf16[64,2048]{1,0:T(8,128)(2,1)S(1)}, u32[]{:S(2)}, u32[]{:S(2)}) %collective-permute-start.3) | collective-permute-done | bytes 262176 | tf_op jit(solution)/shard_map/ppermute | solution.py:349
  90.1 0.0 copy-start.4
  90.1 1.3 collective-permute-done.2.w2_ref
  91.5 0.0 copy-start.5
  91.5 8.6 %collective-permute-done.1.w1_ref = bf16[64,2048]{1,0:T(8,128)(2,1)S(1)} collective-permute-done((bf16[64,2048]{1,0:T(8,128)(2,1)S(1)}, bf16[64,2048]{1,0:T(8,128)(2,1)S(1)}, u32[]{:S(2)}, u32[]{:S(2)}) %collective-permute-start.1) | collective-permute-done | bytes 262176 | tf_op jit(solution)/shard_map/ppermute | solution.py:349
  100.0 0.0 copy-start.6
  100.0 0.0 copy-done.4
  100.0 0.0 copy-done.5
  100.0 0.7 copy-done.6
  100.7 10.5 %shard_map.114 = bf16[8,512,128]{2,1,0:T(8,128)(2,1)} custom-call(s32[1]{0:T(128)} %bitcast.x_ref, bf16[8,528,128]{2,1,0:T(8,128)(2,1)} %copy-done.1, f32[1024,128]{1,0:T(8,128)} %get-tuple-element.15.lse_ref, bf16[1024,2048]{1,0:T(8,128)(2,1)} %bitcast.9, bf16[64,2048]{1,0:T(8,128)(2,1)} %get-tuple-element.17.w0_ref, bf16[64,2048]{1,0:T(8,128)(2,1)} %copy-done.6, ...), custom_call_target="tpu_custom_call" | custom-call | flops 8589934592 | bytes 7340032 | tf_op jit(solution)/shard_map/pallas_call | solution.py:281
  111.2 0.0 all-to-all-done.2.got_ref
  111.2 7.7 %all-to-all-start.1 = ((bf16[8,512,128]{2,1,0:T(8,128)(2,1)}), bf16[8,512,128]{2,1,0:T(8,128)(2,1)S(1)}, u32[]{:S(2)}, u32[]{:S(2)}) async-start(bf16[8,512,128]{2,1,0:T(8,128)(2,1)} %shard_map.114), calls=%async_computation.1 | async-start | bytes 2097152 | tf_op jit(solution)/shard_map/all_to_all | solution.py:352
  118.9 0.2 shard_map.116
  119.1 8.7 %collective-permute-start.4 = (bf16[64,128]{1,0:T(8,128)(2,1)S(1)}, bf16[64,128]{1,0:T(8,128)(2,1)S(1)}, u32[]{:S(2)}, u32[]{:S(2)}) collective-permute-start(bf16[64,128]{1,0:T(8,128)(2,1)S(1)} %get-tuple-element.22), channel_id=1, source_target_pairs={{0,0},{1,8},{2,4},{3,12},{4,1},{5,9},{6,5},{7,13},{8,16},{9,24},{1... | collective-permute-start | bytes 49160 | tf_op jit(solution)/shard_map/ppermute | solution.py:353
  127.9 3.9 %collective-permute-start.5 = (bf16[64,128]{1,0:T(8,128)(2,1)S(1)}, bf16[64,128]{1,0:T(8,128)(2,1)S(1)}, u32[]{:S(2)}, u32[]{:S(2)}) collective-permute-start(bf16[64,128]{1,0:T(8,128)(2,1)S(1)} %get-tuple-element.23), channel_id=1, source_target_pairs={{0,1},{1,9},{2,5},{3,13},{4,16},{5,24},{6,20},{7,28},{8,17},{9,25}... | collective-permute-start | bytes 49160 | tf_op jit(solution)/shard_map/ppermute | solution.py:353
  131.8 8.6 %collective-permute-start.6 = (bf16[64,128]{1,0:T(8,128)(2,1)S(1)}, bf16[64,128]{1,0:T(8,128)(2,1)S(1)}, u32[]{:S(2)}, u32[]{:S(2)}) collective-permute-start(bf16[64,128]{1,0:T(8,128)(2,1)S(1)} %get-tuple-element.24), channel_id=1, source_target_pairs={{0,16},{1,24},{2,20},{3,28},{4,17},{5,25},{6,21},{7,29},{8,0},{9,8... | collective-permute-start | bytes 49160 | tf_op jit(solution)/shard_map/ppermute | solution.py:353
  140.4 1.9 %collective-permute-start.7 = (bf16[64,128]{1,0:T(8,128)(2,1)S(1)}, bf16[64,128]{1,0:T(8,128)(2,1)S(1)}, u32[]{:S(2)}, u32[]{:S(2)}) collective-permute-start(bf16[64,128]{1,0:T(8,128)(2,1)S(1)} %get-tuple-element.25), channel_id=1, source_target_pairs={{0,17},{1,25},{2,21},{3,29},{4,0},{5,8},{6,4},{7,12},{8,1},{9,9},{... | collective-permute-start | bytes 49160 | tf_op jit(solution)/shard_map/ppermute | solution.py:353
  142.3 0.0 collective-permute-done.4.a_ref
  142.3 0.0 collective-permute-done.5.b_ref
  142.3 0.0 collective-permute-done.6.c_ref
  142.3 7.0 %collective-permute-done.7.d_ref = bf16[64,128]{1,0:T(8,128)(2,1)S(1)} collective-permute-done((bf16[64,128]{1,0:T(8,128)(2,1)S(1)}, bf16[64,128]{1,0:T(8,128)(2,1)S(1)}, u32[]{:S(2)}, u32[]{:S(2)}) %collective-permute-start.7) | collective-permute-done | bytes 16416 | tf_op jit(solution)/shard_map/ppermute | solution.py:353
  149.3 0.8 shard_map.117
  150.2 0.0 all-to-all-done.1
  150.2 1.7 %shard_map.115 = (bf16[1,128,2048]{2,1,0:T(8,128)(2,1)}, bf16[1,128,1024]{2,1,0:T(8,128)(2,1)}, bf16[1,128,1024]{2,1,0:T(8,128)(2,1)}) custom-call(bf16[2,4,512,128]{3,2,1,0:T(8,128)(2,1)S(1)} %bitcast.6), custom_call_target="tpu_custom_call" | custom-call | bytes 2097152 | tf_op jit(solution)/shard_map/pallas_call | solution.py:322
  (1 shorter events, 0.0 us)
Async XLA Ops:
  7.2 14.6 %copy-start = (bf16[128,2048]{1,0:T(8,128)(2,1)S(1)}, bf16[128,2048]{1,0:T(8,128)(2,1)}, u32[]{:S(2)}) copy-start(bf16[128,2048]{1,0:T(8,128)(2,1)} %param.12) | copy-start | bytes 1572868
  7.2 55.4 %all-gather.3.cloned.1.call-start = ((), (), s32[]{:S(2)}) async-start(), calls=%async_computation.3 | async-start | bytes 4718592 | tf_op jit(solution)/shard_map/all_gather | solution.py:342
  11.4 25.5 %all-to-all-start = ((bf16[8,528,128]{2,1,0:T(8,128)(2,1)}), bf16[8,528,128]{2,1,0:T(8,128)(2,1)S(1)}, u32[]{:S(2)}, u32[]{:S(2)}) async-start(bf16[8,528,128]{2,1,0:T(8,128)(2,1)} %bitcast.7), calls=%async_computation | async-start | bytes 2162688 | tf_op jit(solution)/shard_map/all_to_all | solution.py:344
  21.8 27.6 %collective-permute-start = (bf16[64,2048]{1,0:T(8,128)(2,1)S(1)}, bf16[64,2048]{1,0:T(8,128)(2,1)S(1)}, u32[]{:S(2)}, u32[]{:S(2)}) collective-permute-start(bf16[64,2048]{1,0:T(8,128)(2,1)S(1)} %constant_dynamic-slice_fusion), channel_id=1, source_target_pairs={{0,0},{8,1},{4,2},{12,3},{16,4},{24,5},{20,6},{28,7},{256,8},{264,... | collective-permute-start | bytes 786440 | tf_op jit(solution)/shard_map/ppermute | solution.py:341
  36.9 1.0 copy-start.1
  49.4 13.1 %copy-start.2 = (bf16[64,2048]{1,0:T(8,128)(2,1)}, bf16[64,2048]{1,0:T(8,128)(2,1)S(1)}, u32[]{:S(2)}) copy-start(bf16[64,2048]{1,0:T(8,128)(2,1)S(1)} %collective-permute-done.w_ref) | copy-start | bytes 786436
  66.7 6.5 %copy-start.3 = (bf16[64,2048]{1,0:T(8,128)(2,1)S(1)}, bf16[64,2048]{1,0:T(8,128)(2,1)}, u32[]{:S(2)}) copy-start(bf16[64,2048]{1,0:T(8,128)(2,1)} %get-tuple-element.17.w0_ref) | copy-start | bytes 786436
  66.7 44.5 %all-to-all-start.2 = ((bf16[16,4,64,128]{3,2,1,0:T(8,128)(2,1)}), bf16[16,4,64,128]{3,2,1,0:T(8,128)(2,1)S(1)}, u32[]{:S(2)}, u32[]{:S(2)}) async-start(bf16[16,4,64,128]{3,2,1,0:T(8,128)(2,1)} %get-tuple-element.21), calls=%async_computation.2 | async-start | bytes 2097152 | tf_op jit(solution)/shard_map/all_to_all | solution.py:347
  73.2 16.9 %collective-permute-start.3 = (bf16[64,2048]{1,0:T(8,128)(2,1)S(1)}, bf16[64,2048]{1,0:T(8,128)(2,1)S(1)}, u32[]{:S(2)}, u32[]{:S(2)}) collective-permute-start(bf16[64,2048]{1,0:T(8,128)(2,1)S(1)} %copy-done.3), channel_id=1, source_target_pairs={{0,384},{128,0},{256,128},{384,256},{1,385},{129,1},{257,129},{385... | collective-permute-start | bytes 786440 | tf_op jit(solution)/shard_map/ppermute | solution.py:349
  77.7 13.7 %collective-permute-start.2 = (bf16[64,2048]{1,0:T(8,128)(2,1)S(1)}, bf16[64,2048]{1,0:T(8,128)(2,1)S(1)}, u32[]{:S(2)}, u32[]{:S(2)}) collective-permute-start(bf16[64,2048]{1,0:T(8,128)(2,1)S(1)} %copy-done.3), channel_id=1, source_target_pairs={{0,256},{128,384},{256,0},{384,128},{1,257},{129,385},{257,1},{385... | collective-permute-start | bytes 786440 | tf_op jit(solution)/shard_map/ppermute | solution.py:349
  80.2 19.8 %collective-permute-start.1 = (bf16[64,2048]{1,0:T(8,128)(2,1)S(1)}, bf16[64,2048]{1,0:T(8,128)(2,1)S(1)}, u32[]{:S(2)}, u32[]{:S(2)}) collective-permute-start(bf16[64,2048]{1,0:T(8,128)(2,1)S(1)} %copy-done.3), channel_id=1, source_target_pairs={{0,128},{128,256},{256,384},{384,0},{1,129},{129,257},{257,385},{3... | collective-permute-start | bytes 786440 | tf_op jit(solution)/shard_map/ppermute | solution.py:349
  90.1 9.9 %copy-start.4 = (bf16[64,2048]{1,0:T(8,128)(2,1)}, bf16[64,2048]{1,0:T(8,128)(2,1)S(1)}, u32[]{:S(2)}) copy-start(bf16[64,2048]{1,0:T(8,128)(2,1)S(1)} %collective-permute-done.3.w3_ref) | copy-start | bytes 786436
  91.5 8.6 %copy-start.5 = (bf16[64,2048]{1,0:T(8,128)(2,1)}, bf16[64,2048]{1,0:T(8,128)(2,1)S(1)}, u32[]{:S(2)}) copy-start(bf16[64,2048]{1,0:T(8,128)(2,1)S(1)} %collective-permute-done.2.w2_ref) | copy-start | bytes 786436
  100.0 0.7 copy-start.6
  111.2 38.9 %all-to-all-start.1 = ((bf16[8,512,128]{2,1,0:T(8,128)(2,1)}), bf16[8,512,128]{2,1,0:T(8,128)(2,1)S(1)}, u32[]{:S(2)}, u32[]{:S(2)}) async-start(bf16[8,512,128]{2,1,0:T(8,128)(2,1)} %shard_map.114), calls=%async_computation.1 | async-start | bytes 2097152 | tf_op jit(solution)/shard_map/all_to_all | solution.py:352
  119.1 23.2 %collective-permute-start.4 = (bf16[64,128]{1,0:T(8,128)(2,1)S(1)}, bf16[64,128]{1,0:T(8,128)(2,1)S(1)}, u32[]{:S(2)}, u32[]{:S(2)}) collective-permute-start(bf16[64,128]{1,0:T(8,128)(2,1)S(1)} %get-tuple-element.22), channel_id=1, source_target_pairs={{0,0},{1,8},{2,4},{3,12},{4,1},{5,9},{6,5},{7,13},{8,16},{9,24},{1... | collective-permute-start | bytes 49160 | tf_op jit(solution)/shard_map/ppermute | solution.py:353
  127.9 14.4 %collective-permute-start.5 = (bf16[64,128]{1,0:T(8,128)(2,1)S(1)}, bf16[64,128]{1,0:T(8,128)(2,1)S(1)}, u32[]{:S(2)}, u32[]{:S(2)}) collective-permute-start(bf16[64,128]{1,0:T(8,128)(2,1)S(1)} %get-tuple-element.23), channel_id=1, source_target_pairs={{0,1},{1,9},{2,5},{3,13},{4,16},{5,24},{6,20},{7,28},{8,17},{9,25}... | collective-permute-start | bytes 49160 | tf_op jit(solution)/shard_map/ppermute | solution.py:353
  131.8 10.6 %collective-permute-start.6 = (bf16[64,128]{1,0:T(8,128)(2,1)S(1)}, bf16[64,128]{1,0:T(8,128)(2,1)S(1)}, u32[]{:S(2)}, u32[]{:S(2)}) collective-permute-start(bf16[64,128]{1,0:T(8,128)(2,1)S(1)} %get-tuple-element.24), channel_id=1, source_target_pairs={{0,16},{1,24},{2,20},{3,28},{4,17},{5,25},{6,21},{7,29},{8,0},{9,8... | collective-permute-start | bytes 49160 | tf_op jit(solution)/shard_map/ppermute | solution.py:353
  140.4 9.0 %collective-permute-start.7 = (bf16[64,128]{1,0:T(8,128)(2,1)S(1)}, bf16[64,128]{1,0:T(8,128)(2,1)S(1)}, u32[]{:S(2)}, u32[]{:S(2)}) collective-permute-start(bf16[64,128]{1,0:T(8,128)(2,1)S(1)} %get-tuple-element.25), channel_id=1, source_target_pairs={{0,17},{1,25},{2,21},{3,29},{4,0},{5,8},{6,4},{7,12},{8,1},{9,9},{... | collective-permute-start | bytes 49160 | tf_op jit(solution)/shard_map/ppermute | solution.py:353
Sparse Core Ops, SparseCore 0:
  10.2 52.3 all-gather.2

commit v8 on v7

--- a/solution.py
+++ b/solution.py
@@ -46,12 +46,11 @@
     return moves
 
 
-def piece_moves(turn):
+def piece_moves():
     moves = []
     for x, yh, yl, w, p, c in devices():
-        piece = (w + turn) % 4
-        head = 2 * key_head(yl, p, c) + piece % 2
-        owner = place(x, yh, piece // 2, head // 4, (head // 2) % 2, head % 2)
+        head = 2 * key_head(yl, p, c) + w % 2
+        owner = place(x, yh, w // 2, head // 4, (head // 2) % 2, head % 2)
         moves.append((place(x, yh, yl, w, p, c), owner))
     return moves
 
@@ -125,11 +124,8 @@
         lse_ref[lo:ext, :] = jnp.where(lane == 0, stats[0], stats[1])
 
 
-def weight_kernel(out_ref, cot_ref, w_ref, wg_ref, share_ref):
-    @pl.when(pl.program_id(0) == 0)
-    def _():
-        share_ref[...] = w_ref[...]
-
+def weight_kernel(out_ref, cot_ref, a_ref, b_ref, c_ref, wg_ref):
+    del a_ref, b_ref, c_ref
     total = dot(out_ref[...], cot_ref[...], ((1,), (0,)))
     left = lax.broadcasted_iota(jnp.int32, (64, HD), 1) < 64
     for b in range(2):
@@ -190,19 +186,18 @@
         dv_ref[0, :, g * HD : (g + 1) * HD] = ret_ref[g, 0, 3 * TOK : 4 * TOK, :]
 
 
-def sum_kernel(w_ref, got_ref, out0_ref, out1_ref, out2_ref, out3_ref, total):
-    total[...] = jnp.sum(got_ref[...].astype(F32), axis=0)
-    for turn, out_ref in enumerate((out0_ref, out1_ref, out2_ref, out3_ref)):
-        out_ref[...] = total[lax.rem(w_ref[0] + turn, 4)].astype(BF16)
-
-
-def spread_kernel(a_ref, b_ref, c_ref, d_ref, out_ref):
-    total = (a_ref[...].astype(F32) + b_ref[...].astype(F32)) + (c_ref[...].astype(F32) + d_ref[...].astype(F32))
+def near_sum_kernel(got_ref, out_ref):
+    out_ref[...] = jnp.sum(got_ref[...].astype(F32), axis=0).astype(BF16)
+
+
+def far_sum_kernel(w_ref, got_ref, out_ref):
+    total = jnp.sum(got_ref[:, w_ref[0]].astype(F32), axis=0)
     out_ref[:, 0:64] = total[:, 0:64].T
     out_ref[:, 64:128] = total[:, 64:128].T
 
 
 SMEM = pl.BlockSpec(memory_space=pltpu.SMEM)
+VMEM = pl.BlockSpec(memory_space=pltpu.VMEM)
 
 
 def whole(*dims):
@@ -260,20 +255,20 @@
     )(arrived)
 
 
-def run_weight(out, cot, quarter):
+def run_weight(out, cot, after):
     return call(
         weight_kernel,
-        (shape((16, 4, 64, HD)), shape(quarter.shape)),
+        shape((16, 4, 64, HD)),
         flops=1 << 30,
         bytes_accessed=6 << 20,
         grid=(2,),
         in_specs=[
             whole(2 * HD, 2 * WINDOW),
             pl.BlockSpec((2 * WINDOW, 1024), lambda i: (0, i)),
-            whole(*quarter.shape),
-        ],
-        out_specs=[pl.BlockSpec((8, 4, 64, HD), lambda i: (i, 0, 0, 0)), whole(*quarter.shape)],
-    )(out, cot, quarter)
+        ]
+        + [pl.BlockSpec(memory_space=pl.ANY)] * 3,
+        out_specs=pl.BlockSpec((8, 4, 64, HD), lambda i: (i, 0, 0, 0)),
+    )(out, cot, *after)
 
 
 def run_backward(x, arrived, lse, cot, quarters):
@@ -296,26 +291,26 @@
     )(x, arrived, lse, cot, *quarters)
 
 
-def run_sum(w, got):
-    return call(
-        sum_kernel,
-        (shape((64, HD)),) * 4,
+def run_near_sum(got):
+    return call(
+        near_sum_kernel,
+        shape(got.shape[1:]),
         room=16,
         bytes_accessed=1 << 20,
-        in_specs=[SMEM, pl.BlockSpec(memory_space=pltpu.VMEM)],
-        out_specs=[pl.BlockSpec(memory_space=pltpu.VMEM)] * 4,
-        scratch_shapes=[pltpu.VMEM((4, 64, HD), F32)],
-    )(w, got)
-
-
-def run_spread(pieces):
-    return call(
-        spread_kernel,
+        in_specs=[VMEM],
+        out_specs=VMEM,
+    )(got)
+
+
+def run_far_sum(w, got):
+    return call(
+        far_sum_kernel,
         shape((64, HD), F32),
         room=16,
-        in_specs=[pl.BlockSpec(memory_space=pltpu.VMEM)] * 4,
-        out_specs=pl.BlockSpec(memory_space=pltpu.VMEM),
-    )(*pieces)
+        bytes_accessed=1 << 18,
+        in_specs=[SMEM, VMEM],
+        out_specs=VMEM,
+    )(w, got)
 
 
 def run_unpack(home, query_shape, key_shape):
@@ -343,15 +338,15 @@
     payload = run_pack(queries, keys, values, segment, row_type, pair_index)
     arrived = lax.all_to_all(payload, NEAR, 0, 0)
     out, lse = run_forward(arrived)
-    pieces, share = run_weight(out, cot, quarter)
+    quarters = [quarter] + [
+        lax.ppermute(quarter, "x", [(i, (i + turn) % 4) for i in range(4)]) for turn in (1, 2, 3)
+    ]
+    pieces = run_weight(out, cot, quarters[1:])
     got = lax.all_to_all(pieces, FAR, 0, 0)
-    quarters = [share] + [
-        lax.ppermute(share, "x", [(i, (i + turn) % 4) for i in range(4)]) for turn in (1, 2, 3)
-    ]
     back = run_backward(x.reshape(1), arrived, lse, cot, quarters)
     home = lax.all_to_all(back, NEAR, 0, 0)
-    sent = [lax.ppermute(part, AXES, piece_moves(turn)) for turn, part in enumerate(run_sum(w, got))]
-    weight_grad = run_spread(sent).T
+    windows = lax.all_gather(run_near_sum(got), "w", axis=0)
+    weight_grad = lax.ppermute(run_far_sum(w, windows), AXES, piece_moves()).T
     query_grad, key_grad, value_grad = run_unpack(home, queries.shape, keys.shape)
     return query_grad, key_grad, value_grad, weight_grad
 

time: 159 us -> 158 us (level)
  the two profiles are of different devices: /device:TPU:1 before, /device:TPU:8 now
where the time goes in v8:
time: 158 us; the launch traced here: 157 us
  waiting for transfers between devices  57.2 us (36%)
  starting transfers between devices  32.7 us (21%)
  blocking collectives  25.5 us (16%)
  Pallas kernels  25.4 us (16%)
  between operations  14.2 us (9%)
  local copies, waits for them, and re-layouts  2.33 us (1%)
    all_gather x1, blocking collectives, local(): windows = lax.all_gather(run_near_sum(got), 'w', axis=0)  25.5 us
    ppermute x1, waiting for transfers between devices, local(): quarter = lax.ppermute(share, AXES, weight_moves())  25.3 us
    all_to_all x1, waiting for transfers between devices, local(): got = lax.all_to_all(pieces, FAR, 0, 0)  19.6 us
    pallas_call x1, Pallas kernels, run_backward(): call(backward_kernel, shape((8, 4 * TOK, HD)), flops=8 << 30, bytes_acces...  10.5 us
    all_to_all x1, starting transfers between devices, local(): arrived = lax.all_to_all(payload, NEAR, 0, 0)  9.3 us
    ppermute x3, starting transfers between devices, local(): lax.ppermute(quarter, 'x', [(i, (i + turn) % 4) for i in range(4)])  8.76 us
    all_to_all x1, starting transfers between devices, local(): home = lax.all_to_all(back, NEAR, 0, 0)  6.77 us
    ppermute x1, waiting for transfers between devices, local(): weight_grad = lax.ppermute(run_far_sum(w, windows), AXES, piece_moves()).T  6.65 us
  transfers between devices with their start and end apart: 9, of which 4 were waited for; matrix products, arithmetic and copies ran while one was open for 0% of the time, Pallas kernels for 14%

profile of v8, /device:TPU:8, one launch (start us, length us, event | category | flops | bytes accessed | tf_op | source)
XLA Modules:
  0.0 157.4 jit_solution(17581731349860415397)
XLA Ops:
  7.2 0.0 copy-start
  7.2 0.0 all-gather.4.cloned.1.call-start
  7.2 0.7 all-gather.4.cloned.1.call-update
  7.9 3.5 %shard_map.111 = bf16[2,4,528,128]{3,2,1,0:T(8,128)(2,1)} custom-call(bf16[1,128,2048]{2,1,0:T(8,128)(2,1)} %q_ref.1, bf16[1,128,1024]{2,1,0:T(8,128)(2,1)} %k_ref.1, bf16[1,128,1024]{2,1,0:T(8,128)(2,1)} %v_ref.1, s32[1,128]{1,0:T(1,128)} %seg_ref.1, s32[1,128]{1,0:T(1,128)} %type_ref.1, s32[1,24]{1,0:T(1,128)} %pair_ref.1), custom_call_target="tpu_custom_call" | custom-call | bytes 2097152 | tf_op jit(solution)/shard_map/pallas_call | solution.py:226
  11.4 9.3 %all-to-all-start = ((bf16[8,528,128]{2,1,0:T(8,128)(2,1)}), bf16[8,528,128]{2,1,0:T(8,128)(2,1)S(1)}, u32[]{:S(2)}, u32[]{:S(2)}) async-start(bf16[8,528,128]{2,1,0:T(8,128)(2,1)} %bitcast.9), calls=%async_computation | async-start | bytes 2162688 | tf_op jit(solution)/shard_map/all_to_all | solution.py:339
  20.7 0.0 copy-done
  20.8 1.9 %collective-permute-start = (bf16[64,2048]{1,0:T(8,128)(2,1)S(1)}, bf16[64,2048]{1,0:T(8,128)(2,1)S(1)}, u32[]{:S(2)}, u32[]{:S(2)}) collective-permute-start(bf16[64,2048]{1,0:T(8,128)(2,1)S(1)} %constant_dynamic-slice_fusion), channel_id=1, source_target_pairs={{0,0},{8,1},{4,2},{12,3},{16,4},{24,5},{20,6},{28,7},{256,8},{264,... | collective-permute-start | bytes 786440 | tf_op jit(solution)/shard_map/ppermute | solution.py:336
  22.7 25.3 %collective-permute-done.w0_ref = bf16[64,2048]{1,0:T(8,128)(2,1)S(1)} collective-permute-done((bf16[64,2048]{1,0:T(8,128)(2,1)S(1)}, bf16[64,2048]{1,0:T(8,128)(2,1)S(1)}, u32[]{:S(2)}, u32[]{:S(2)}) %collective-permute-start) | collective-permute-done | bytes 262176 | tf_op jit(solution)/shard_map/ppermute | solution.py:336
  48.0 0.0 copy-start.5
  48.0 1.9 %collective-permute-start.3 = (bf16[64,2048]{1,0:T(8,128)(2,1)S(1)}, bf16[64,2048]{1,0:T(8,128)(2,1)S(1)}, u32[]{:S(2)}, u32[]{:S(2)}) collective-permute-start(bf16[64,2048]{1,0:T(8,128)(2,1)S(1)} %collective-permute-done.w0_ref), channel_id=1, source_target_pairs={{0,384},{128,0},{256,128},{384,256},{1,385},{129,1},{257,129},{385... | collective-permute-start | bytes 786440 | tf_op jit(solution)/shard_map/ppermute | solution.py:342
  49.9 3.5 %collective-permute-start.2 = (bf16[64,2048]{1,0:T(8,128)(2,1)S(1)}, bf16[64,2048]{1,0:T(8,128)(2,1)S(1)}, u32[]{:S(2)}, u32[]{:S(2)}) collective-permute-start(bf16[64,2048]{1,0:T(8,128)(2,1)S(1)} %collective-permute-done.w0_ref), channel_id=1, source_target_pairs={{0,256},{128,384},{256,0},{384,128},{1,257},{129,385},{257,1},{385... | collective-permute-start | bytes 786440 | tf_op jit(solution)/shard_map/ppermute | solution.py:342
  53.5 3.3 %collective-permute-start.1 = (bf16[64,2048]{1,0:T(8,128)(2,1)S(1)}, bf16[64,2048]{1,0:T(8,128)(2,1)S(1)}, u32[]{:S(2)}, u32[]{:S(2)}) collective-permute-start(bf16[64,2048]{1,0:T(8,128)(2,1)S(1)} %collective-permute-done.w0_ref), channel_id=1, source_target_pairs={{0,128},{128,256},{256,384},{384,0},{1,129},{129,257},{257,385},{3... | collective-permute-start | bytes 786440 | tf_op jit(solution)/shard_map/ppermute | solution.py:342
  56.8 0.0 all-to-all-done.pay_ref
  56.8 0.0 copy-start.1
  56.8 1.0 copy-done.1
  57.8 5.3 %shard_map.112 = (bf16[256,1024]{1,0:T(8,128)(2,1)}, f32[1024,128]{1,0:T(8,128)}) custom-call(bf16[8,528,128]{2,1,0:T(8,128)(2,1)} %copy-done.1), custom_call_target="tpu_custom_call" | custom-call | flops 4294967296 | bytes 2097152 | tf_op jit(solution)/shard_map/pallas_call | solution.py:244
  63.1 0.0 copy-done.5
  63.1 0.0 collective-permute-done.3.w3_ref.c_ref
  63.1 0.0 copy-start.2
  63.1 0.0 collective-permute-done.2.w2_ref.b_ref
  63.1 0.0 copy-start.3
  63.1 4.9 %collective-permute-done.1.w1_ref.a_ref = bf16[64,2048]{1,0:T(8,128)(2,1)S(1)} collective-permute-done((bf16[64,2048]{1,0:T(8,128)(2,1)S(1)}, bf16[64,2048]{1,0:T(8,128)(2,1)S(1)}, u32[]{:S(2)}, u32[]{:S(2)}) %collective-permute-start.1) | collective-permute-done | bytes 262176 | tf_op jit(solution)/shard_map/ppermute | solution.py:342
  68.0 0.0 copy-start.4
  68.0 0.0 all-gather.4.cloned.1.call-done
  68.1 0.0 copy-done.2
  68.1 0.0 copy-done.3
  68.1 0.7 copy-done.4
  68.8 4.1 %shard_map.115 = bf16[16,4,64,128]{3,2,1,0:T(8,128)(2,1)} custom-call(bf16[256,1024]{1,0:T(8,128)(2,1)} %get-tuple-element.13.out_ref, bf16[1024,2048]{1,0:T(8,128)(2,1)} %bitcast.10, bf16[64,2048]{1,0:T(8,128)(2,1)} %copy-done.4, bf16[64,2048]{1,0:T(8,128)(2,1)} %copy-done.3, bf16[64,2048]{1,0:T(8,128)(2,1)} %copy-done.2), custom_call_target="tpu_custom_call" | custom-call | flops 1073741824 | bytes 6291456 | tf_op jit(solution)/shard_map/pallas_call | solution.py:259
  72.8 3.7 %all-to-all-start.2 = ((bf16[16,4,64,128]{3,2,1,0:T(8,128)(2,1)}), bf16[16,4,64,128]{3,2,1,0:T(8,128)(2,1)S(1)}, u32[]{:S(2)}, u32[]{:S(2)}) async-start(bf16[16,4,64,128]{3,2,1,0:T(8,128)(2,1)} %shard_map.115), calls=%async_computation.2 | async-start | bytes 2097152 | tf_op jit(solution)/shard_map/all_to_all | solution.py:345
  76.5 10.5 %shard_map.113 = bf16[8,512,128]{2,1,0:T(8,128)(2,1)} custom-call(s32[1]{0:T(128)} %bitcast.x_ref, bf16[8,528,128]{2,1,0:T(8,128)(2,1)} %copy-done.1, f32[1024,128]{1,0:T(8,128)} %get-tuple-element.9.lse_ref, bf16[1024,2048]{1,0:T(8,128)(2,1)} %bitcast.11, bf16[64,2048]{1,0:T(8,128)(2,1)} %copy-done.5, bf16[64,2048]{1,0:T(8,128)(2,1)} %copy-done.4, ...), custom_call_target="tpu_custom_call" | custom-call | flops 8589934592 | bytes 7340032 | tf_op jit(solution)/shard_map/pallas_call | solution.py:276
  87.0 19.6 %all-to-all-done.2.got_ref = bf16[16,4,64,128]{3,2,1,0:T(8,128)(2,1)S(1)} async-done(((bf16[16,4,64,128]{3,2,1,0:T(8,128)(2,1)}), bf16[16,4,64,128]{3,2,1,0:T(8,128)(2,1)S(1)}, u32[]{:S(2)}, u32[]{:S(2)}) %all-to-all-start.2) | async-done | bytes 1048608 | tf_op jit(solution)/shard_map/all_to_all | solution.py:345
  106.7 6.8 %all-to-all-start.1 = ((bf16[8,512,128]{2,1,0:T(8,128)(2,1)}), bf16[8,512,128]{2,1,0:T(8,128)(2,1)S(1)}, u32[]{:S(2)}, u32[]{:S(2)}) async-start(bf16[8,512,128]{2,1,0:T(8,128)(2,1)} %shard_map.113), calls=%async_computation.1 | async-start | bytes 2097152 | tf_op jit(solution)/shard_map/all_to_all | solution.py:347
  113.4 0.1 shard_map.116
  113.6 25.5 %all-gather.1 = bf16[16,64,128]{2,1,0:T(8,128)(2,1)S(1)} all-gather(bf16[4,64,128]{2,1,0:T(8,128)(2,1)S(1)} %shard_map.116), channel_id=3, replica_groups=mesh['x'=4,'yh'=4,'yl'=2,'w'=4,'p'=2,'c'=2] {'w'}, dimensions={0}, use_global_device_ids=true | all-gather | bytes 327680 | tf_op jit(solution)/shard_map/all_gather | solution.py:348
  139.1 0.2 shard_map.117
  139.3 2.3 %collective-permute-start.4 = (f32[64,128]{1,0:T(8,128)S(1)}, f32[64,128]{1,0:T(8,128)S(1)}, u32[]{:S(2)}, u32[]{:S(2)}) collective-permute-start(f32[64,128]{1,0:T(8,128)S(1)} %shard_map.117), channel_id=1, source_target_pairs={{0,0},{1,8},{2,4},{3,12},{4,1},{5,9},{6,5},{7,13},{8,16},{9,24},{1... | collective-permute-start | bytes 98312 | tf_op jit(solution)/shard_map/ppermute | solution.py:349
  141.6 0.0 all-to-all-done.1
  141.6 1.7 %shard_map.114 = (bf16[1,128,2048]{2,1,0:T(8,128)(2,1)}, bf16[1,128,1024]{2,1,0:T(8,128)(2,1)}, bf16[1,128,1024]{2,1,0:T(8,128)(2,1)}) custom-call(bf16[2,4,512,128]{3,2,1,0:T(8,128)(2,1)S(1)} %bitcast.7), custom_call_target="tpu_custom_call" | custom-call | bytes 2097152 | tf_op jit(solution)/shard_map/pallas_call | solution.py:317
  143.3 6.6 %collective-permute-done.4 = f32[64,128]{1,0:T(8,128)S(1)} collective-permute-done((f32[64,128]{1,0:T(8,128)S(1)}, f32[64,128]{1,0:T(8,128)S(1)}, u32[]{:S(2)}, u32[]{:S(2)}) %collective-permute-start.4) | collective-permute-done | bytes 32800 | tf_op jit(solution)/shard_map/ppermute | solution.py:349
  149.9 0.6 copy.13
  (1 shorter events, 0.0 us)
Async XLA Ops:
  7.2 13.6 %copy-start = (bf16[128,2048]{1,0:T(8,128)(2,1)S(1)}, bf16[128,2048]{1,0:T(8,128)(2,1)}, u32[]{:S(2)}) copy-start(bf16[128,2048]{1,0:T(8,128)(2,1)} %param.12) | copy-start | bytes 1572868
  7.2 60.9 %all-gather.4.cloned.1.call-start = ((), (), s32[]{:S(2)}) async-start(), calls=%async_computation.3 | async-start | bytes 4718592 | tf_op jit(solution)/shard_map/all_gather | solution.py:337
  11.4 45.4 %all-to-all-start = ((bf16[8,528,128]{2,1,0:T(8,128)(2,1)}), bf16[8,528,128]{2,1,0:T(8,128)(2,1)S(1)}, u32[]{:S(2)}, u32[]{:S(2)}) async-start(bf16[8,528,128]{2,1,0:T(8,128)(2,1)} %bitcast.9), calls=%async_computation | async-start | bytes 2162688 | tf_op jit(solution)/shard_map/all_to_all | solution.py:339
  20.8 27.3 %collective-permute-start = (bf16[64,2048]{1,0:T(8,128)(2,1)S(1)}, bf16[64,2048]{1,0:T(8,128)(2,1)S(1)}, u32[]{:S(2)}, u32[]{:S(2)}) collective-permute-start(bf16[64,2048]{1,0:T(8,128)(2,1)S(1)} %constant_dynamic-slice_fusion), channel_id=1, source_target_pairs={{0,0},{8,1},{4,2},{12,3},{16,4},{24,5},{20,6},{28,7},{256,8},{264,... | collective-permute-start | bytes 786440 | tf_op jit(solution)/shard_map/ppermute | solution.py:336
  48.0 15.1 %copy-start.5 = (bf16[64,2048]{1,0:T(8,128)(2,1)}, bf16[64,2048]{1,0:T(8,128)(2,1)S(1)}, u32[]{:S(2)}) copy-start(bf16[64,2048]{1,0:T(8,128)(2,1)S(1)} %collective-permute-done.w0_ref) | copy-start | bytes 786436
  48.0 15.1 %collective-permute-start.3 = (bf16[64,2048]{1,0:T(8,128)(2,1)S(1)}, bf16[64,2048]{1,0:T(8,128)(2,1)S(1)}, u32[]{:S(2)}, u32[]{:S(2)}) collective-permute-start(bf16[64,2048]{1,0:T(8,128)(2,1)S(1)} %collective-permute-done.w0_ref), channel_id=1, source_target_pairs={{0,384},{128,0},{256,128},{384,256},{1,385},{129,1},{257,129},{385... | collective-permute-start | bytes 786440 | tf_op jit(solution)/shard_map/ppermute | solution.py:342
  49.9 13.2 %collective-permute-start.2 = (bf16[64,2048]{1,0:T(8,128)(2,1)S(1)}, bf16[64,2048]{1,0:T(8,128)(2,1)S(1)}, u32[]{:S(2)}, u32[]{:S(2)}) collective-permute-start(bf16[64,2048]{1,0:T(8,128)(2,1)S(1)} %collective-permute-done.w0_ref), channel_id=1, source_target_pairs={{0,256},{128,384},{256,0},{384,128},{1,257},{129,385},{257,1},{385... | collective-permute-start | bytes 786440 | tf_op jit(solution)/shard_map/ppermute | solution.py:342
  53.5 14.6 %collective-permute-start.1 = (bf16[64,2048]{1,0:T(8,128)(2,1)S(1)}, bf16[64,2048]{1,0:T(8,128)(2,1)S(1)}, u32[]{:S(2)}, u32[]{:S(2)}) collective-permute-start(bf16[64,2048]{1,0:T(8,128)(2,1)S(1)} %collective-permute-done.w0_ref), channel_id=1, source_target_pairs={{0,128},{128,256},{256,384},{384,0},{1,129},{129,257},{257,385},{3... | collective-permute-start | bytes 786440 | tf_op jit(solution)/shard_map/ppermute | solution.py:342
  56.8 1.0 copy-start.1
  63.1 5.0 %copy-start.2 = (bf16[64,2048]{1,0:T(8,128)(2,1)}, bf16[64,2048]{1,0:T(8,128)(2,1)S(1)}, u32[]{:S(2)}) copy-start(bf16[64,2048]{1,0:T(8,128)(2,1)S(1)} %collective-permute-done.3.w3_ref.c_ref) | copy-start | bytes 786436
  63.1 4.9 %copy-start.3 = (bf16[64,2048]{1,0:T(8,128)(2,1)}, bf16[64,2048]{1,0:T(8,128)(2,1)S(1)}, u32[]{:S(2)}) copy-start(bf16[64,2048]{1,0:T(8,128)(2,1)S(1)} %collective-permute-done.2.w2_ref.b_ref) | copy-start | bytes 786436
  68.0 0.7 copy-start.4
  72.8 33.8 %all-to-all-start.2 = ((bf16[16,4,64,128]{3,2,1,0:T(8,128)(2,1)}), bf16[16,4,64,128]{3,2,1,0:T(8,128)(2,1)S(1)}, u32[]{:S(2)}, u32[]{:S(2)}) async-start(bf16[16,4,64,128]{3,2,1,0:T(8,128)(2,1)} %shard_map.115), calls=%async_computation.2 | async-start | bytes 2097152 | tf_op jit(solution)/shard_map/all_to_all | solution.py:345
  106.7 34.9 %all-to-all-start.1 = ((bf16[8,512,128]{2,1,0:T(8,128)(2,1)}), bf16[8,512,128]{2,1,0:T(8,128)(2,1)S(1)}, u32[]{:S(2)}, u32[]{:S(2)}) async-start(bf16[8,512,128]{2,1,0:T(8,128)(2,1)} %shard_map.113), calls=%async_computation.1 | async-start | bytes 2097152 | tf_op jit(solution)/shard_map/all_to_all | solution.py:347
  139.3 10.6 %collective-permute-start.4 = (f32[64,128]{1,0:T(8,128)S(1)}, f32[64,128]{1,0:T(8,128)S(1)}, u32[]{:S(2)}, u32[]{:S(2)}) collective-permute-start(f32[64,128]{1,0:T(8,128)S(1)} %shard_map.117), channel_id=1, source_target_pairs={{0,0},{1,8},{2,4},{3,12},{4,1},{5,9},{6,5},{7,13},{8,16},{9,24},{1... | collective-permute-start | bytes 98312 | tf_op jit(solution)/shard_map/ppermute | solution.py:349
Sparse Core Ops, SparseCore 0:
  10.2 48.8 all-gather.3

commit v9 on v8

--- a/solution.py
+++ b/solution.py
@@ -136,11 +136,13 @@
             wg_ref[m, 2 + b] = jnp.where(left, pltpu.roll(upper, 64, 1), lower).astype(BF16)
 
 
-def backward_kernel(x_ref, pay_ref, lse_ref, cot_ref, w0_ref, w1_ref, w2_ref, w3_ref, ret_ref, wbuf, ghbuf):
+def backward_kernel(me_ref, pay_ref, lse_ref, cot_ref, w0_ref, w1_ref, w2_ref, w3_ref, *refs):
+    *out_refs, wbuf, ghbuf, ret_ref = refs
+
     @pl.when(pl.program_id(0) == 0)
     def _():
         for turn, quarter in enumerate((w0_ref, w1_ref, w2_ref, w3_ref)):
-            first = pl.multiple_of(lax.rem(x_ref[0] + 4 - turn, 4) * 64, 64)
+            first = pl.multiple_of(lax.rem(me_ref[0] + 4 - turn, 4) * 64, 64)
             wbuf[pl.ds(first, 64), :] = quarter[...]
 
     ghbuf[...] = dot(cot_ref[...], wbuf[...], ((1,), (1,))).astype(BF16)
@@ -176,14 +178,24 @@
         for first, parts in ((2 * TOK, kparts), (3 * TOK, vparts)):
             both = parts[0][block].astype(BF16).astype(F32) + parts[1][block].astype(BF16).astype(F32)
             ret_ref[2 * block : 2 * block + 2, first : first + TOK, :] = both.astype(BF16).reshape(2, TOK, HD)
-
-
-def unpack_kernel(ret_ref, dq_ref, dk_ref, dv_ref):
-    for g in range(2):
-        dq_ref[0, :, 2 * g * HD : (2 * g + 1) * HD] = ret_ref[g, 0, 0:TOK, :]
-        dq_ref[0, :, (2 * g + 1) * HD : (2 * g + 2) * HD] = ret_ref[g, 0, TOK : 2 * TOK, :]
-        dk_ref[0, :, g * HD : (g + 1) * HD] = ret_ref[g, 0, 2 * TOK : 3 * TOK, :]
-        dv_ref[0, :, g * HD : (g + 1) * HD] = ret_ref[g, 0, 3 * TOK : 4 * TOK, :]
+    for step in range(2):
+
+        @pl.when(pl.program_id(0) == step)
+        def _():
+            for k in range(4):
+                out_refs[4 * step + k][...] = ret_ref[jnp.bitwise_xor(me_ref[2], k)]
+
+
+def unpack_kernel(me_ref, *refs):
+    *got_refs, dq_ref, dk_ref, dv_ref = refs
+    for k, got_ref in enumerate(got_refs):
+        source = jnp.bitwise_xor(4 * me_ref[1] + me_ref[2], k)
+        head = key_head(source // 4, (source // 2) % 2, source % 2)
+        near = pl.ds(pl.multiple_of(head * HD, HD), HD)
+        dq_ref[0, :, pl.ds(pl.multiple_of(head * 2 * HD, HD), HD)] = got_ref[0:TOK, :]
+        dq_ref[0, :, pl.ds(pl.multiple_of(head * 2 * HD + HD, HD), HD)] = got_ref[TOK : 2 * TOK, :]
+        dk_ref[0, :, near] = got_ref[2 * TOK : 3 * TOK, :]
+        dv_ref[0, :, near] = got_ref[3 * TOK : 4 * TOK, :]
 
 
 def near_sum_kernel(got_ref, out_ref):
@@ -271,24 +283,35 @@
     )(out, cot, *after)
 
 
-def run_backward(x, arrived, lse, cot, quarters):
+def run_backward(me, arrived, lse, cot, quarters):
     width = cot.shape[1]
+
+    def row(step, me_ref):
+        return jnp.bitwise_xor(step, me_ref[1])
+
+    grid_spec = pltpu.PrefetchScalarGridSpec(
+        num_scalar_prefetch=1,
+        grid=(2,),
+        in_specs=[
+            pl.BlockSpec((4, PAY, HD), lambda i, me_ref: (row(i, me_ref), 0, 0)),
+            pl.BlockSpec((WINDOW, HD), lambda i, me_ref: (row(i, me_ref), 0)),
+            pl.BlockSpec((WINDOW, width), lambda i, me_ref: (row(i, me_ref), 0)),
+        ]
+        + [whole(64, width)] * 4,
+        out_specs=[whole(4 * TOK, HD)] * 8,
+        scratch_shapes=[
+            pltpu.VMEM((2 * HD, width), BF16),
+            pltpu.VMEM((WINDOW, 2 * HD), BF16),
+            pltpu.VMEM((4, 4 * TOK, HD), BF16),
+        ],
+    )
     return call(
         backward_kernel,
-        shape((8, 4 * TOK, HD)),
+        (shape((4 * TOK, HD)),) * 8,
         flops=8 << 30,
         bytes_accessed=7 << 20,
-        grid=(2,),
-        in_specs=[
-            SMEM,
-            pl.BlockSpec((4, PAY, HD), lambda u: (u, 0, 0)),
-            pl.BlockSpec((WINDOW, HD), lambda u: (u, 0)),
-            pl.BlockSpec((WINDOW, width), lambda u: (u, 0)),
-        ]
-        + [whole(64, width)] * 4,
-        out_specs=pl.BlockSpec((4, 4 * TOK, HD), lambda u: (u, 0, 0)),
-        scratch_shapes=[pltpu.VMEM((2 * HD, width), BF16), pltpu.VMEM((WINDOW, 2 * HD), BF16)],
-    )(x, arrived, lse, cot, *quarters)
+        grid_spec=grid_spec,
+    )(me, arrived, lse, cot, *quarters)
 
 
 def run_near_sum(got):
@@ -313,20 +336,15 @@
     )(w, got)
 
 
-def run_unpack(home, query_shape, key_shape):
+def run_unpack(me, home, query_shape, key_shape):
     return call(
         unpack_kernel,
         (shape(query_shape), shape(key_shape), shape(key_shape)),
         room=16,
         bytes_accessed=2 << 20,
-        grid=(4,),
-        in_specs=[pl.BlockSpec((2, 1, 4 * TOK, HD), pair_of_heads)],
-        out_specs=[
-            pl.BlockSpec((1, TOK, 4 * HD), lambda i: (0, 0, i)),
-            pl.BlockSpec((1, TOK, 2 * HD), lambda i: (0, 0, i)),
-            pl.BlockSpec((1, TOK, 2 * HD), lambda i: (0, 0, i)),
-        ],
-    )(home.reshape(2, 4, 4 * TOK, HD))
+        in_specs=[SMEM] + [VMEM] * 8,
+        out_specs=[whole(*query_shape), whole(*key_shape), whole(*key_shape)],
+    )(me, *home)
 
 
 def local(queries, keys, values, cotangent, out_weight, segment, row_type, pair_index):
@@ -343,11 +361,14 @@
     ]
     pieces = run_weight(out, cot, quarters[1:])
     got = lax.all_to_all(pieces, FAR, 0, 0)
-    back = run_backward(x.reshape(1), arrived, lse, cot, quarters)
-    home = lax.all_to_all(back, NEAR, 0, 0)
+    me = jnp.stack([x, lax.axis_index("yl"), 2 * lax.axis_index("p") + lax.axis_index("c")]).astype(jnp.int32)
+    own, *others = run_backward(me, arrived, lse, cot, quarters)
+    home = [own] + [
+        lax.ppermute(other, NEAR, [(i, i ^ (k + 1)) for i in range(8)]) for k, other in enumerate(others)
+    ]
     windows = lax.all_gather(run_near_sum(got), "w", axis=0)
     weight_grad = lax.ppermute(run_far_sum(w, windows), AXES, piece_moves()).T
-    query_grad, key_grad, value_grad = run_unpack(home, queries.shape, keys.shape)
+    query_grad, key_grad, value_grad = run_unpack(me, home, queries.shape, keys.shape)
     return query_grad, key_grad, value_grad, weight_grad
 
 

time: 158 us -> 152 us (0.962)
  the two profiles are of different devices: /device:TPU:8 before, /device:TPU:1 now
where the time goes in v9:
time: 152 us; the launch traced here: 149 us
  starting transfers between devices  62 us (41%)
  waiting for transfers between devices  28.5 us (19%)
  Pallas kernels  26.4 us (17%)
  blocking collectives  15 us (10%)
  between operations  14.3 us (9%)
  local copies, waits for them, and re-layouts  2.39 us (2%)
    ppermute x7, starting transfers between devices, local(): lax.ppermute(other, NEAR, [(i, i ^ k + 1) for i in range(8)])  24.9 us
    ppermute x1, waiting for transfers between devices, local(): quarter = lax.ppermute(share, AXES, weight_moves())  23.6 us
    all_gather x1, blocking collectives, local(): windows = lax.all_gather(run_near_sum(got), 'w', axis=0)  15 us
    pallas_call x1, Pallas kernels, run_backward(): call(backward_kernel, (shape((4 * TOK, HD)),) * 8, flops=8 << 30, bytes_a...  11.4 us
    all_to_all x1, starting transfers between devices, local(): arrived = lax.all_to_all(payload, NEAR, 0, 0)  10.3 us
    ppermute x3, starting transfers between devices, local(): lax.ppermute(quarter, 'x', [(i, (i + turn) % 4) for i in range(4)])  9.17 us
    ppermute x1, starting transfers between devices, local(): weight_grad = lax.ppermute(run_far_sum(w, windows), AXES, piece_moves()).T  7.86 us
    all_to_all x1, starting transfers between devices, local(): got = lax.all_to_all(pieces, FAR, 0, 0)  5.76 us
  transfers between devices with their start and end apart: 15, of which 3 were waited for; matrix products, arithmetic and copies ran while one was open for 0% of the time, Pallas kernels for 15%

profile of v9, /device:TPU:1, one launch (start us, length us, event | category | flops | bytes accessed | tf_op | source)
XLA Modules:
  0.0 149.3 jit_solution(2184286968611189430)
XLA Ops:
  7.2 0.0 copy-start
  7.2 0.0 all-gather.4.cloned.1.call-start
  7.2 0.7 all-gather.4.cloned.1.call-update
  7.9 3.5 %shard_map.111 = bf16[2,4,528,128]{3,2,1,0:T(8,128)(2,1)} custom-call(bf16[1,128,2048]{2,1,0:T(8,128)(2,1)} %q_ref.1, bf16[1,128,1024]{2,1,0:T(8,128)(2,1)} %k_ref.1, bf16[1,128,1024]{2,1,0:T(8,128)(2,1)} %v_ref.1, s32[1,128]{1,0:T(1,128)} %seg_ref.1, s32[1,128]{1,0:T(1,128)} %type_ref.1, s32[1,24]{1,0:T(1,128)} %pair_ref.1), custom_call_target="tpu_custom_call" | custom-call | bytes 2097152 | tf_op jit(solution)/shard_map/pallas_call | solution.py:238
  11.4 10.3 %all-to-all-start = ((bf16[8,528,128]{2,1,0:T(8,128)(2,1)}), bf16[8,528,128]{2,1,0:T(8,128)(2,1)S(1)}, u32[]{:S(2)}, u32[]{:S(2)}) async-start(bf16[8,528,128]{2,1,0:T(8,128)(2,1)} %bitcast.9), calls=%async_computation | async-start | bytes 2162688 | tf_op jit(solution)/shard_map/all_to_all | solution.py:357
  21.8 0.0 copy-done
  21.8 4.0 %collective-permute-start = (bf16[64,2048]{1,0:T(8,128)(2,1)S(1)}, bf16[64,2048]{1,0:T(8,128)(2,1)S(1)}, u32[]{:S(2)}, u32[]{:S(2)}) collective-permute-start(bf16[64,2048]{1,0:T(8,128)(2,1)S(1)} %constant_dynamic-slice_fusion), channel_id=1, source_target_pairs={{0,0},{8,1},{4,2},{12,3},{16,4},{24,5},{20,6},{28,7},{256,8},{264,... | collective-permute-start | bytes 786440 | tf_op jit(solution)/shard_map/ppermute | solution.py:354
  25.8 23.6 %collective-permute-done.w0_ref = bf16[64,2048]{1,0:T(8,128)(2,1)S(1)} collective-permute-done((bf16[64,2048]{1,0:T(8,128)(2,1)S(1)}, bf16[64,2048]{1,0:T(8,128)(2,1)S(1)}, u32[]{:S(2)}, u32[]{:S(2)}) %collective-permute-start) | collective-permute-done | bytes 262176 | tf_op jit(solution)/shard_map/ppermute | solution.py:354
  49.3 0.0 copy-start.7
  49.4 4.8 %collective-permute-start.3 = (bf16[64,2048]{1,0:T(8,128)(2,1)S(1)}, bf16[64,2048]{1,0:T(8,128)(2,1)S(1)}, u32[]{:S(2)}, u32[]{:S(2)}) collective-permute-start(bf16[64,2048]{1,0:T(8,128)(2,1)S(1)} %collective-permute-done.w0_ref), channel_id=1, source_target_pairs={{0,384},{128,0},{256,128},{384,256},{1,385},{129,1},{257,129},{385... | collective-permute-start | bytes 786440 | tf_op jit(solution)/shard_map/ppermute | solution.py:360
  54.1 1.9 %collective-permute-start.2 = (bf16[64,2048]{1,0:T(8,128)(2,1)S(1)}, bf16[64,2048]{1,0:T(8,128)(2,1)S(1)}, u32[]{:S(2)}, u32[]{:S(2)}) collective-permute-start(bf16[64,2048]{1,0:T(8,128)(2,1)S(1)} %collective-permute-done.w0_ref), channel_id=1, source_target_pairs={{0,256},{128,384},{256,0},{384,128},{1,257},{129,385},{257,1},{385... | collective-permute-start | bytes 786440 | tf_op jit(solution)/shard_map/ppermute | solution.py:360
  56.1 2.5 %collective-permute-start.1 = (bf16[64,2048]{1,0:T(8,128)(2,1)S(1)}, bf16[64,2048]{1,0:T(8,128)(2,1)S(1)}, u32[]{:S(2)}, u32[]{:S(2)}) collective-permute-start(bf16[64,2048]{1,0:T(8,128)(2,1)S(1)} %collective-permute-done.w0_ref), channel_id=1, source_target_pairs={{0,128},{128,256},{256,384},{384,0},{1,129},{129,257},{257,385},{3... | collective-permute-start | bytes 786440 | tf_op jit(solution)/shard_map/ppermute | solution.py:360
  58.5 0.0 all-to-all-done.pay_ref
  58.6 0.0 copy-start.3
  58.6 1.0 copy-done.3
  59.6 5.2 %shard_map.112 = (bf16[256,1024]{1,0:T(8,128)(2,1)}, f32[1024,128]{1,0:T(8,128)}) custom-call(bf16[8,528,128]{2,1,0:T(8,128)(2,1)} %copy-done.3), custom_call_target="tpu_custom_call" | custom-call | flops 4294967296 | bytes 2097152 | tf_op jit(solution)/shard_map/pallas_call | solution.py:256
  64.8 0.0 copy-done.7
  64.8 0.0 collective-permute-done.3.w3_ref.c_ref
  64.8 0.0 copy-start.4
  64.9 0.7 collective-permute-done.2.w2_ref.b_ref
  65.5 0.0 copy-start.5
  65.5 3.5 %collective-permute-done.1.w1_ref.a_ref = bf16[64,2048]{1,0:T(8,128)(2,1)S(1)} collective-permute-done((bf16[64,2048]{1,0:T(8,128)(2,1)S(1)}, bf16[64,2048]{1,0:T(8,128)(2,1)S(1)}, u32[]{:S(2)}, u32[]{:S(2)}) %collective-permute-start.1) | collective-permute-done | bytes 262176 | tf_op jit(solution)/shard_map/ppermute | solution.py:360
  69.1 0.0 copy-start.6
  69.1 0.0 all-gather.4.cloned.1.call-done
  69.1 0.0 copy-done.4
  69.1 0.0 copy-done.5
  69.1 0.7 copy-done.6
  69.8 4.1 %shard_map.115 = bf16[16,4,64,128]{3,2,1,0:T(8,128)(2,1)} custom-call(bf16[256,1024]{1,0:T(8,128)(2,1)} %get-tuple-element.29.out_ref, bf16[1024,2048]{1,0:T(8,128)(2,1)} %bitcast.10, bf16[64,2048]{1,0:T(8,128)(2,1)} %copy-done.6, bf16[64,2048]{1,0:T(8,128)(2,1)} %copy-done.5, bf16[64,2048]{1,0:T(8,128)(2,1)} %copy-done.4), custom_call_target="tpu_custom_call" | custom-call | flops 1073741824 | bytes 6291456 | tf_op jit(solution)/shard_map/pallas_call | solution.py:271
  73.8 5.8 %all-to-all-start.1 = ((bf16[16,4,64,128]{3,2,1,0:T(8,128)(2,1)}), bf16[16,4,64,128]{3,2,1,0:T(8,128)(2,1)S(1)}, u32[]{:S(2)}, u32[]{:S(2)}) async-start(bf16[16,4,64,128]{3,2,1,0:T(8,128)(2,1)} %shard_map.115), calls=%async_computation.1 | async-start | bytes 2097152 | tf_op jit(solution)/shard_map/all_to_all | solution.py:363
  79.6 0.6 pad_add_fusion.me_ref
  80.3 11.4 %shard_map.113 = (bf16[512,128]{1,0:T(8,128)(2,1)}, bf16[512,128]{1,0:T(8,128)(2,1)}, bf16[512,128]{1,0:T(8,128)(2,1)}, bf16[512,128]{1,0:T(8,128)(2,1)}, bf16[5...) custom-call(s32[3]{0:T(128)} %pad_add_fusion.me_ref, ...), custom_call_target="tpu_custom_call" | custom-call | flops 8589934592 | bytes 7340032 | tf_op jit(solution)/shard_map/pallas_call | solution.py:308
  91.7 0.0 copy-start.9
  91.7 0.0 copy-start.8
  91.7 0.0 copy-start.1
  91.7 0.0 copy-start.2
  91.7 2.1 %collective-permute-start.4 = (bf16[512,128]{1,0:T(8,128)(2,1)}, bf16[512,128]{1,0:T(8,128)(2,1)S(1)}, u32[]{:S(2)}, u32[]{:S(2)}) collective-permute-start(bf16[512,128]{1,0:T(8,128)(2,1)} %get-tuple-element.19), channel_id=1, source_target_pairs={{0,1},{1,0},{2,3},{3,2},{16,17},{17,16},{18,19},{19,18},{4,5},{5,4... | collective-permute-start | bytes 393224 | tf_op jit(solution)/shard_map/ppermute | solution.py:367
  93.8 8.5 %collective-permute-start.5 = (bf16[512,128]{1,0:T(8,128)(2,1)}, bf16[512,128]{1,0:T(8,128)(2,1)S(1)}, u32[]{:S(2)}, u32[]{:S(2)}) collective-permute-start(bf16[512,128]{1,0:T(8,128)(2,1)} %get-tuple-element.20), channel_id=1, source_target_pairs={{0,2},{1,3},{2,0},{3,1},{16,18},{17,19},{18,16},{19,17},{4,6},{5,7... | collective-permute-start | bytes 393224 | tf_op jit(solution)/shard_map/ppermute | solution.py:367
  102.2 2.3 %collective-permute-start.6 = (bf16[512,128]{1,0:T(8,128)(2,1)}, bf16[512,128]{1,0:T(8,128)(2,1)S(1)}, u32[]{:S(2)}, u32[]{:S(2)}) collective-permute-start(bf16[512,128]{1,0:T(8,128)(2,1)} %get-tuple-element.21), channel_id=1, source_target_pairs={{0,3},{1,2},{2,1},{3,0},{16,19},{17,18},{18,17},{19,16},{4,7},{5,6... | collective-permute-start | bytes 393224 | tf_op jit(solution)/shard_map/ppermute | solution.py:367
  104.6 1.9 %collective-permute-start.7 = (bf16[512,128]{1,0:T(8,128)(2,1)}, bf16[512,128]{1,0:T(8,128)(2,1)S(1)}, u32[]{:S(2)}, u32[]{:S(2)}) collective-permute-start(bf16[512,128]{1,0:T(8,128)(2,1)} %get-tuple-element.22), channel_id=1, source_target_pairs={{0,16},{1,17},{2,18},{3,19},{16,0},{17,1},{18,2},{19,3},{4,20},{5,... | collective-permute-start | bytes 393224 | tf_op jit(solution)/shard_map/ppermute | solution.py:367
  106.5 3.9 %collective-permute-start.8 = (bf16[512,128]{1,0:T(8,128)(2,1)}, bf16[512,128]{1,0:T(8,128)(2,1)S(1)}, u32[]{:S(2)}, u32[]{:S(2)}) collective-permute-start(bf16[512,128]{1,0:T(8,128)(2,1)} %get-tuple-element.23), channel_id=1, source_target_pairs={{0,17},{1,16},{2,19},{3,18},{16,1},{17,0},{18,3},{19,2},{4,21},{5,... | collective-permute-start | bytes 393224 | tf_op jit(solution)/shard_map/ppermute | solution.py:367
  110.4 0.0 all-to-all-done.1.got_ref
  110.4 0.1 shard_map.116
  110.6 0.0 collective-permute-done.4.refs_1_
  110.6 0.0 copy-done.9
  110.6 2.8 %collective-permute-start.9 = (bf16[512,128]{1,0:T(8,128)(2,1)S(1)}, bf16[512,128]{1,0:T(8,128)(2,1)S(1)}, u32[]{:S(2)}, u32[]{:S(2)}) collective-permute-start(bf16[512,128]{1,0:T(8,128)(2,1)S(1)} %copy-done.9), channel_id=1, source_target_pairs={{0,18},{1,19},{2,16},{3,17},{16,2},{17,3},{18,0},{19,1},{4,22},{5,... | collective-permute-start | bytes 393224 | tf_op jit(solution)/shard_map/ppermute | solution.py:367
  113.4 0.0 collective-permute-done.5.refs_2_
  113.4 0.0 copy-done.8
  113.4 3.4 %collective-permute-start.10 = (bf16[512,128]{1,0:T(8,128)(2,1)S(1)}, bf16[512,128]{1,0:T(8,128)(2,1)S(1)}, u32[]{:S(2)}, u32[]{:S(2)}) collective-permute-start(bf16[512,128]{1,0:T(8,128)(2,1)S(1)} %copy-done.8), channel_id=1, source_target_pairs={{0,19},{1,18},{2,17},{3,16},{16,3},{17,2},{18,1},{19,0},{4,23},{5,... | collective-permute-start | bytes 393224 | tf_op jit(solution)/shard_map/ppermute | solution.py:367
  116.9 15.0 %all-gather.1 = bf16[16,64,128]{2,1,0:T(8,128)(2,1)S(1)} all-gather(bf16[4,64,128]{2,1,0:T(8,128)(2,1)S(1)} %shard_map.116), channel_id=3, replica_groups=mesh['x'=4,'yh'=4,'yl'=2,'w'=4,'p'=2,'c'=2] {'w'}, dimensions={0}, use_global_device_ids=true | all-gather | bytes 327680 | tf_op jit(solution)/shard_map/all_gather | solution.py:369
  131.9 0.2 shard_map.117
  132.1 0.0 collective-permute-done.6.refs_3_
  132.1 7.9 %collective-permute-start.11 = (f32[64,128]{1,0:T(8,128)S(1)}, f32[64,128]{1,0:T(8,128)S(1)}, u32[]{:S(2)}, u32[]{:S(2)}) collective-permute-start(f32[64,128]{1,0:T(8,128)S(1)} %shard_map.117), channel_id=1, source_target_pairs={{0,0},{1,8},{2,4},{3,12},{4,1},{5,9},{6,5},{7,13},{8,16},{9,24},{1... | collective-permute-start | bytes 98312 | tf_op jit(solution)/shard_map/ppermute | solution.py:370
  140.0 0.0 collective-permute-done.7.refs_4_
  140.0 0.0 collective-permute-done.8.refs_5_
  140.0 0.0 collective-permute-done.9.refs_6_
  140.0 0.0 collective-permute-done.10.refs_7_
  140.0 0.0 copy-done.1
  140.0 0.0 copy-done.2
  140.0 1.8 %shard_map.114 = (bf16[1,128,2048]{2,1,0:T(8,128)(2,1)}, bf16[1,128,1024]{2,1,0:T(8,128)(2,1)}, bf16[1,128,1024]{2,1,0:T(8,128)(2,1)}) custom-call(s32[3]{0:T(128)S(1)} %copy-done.2, bf16[512,128]{1,0:T(8,128)(2,1)S(1)} %copy-done.1, bf16[512,128]{1,0:T(8,128)(2,1)S(1)} %collective-permute-done.4.refs_1_, ...), custom_call_target="tpu_custom_call" | custom-call | bytes 2097152 | tf_op jit(solution)/shard_map/pallas_call | solution.py:340
  141.8 0.0 collective-permute-done.11
  141.8 0.6 copy.13
  (1 shorter events, 0.0 us)
Async XLA Ops:
  7.2 14.6 %copy-start = (bf16[128,2048]{1,0:T(8,128)(2,1)S(1)}, bf16[128,2048]{1,0:T(8,128)(2,1)}, u32[]{:S(2)}) copy-start(bf16[128,2048]{1,0:T(8,128)(2,1)} %param.12) | copy-start | bytes 1572868
  7.2 61.9 %all-gather.4.cloned.1.call-start = ((), (), s32[]{:S(2)}) async-start(), calls=%async_computation.2 | async-start | bytes 4718592 | tf_op jit(solution)/shard_map/all_gather | solution.py:355
  11.4 47.1 %all-to-all-start = ((bf16[8,528,128]{2,1,0:T(8,128)(2,1)}), bf16[8,528,128]{2,1,0:T(8,128)(2,1)S(1)}, u32[]{:S(2)}, u32[]{:S(2)}) async-start(bf16[8,528,128]{2,1,0:T(8,128)(2,1)} %bitcast.9), calls=%async_computation | async-start | bytes 2162688 | tf_op jit(solution)/shard_map/all_to_all | solution.py:357
  21.8 27.6 %collective-permute-start = (bf16[64,2048]{1,0:T(8,128)(2,1)S(1)}, bf16[64,2048]{1,0:T(8,128)(2,1)S(1)}, u32[]{:S(2)}, u32[]{:S(2)}) collective-permute-start(bf16[64,2048]{1,0:T(8,128)(2,1)S(1)} %constant_dynamic-slice_fusion), channel_id=1, source_target_pairs={{0,0},{8,1},{4,2},{12,3},{16,4},{24,5},{20,6},{28,7},{256,8},{264,... | collective-permute-start | bytes 786440 | tf_op jit(solution)/shard_map/ppermute | solution.py:354
  49.3 15.5 %copy-start.7 = (bf16[64,2048]{1,0:T(8,128)(2,1)}, bf16[64,2048]{1,0:T(8,128)(2,1)S(1)}, u32[]{:S(2)}) copy-start(bf16[64,2048]{1,0:T(8,128)(2,1)S(1)} %collective-permute-done.w0_ref) | copy-start | bytes 786436
  49.4 15.5 %collective-permute-start.3 = (bf16[64,2048]{1,0:T(8,128)(2,1)S(1)}, bf16[64,2048]{1,0:T(8,128)(2,1)S(1)}, u32[]{:S(2)}, u32[]{:S(2)}) collective-permute-start(bf16[64,2048]{1,0:T(8,128)(2,1)S(1)} %collective-permute-done.w0_ref), channel_id=1, source_target_pairs={{0,384},{128,0},{256,128},{384,256},{1,385},{129,1},{257,129},{385... | collective-permute-start | bytes 786440 | tf_op jit(solution)/shard_map/ppermute | solution.py:360
  54.1 11.4 %collective-permute-start.2 = (bf16[64,2048]{1,0:T(8,128)(2,1)S(1)}, bf16[64,2048]{1,0:T(8,128)(2,1)S(1)}, u32[]{:S(2)}, u32[]{:S(2)}) collective-permute-start(bf16[64,2048]{1,0:T(8,128)(2,1)S(1)} %collective-permute-done.w0_ref), channel_id=1, source_target_pairs={{0,256},{128,384},{256,0},{384,128},{1,257},{129,385},{257,1},{385... | collective-permute-start | bytes 786440 | tf_op jit(solution)/shard_map/ppermute | solution.py:360
  56.1 13.0 %collective-permute-start.1 = (bf16[64,2048]{1,0:T(8,128)(2,1)S(1)}, bf16[64,2048]{1,0:T(8,128)(2,1)S(1)}, u32[]{:S(2)}, u32[]{:S(2)}) collective-permute-start(bf16[64,2048]{1,0:T(8,128)(2,1)S(1)} %collective-permute-done.w0_ref), channel_id=1, source_target_pairs={{0,128},{128,256},{256,384},{384,0},{1,129},{129,257},{257,385},{3... | collective-permute-start | bytes 786440 | tf_op jit(solution)/shard_map/ppermute | solution.py:360
  58.6 1.0 copy-start.3
  64.8 4.2 %copy-start.4 = (bf16[64,2048]{1,0:T(8,128)(2,1)}, bf16[64,2048]{1,0:T(8,128)(2,1)S(1)}, u32[]{:S(2)}) copy-start(bf16[64,2048]{1,0:T(8,128)(2,1)S(1)} %collective-permute-done.3.w3_ref.c_ref) | copy-start | bytes 786436
  65.5 3.5 %copy-start.5 = (bf16[64,2048]{1,0:T(8,128)(2,1)}, bf16[64,2048]{1,0:T(8,128)(2,1)S(1)}, u32[]{:S(2)}) copy-start(bf16[64,2048]{1,0:T(8,128)(2,1)S(1)} %collective-permute-done.2.w2_ref.b_ref) | copy-start | bytes 786436
  69.1 0.7 copy-start.6
  73.8 36.6 %all-to-all-start.1 = ((bf16[16,4,64,128]{3,2,1,0:T(8,128)(2,1)}), bf16[16,4,64,128]{3,2,1,0:T(8,128)(2,1)S(1)}, u32[]{:S(2)}, u32[]{:S(2)}) async-start(bf16[16,4,64,128]{3,2,1,0:T(8,128)(2,1)} %shard_map.115), calls=%async_computation.1 | async-start | bytes 2097152 | tf_op jit(solution)/shard_map/all_to_all | solution.py:363
  91.7 18.9 %copy-start.9 = (bf16[512,128]{1,0:T(8,128)(2,1)S(1)}, bf16[512,128]{1,0:T(8,128)(2,1)}, u32[]{:S(2)}) copy-start(bf16[512,128]{1,0:T(8,128)(2,1)} %get-tuple-element.24) | copy-start | bytes 393220
  91.7 21.7 %copy-start.8 = (bf16[512,128]{1,0:T(8,128)(2,1)S(1)}, bf16[512,128]{1,0:T(8,128)(2,1)}, u32[]{:S(2)}) copy-start(bf16[512,128]{1,0:T(8,128)(2,1)} %get-tuple-element.25) | copy-start | bytes 393220
  91.7 48.3 %copy-start.1 = (bf16[512,128]{1,0:T(8,128)(2,1)S(1)}, bf16[512,128]{1,0:T(8,128)(2,1)}, u32[]{:S(2)}) copy-start(bf16[512,128]{1,0:T(8,128)(2,1)} %get-tuple-element.18.refs_0_) | copy-start | bytes 393220
  91.7 48.3 %copy-start.2 = (s32[3]{0:T(128)S(1)}, s32[3]{0:T(128)}, u32[]{:S(2)}) copy-start(s32[3]{0:T(128)} %pad_add_fusion.me_ref) | copy-start | bytes 40
  91.7 18.9 %collective-permute-start.4 = (bf16[512,128]{1,0:T(8,128)(2,1)}, bf16[512,128]{1,0:T(8,128)(2,1)S(1)}, u32[]{:S(2)}, u32[]{:S(2)}) collective-permute-start(bf16[512,128]{1,0:T(8,128)(2,1)} %get-tuple-element.19), channel_id=1, source_target_pairs={{0,1},{1,0},{2,3},{3,2},{16,17},{17,16},{18,19},{19,18},{4,5},{5,4... | collective-permute-start | bytes 393224 | tf_op jit(solution)/shard_map/ppermute | solution.py:367
  93.8 19.7 %collective-permute-start.5 = (bf16[512,128]{1,0:T(8,128)(2,1)}, bf16[512,128]{1,0:T(8,128)(2,1)S(1)}, u32[]{:S(2)}, u32[]{:S(2)}) collective-permute-start(bf16[512,128]{1,0:T(8,128)(2,1)} %get-tuple-element.20), channel_id=1, source_target_pairs={{0,2},{1,3},{2,0},{3,1},{16,18},{17,19},{18,16},{19,17},{4,6},{5,7... | collective-permute-start | bytes 393224 | tf_op jit(solution)/shard_map/ppermute | solution.py:367
  102.2 29.8 %collective-permute-start.6 = (bf16[512,128]{1,0:T(8,128)(2,1)}, bf16[512,128]{1,0:T(8,128)(2,1)S(1)}, u32[]{:S(2)}, u32[]{:S(2)}) collective-permute-start(bf16[512,128]{1,0:T(8,128)(2,1)} %get-tuple-element.21), channel_id=1, source_target_pairs={{0,3},{1,2},{2,1},{3,0},{16,19},{17,18},{18,17},{19,16},{4,7},{5,6... | collective-permute-start | bytes 393224 | tf_op jit(solution)/shard_map/ppermute | solution.py:367
  104.6 35.4 %collective-permute-start.7 = (bf16[512,128]{1,0:T(8,128)(2,1)}, bf16[512,128]{1,0:T(8,128)(2,1)S(1)}, u32[]{:S(2)}, u32[]{:S(2)}) collective-permute-start(bf16[512,128]{1,0:T(8,128)(2,1)} %get-tuple-element.22), channel_id=1, source_target_pairs={{0,16},{1,17},{2,18},{3,19},{16,0},{17,1},{18,2},{19,3},{4,20},{5,... | collective-permute-start | bytes 393224 | tf_op jit(solution)/shard_map/ppermute | solution.py:367
  106.5 33.5 %collective-permute-start.8 = (bf16[512,128]{1,0:T(8,128)(2,1)}, bf16[512,128]{1,0:T(8,128)(2,1)S(1)}, u32[]{:S(2)}, u32[]{:S(2)}) collective-permute-start(bf16[512,128]{1,0:T(8,128)(2,1)} %get-tuple-element.23), channel_id=1, source_target_pairs={{0,17},{1,16},{2,19},{3,18},{16,1},{17,0},{18,3},{19,2},{4,21},{5,... | collective-permute-start | bytes 393224 | tf_op jit(solution)/shard_map/ppermute | solution.py:367
  110.6 29.4 %collective-permute-start.9 = (bf16[512,128]{1,0:T(8,128)(2,1)S(1)}, bf16[512,128]{1,0:T(8,128)(2,1)S(1)}, u32[]{:S(2)}, u32[]{:S(2)}) collective-permute-start(bf16[512,128]{1,0:T(8,128)(2,1)S(1)} %copy-done.9), channel_id=1, source_target_pairs={{0,18},{1,19},{2,16},{3,17},{16,2},{17,3},{18,0},{19,1},{4,22},{5,... | collective-permute-start | bytes 393224 | tf_op jit(solution)/shard_map/ppermute | solution.py:367
  113.4 26.6 %collective-permute-start.10 = (bf16[512,128]{1,0:T(8,128)(2,1)S(1)}, bf16[512,128]{1,0:T(8,128)(2,1)S(1)}, u32[]{:S(2)}, u32[]{:S(2)}) collective-permute-start(bf16[512,128]{1,0:T(8,128)(2,1)S(1)} %copy-done.8), channel_id=1, source_target_pairs={{0,19},{1,18},{2,17},{3,16},{16,3},{17,2},{18,1},{19,0},{4,23},{5,... | collective-permute-start | bytes 393224 | tf_op jit(solution)/shard_map/ppermute | solution.py:367
  132.1 9.7 %collective-permute-start.11 = (f32[64,128]{1,0:T(8,128)S(1)}, f32[64,128]{1,0:T(8,128)S(1)}, u32[]{:S(2)}, u32[]{:S(2)}) collective-permute-start(f32[64,128]{1,0:T(8,128)S(1)} %shard_map.117), channel_id=1, source_target_pairs={{0,0},{1,8},{2,4},{3,12},{4,1},{5,9},{6,5},{7,13},{8,16},{9,24},{1... | collective-permute-start | bytes 98312 | tf_op jit(solution)/shard_map/ppermute | solution.py:370
Sparse Core Ops, SparseCore 0:
  10.2 52.3 all-gather.3

commit v10 on v9

--- a/solution.py
+++ b/solution.py
@@ -17,7 +17,7 @@
 AXES = ("x", "yh", "yl", "w", "p", "c")
 SIZES = (4, 4, 2, 4, 2, 2)
 NEAR = ("yl", "p", "c")
-FAR = ("x", "yh")
+FAR = ("x", "yh", "w")
 CODE = 16
 PAY = 4 * TOK + CODE
 NONE = 99
@@ -132,8 +132,8 @@
         for m in range(8):
             upper = total[b * HD : b * HD + 64, m * HD : (m + 1) * HD]
             lower = total[b * HD + 64 : (b + 1) * HD, m * HD : (m + 1) * HD]
-            wg_ref[m, b] = jnp.where(left, upper, pltpu.roll(lower, 64, 1)).astype(BF16)
-            wg_ref[m, 2 + b] = jnp.where(left, pltpu.roll(upper, 64, 1), lower).astype(BF16)
+            wg_ref[4 * m + b] = jnp.where(left, upper, pltpu.roll(lower, 64, 1)).astype(BF16)
+            wg_ref[4 * m + 2 + b] = jnp.where(left, pltpu.roll(upper, 64, 1), lower).astype(BF16)
 
 
 def backward_kernel(me_ref, pay_ref, lse_ref, cot_ref, w0_ref, w1_ref, w2_ref, w3_ref, *refs):
@@ -198,12 +198,8 @@
         dv_ref[0, :, near] = got_ref[3 * TOK : 4 * TOK, :]
 
 
-def near_sum_kernel(got_ref, out_ref):
-    out_ref[...] = jnp.sum(got_ref[...].astype(F32), axis=0).astype(BF16)
-
-
-def far_sum_kernel(w_ref, got_ref, out_ref):
-    total = jnp.sum(got_ref[:, w_ref[0]].astype(F32), axis=0)
+def sum_kernel(got_ref, out_ref):
+    total = jnp.sum(got_ref[...].astype(F32), axis=0)
     out_ref[:, 0:64] = total[:, 0:64].T
     out_ref[:, 64:128] = total[:, 64:128].T
 
@@ -270,7 +266,7 @@
 def run_weight(out, cot, after):
     return call(
         weight_kernel,
-        shape((16, 4, 64, HD)),
+        shape((64, 64, HD)),
         flops=1 << 30,
         bytes_accessed=6 << 20,
         grid=(2,),
@@ -279,7 +275,7 @@
             pl.BlockSpec((2 * WINDOW, 1024), lambda i: (0, i)),
         ]
         + [pl.BlockSpec(memory_space=pl.ANY)] * 3,
-        out_specs=pl.BlockSpec((8, 4, 64, HD), lambda i: (i, 0, 0, 0)),
+        out_specs=pl.BlockSpec((32, 64, HD), lambda i: (i, 0, 0)),
     )(out, cot, *after)
 
 
@@ -314,26 +310,15 @@
     )(me, arrived, lse, cot, *quarters)
 
 
-def run_near_sum(got):
-    return call(
-        near_sum_kernel,
-        shape(got.shape[1:]),
+def run_sum(got):
+    return call(
+        sum_kernel,
+        shape((64, HD), F32),
         room=16,
         bytes_accessed=1 << 20,
         in_specs=[VMEM],
         out_specs=VMEM,
     )(got)
-
-
-def run_far_sum(w, got):
-    return call(
-        far_sum_kernel,
-        shape((64, HD), F32),
-        room=16,
-        bytes_accessed=1 << 18,
-        in_specs=[SMEM, VMEM],
-        out_specs=VMEM,
-    )(w, got)
 
 
 def run_unpack(me, home, query_shape, key_shape):
@@ -349,7 +334,6 @@
 
 def local(queries, keys, values, cotangent, out_weight, segment, row_type, pair_index):
     x = lax.axis_index("x").astype(jnp.int32)
-    w = lax.axis_index("w").astype(jnp.int32).reshape(1)
     share = lax.dynamic_slice_in_dim(out_weight, 64 * lax.rem(x, 2), 64, axis=0)
     quarter = lax.ppermute(share, AXES, weight_moves())
     cot = lax.all_gather(cotangent[0], NEAR, axis=0, tiled=True)
@@ -366,8 +350,7 @@
     home = [own] + [
         lax.ppermute(other, NEAR, [(i, i ^ (k + 1)) for i in range(8)]) for k, other in enumerate(others)
     ]
-    windows = lax.all_gather(run_near_sum(got), "w", axis=0)
-    weight_grad = lax.ppermute(run_far_sum(w, windows), AXES, piece_moves()).T
+    weight_grad = lax.ppermute(run_sum(got), AXES, piece_moves()).T
     query_grad, key_grad, value_grad = run_unpack(me, home, queries.shape, keys.shape)
     return query_grad, key_grad, value_grad, weight_grad
 

time: 152 us -> 141 us (0.928)
  blocking collectives: 15 us -> 0 us
  starting transfers between devices: 62 us -> 67.4 us
    all_gather x1 -> x0, blocking collectives: 15 us -> none  [local(): windows = lax.all_gather(run_near_sum(got), 'w', axis=0)]
    all_to_all x1, starting transfers between devices: 5.76 us -> 14.3 us  [local(): got = lax.all_to_all(pieces, FAR, 0, 0)]
    ppermute x7, starting transfers between devices: 24.9 us -> 22.5 us  [local(): lax.ppermute(other, NEAR, [(i, i ^ k + 1) for i in range(8)])]
    pallas_call x3 -> x2, Pallas kernels: 4.41 us -> 4.44 us  [the longest x1 4.08 us: run_weight(): call(weight_kernel, shape((64, 64, HD)), flops=1 << 30, bytes_accessed=6...]
  transfers between devices with their start and end apart: 15 -> 15, of which waited for: 3 -> 3; matrix products, arithmetic and copies ran while one was open for 0% -> 0% of each run, Pallas kernels for 15% -> 16%
where the time goes in v10:
time: 141 us; the launch traced here: 140 us
  starting transfers between devices  67.4 us (48%)
  waiting for transfers between devices  28.5 us (20%)
  Pallas kernels  26.5 us (19%)
  between operations  14.3 us (10%)
  local copies, waits for them, and re-layouts  2.37 us (2%)
    ppermute x1, waiting for transfers between devices, local(): quarter = lax.ppermute(share, AXES, weight_moves())  23.6 us
    ppermute x7, starting transfers between devices, local(): lax.ppermute(other, NEAR, [(i, i ^ k + 1) for i in range(8)])  22.5 us
    all_to_all x1, starting transfers between devices, local(): got = lax.all_to_all(pieces, FAR, 0, 0)  14.3 us
    pallas_call x1, Pallas kernels, run_backward(): call(backward_kernel, (shape((4 * TOK, HD)),) * 8, flops=8 << 30, bytes_a...  11.4 us
    all_to_all x1, starting transfers between devices, local(): arrived = lax.all_to_all(payload, NEAR, 0, 0)  10.3 us
    ppermute x3, starting transfers between devices, local(): lax.ppermute(quarter, 'x', [(i, (i + turn) % 4) for i in range(4)])  9.17 us
    ppermute x1, starting transfers between devices, local(): weight_grad = lax.ppermute(run_sum(got), AXES, piece_moves()).T  7.1 us
    pallas_call x1, Pallas kernels, run_forward(): call(forward_kernel, (shape((2 * HD, 2 * WINDOW)), shape((2 * WINDOW, HD)...  5.25 us
  transfers between devices with their start and end apart: 15, of which 3 were waited for; matrix products, arithmetic and copies ran while one was open for 0% of the time, Pallas kernels for 16%

profile of v10, /device:TPU:1, one launch (start us, length us, event | category | flops | bytes accessed | tf_op | source)
XLA Modules:
  0.0 139.7 jit_solution(5128428419635906213)
XLA Ops:
  7.2 0.0 copy-start
  7.2 0.0 all-gather.3.cloned.1.call-start
  7.2 0.7 all-gather.3.cloned.1.call-update
  7.9 3.5 %shard_map.111 = bf16[2,4,528,128]{3,2,1,0:T(8,128)(2,1)} custom-call(bf16[1,128,2048]{2,1,0:T(8,128)(2,1)} %q_ref.1, bf16[1,128,1024]{2,1,0:T(8,128)(2,1)} %k_ref.1, bf16[1,128,1024]{2,1,0:T(8,128)(2,1)} %v_ref.1, s32[1,128]{1,0:T(1,128)} %seg_ref.1, s32[1,128]{1,0:T(1,128)} %type_ref.1, s32[1,24]{1,0:T(1,128)} %pair_ref.1), custom_call_target="tpu_custom_call" | custom-call | bytes 2097152 | tf_op jit(solution)/shard_map/pallas_call | solution.py:234
  11.4 10.3 %all-to-all-start = ((bf16[8,528,128]{2,1,0:T(8,128)(2,1)}), bf16[8,528,128]{2,1,0:T(8,128)(2,1)S(1)}, u32[]{:S(2)}, u32[]{:S(2)}) async-start(bf16[8,528,128]{2,1,0:T(8,128)(2,1)} %bitcast.6), calls=%async_computation | async-start | bytes 2162688 | tf_op jit(solution)/shard_map/all_to_all | solution.py:341
  21.8 0.0 copy-done
  21.8 4.0 %collective-permute-start = (bf16[64,2048]{1,0:T(8,128)(2,1)S(1)}, bf16[64,2048]{1,0:T(8,128)(2,1)S(1)}, u32[]{:S(2)}, u32[]{:S(2)}) collective-permute-start(bf16[64,2048]{1,0:T(8,128)(2,1)S(1)} %constant_dynamic-slice_fusion), channel_id=1, source_target_pairs={{0,0},{8,1},{4,2},{12,3},{16,4},{24,5},{20,6},{28,7},{256,8},{264,... | collective-permute-start | bytes 786440 | tf_op jit(solution)/shard_map/ppermute | solution.py:338
  25.8 23.6 %collective-permute-done.w0_ref = bf16[64,2048]{1,0:T(8,128)(2,1)S(1)} collective-permute-done((bf16[64,2048]{1,0:T(8,128)(2,1)S(1)}, bf16[64,2048]{1,0:T(8,128)(2,1)S(1)}, u32[]{:S(2)}, u32[]{:S(2)}) %collective-permute-start) | collective-permute-done | bytes 262176 | tf_op jit(solution)/shard_map/ppermute | solution.py:338
  49.4 0.0 copy-start.7
  49.4 4.8 %collective-permute-start.3 = (bf16[64,2048]{1,0:T(8,128)(2,1)S(1)}, bf16[64,2048]{1,0:T(8,128)(2,1)S(1)}, u32[]{:S(2)}, u32[]{:S(2)}) collective-permute-start(bf16[64,2048]{1,0:T(8,128)(2,1)S(1)} %collective-permute-done.w0_ref), channel_id=1, source_target_pairs={{0,384},{128,0},{256,128},{384,256},{1,385},{129,1},{257,129},{385... | collective-permute-start | bytes 786440 | tf_op jit(solution)/shard_map/ppermute | solution.py:344
  54.2 1.9 %collective-permute-start.2 = (bf16[64,2048]{1,0:T(8,128)(2,1)S(1)}, bf16[64,2048]{1,0:T(8,128)(2,1)S(1)}, u32[]{:S(2)}, u32[]{:S(2)}) collective-permute-start(bf16[64,2048]{1,0:T(8,128)(2,1)S(1)} %collective-permute-done.w0_ref), channel_id=1, source_target_pairs={{0,256},{128,384},{256,0},{384,128},{1,257},{129,385},{257,1},{385... | collective-permute-start | bytes 786440 | tf_op jit(solution)/shard_map/ppermute | solution.py:344
  56.1 2.5 %collective-permute-start.1 = (bf16[64,2048]{1,0:T(8,128)(2,1)S(1)}, bf16[64,2048]{1,0:T(8,128)(2,1)S(1)}, u32[]{:S(2)}, u32[]{:S(2)}) collective-permute-start(bf16[64,2048]{1,0:T(8,128)(2,1)S(1)} %collective-permute-done.w0_ref), channel_id=1, source_target_pairs={{0,128},{128,256},{256,384},{384,0},{1,129},{129,257},{257,385},{3... | collective-permute-start | bytes 786440 | tf_op jit(solution)/shard_map/ppermute | solution.py:344
  58.6 0.0 all-to-all-done.pay_ref
  58.6 0.0 copy-start.3
  58.6 1.0 copy-done.3
  59.6 5.3 %shard_map.112 = (bf16[256,1024]{1,0:T(8,128)(2,1)}, f32[1024,128]{1,0:T(8,128)}) custom-call(bf16[8,528,128]{2,1,0:T(8,128)(2,1)} %copy-done.3), custom_call_target="tpu_custom_call" | custom-call | flops 4294967296 | bytes 2097152 | tf_op jit(solution)/shard_map/pallas_call | solution.py:252
  64.9 0.0 copy-done.7
  64.9 0.0 collective-permute-done.3.w3_ref.c_ref
  64.9 0.0 copy-start.4
  64.9 0.7 collective-permute-done.2.w2_ref.b_ref
  65.6 0.0 copy-start.5
  65.6 3.5 %collective-permute-done.1.w1_ref.a_ref = bf16[64,2048]{1,0:T(8,128)(2,1)S(1)} collective-permute-done((bf16[64,2048]{1,0:T(8,128)(2,1)S(1)}, bf16[64,2048]{1,0:T(8,128)(2,1)S(1)}, u32[]{:S(2)}, u32[]{:S(2)}) %collective-permute-start.1) | collective-permute-done | bytes 262176 | tf_op jit(solution)/shard_map/ppermute | solution.py:344
  69.1 0.0 copy-start.6
  69.1 0.0 all-gather.3.cloned.1.call-done
  69.1 0.0 copy-done.4
  69.1 0.0 copy-done.5
  69.1 0.7 copy-done.6
  69.8 4.1 %shard_map.115 = bf16[64,64,128]{2,1,0:T(8,128)(2,1)} custom-call(bf16[256,1024]{1,0:T(8,128)(2,1)} %get-tuple-element.29.out_ref, bf16[1024,2048]{1,0:T(8,128)(2,1)} %bitcast.7, bf16[64,2048]{1,0:T(8,128)(2,1)} %copy-done.6, bf16[64,2048]{1,0:T(8,128)(2,1)} %copy-done.5, bf16[64,2048]{1,0:T(8,128)(2,1)} %copy-done.4), custom_call_target="tpu_custom_call" | custom-call | flops 1073741824 | bytes 6291456 | tf_op jit(solution)/shard_map/pallas_call | solution.py:267
  73.9 14.3 %all-to-all-start.1 = ((bf16[64,64,128]{2,1,0:T(8,128)(2,1)}), bf16[64,64,128]{2,1,0:T(8,128)(2,1)S(1)}, u32[]{:S(2)}, u32[]{:S(2)}) async-start(bf16[64,64,128]{2,1,0:T(8,128)(2,1)} %shard_map.115), calls=%async_computation.1 | async-start | bytes 2097152 | tf_op jit(solution)/shard_map/all_to_all | solution.py:347
  88.2 0.6 pad_add_fusion.me_ref
  88.8 11.4 %shard_map.113 = (bf16[512,128]{1,0:T(8,128)(2,1)}, bf16[512,128]{1,0:T(8,128)(2,1)}, bf16[512,128]{1,0:T(8,128)(2,1)}, bf16[512,128]{1,0:T(8,128)(2,1)}, bf16[5...) custom-call(s32[3]{0:T(128)} %pad_add_fusion.me_ref, ...), custom_call_target="tpu_custom_call" | custom-call | flops 8589934592 | bytes 7340032 | tf_op jit(solution)/shard_map/pallas_call | solution.py:304
  100.3 0.0 copy-start.1
  100.3 0.0 copy-start.2
  100.3 2.7 %collective-permute-start.4 = (bf16[512,128]{1,0:T(8,128)(2,1)}, bf16[512,128]{1,0:T(8,128)(2,1)S(1)}, u32[]{:S(2)}, u32[]{:S(2)}) collective-permute-start(bf16[512,128]{1,0:T(8,128)(2,1)} %get-tuple-element.19), channel_id=1, source_target_pairs={{0,1},{1,0},{2,3},{3,2},{16,17},{17,16},{18,19},{19,18},{4,5},{5,4... | collective-permute-start | bytes 393224 | tf_op jit(solution)/shard_map/ppermute | solution.py:351
  103.0 3.0 %collective-permute-start.5 = (bf16[512,128]{1,0:T(8,128)(2,1)}, bf16[512,128]{1,0:T(8,128)(2,1)S(1)}, u32[]{:S(2)}, u32[]{:S(2)}) collective-permute-start(bf16[512,128]{1,0:T(8,128)(2,1)} %get-tuple-element.20), channel_id=1, source_target_pairs={{0,2},{1,3},{2,0},{3,1},{16,18},{17,19},{18,16},{19,17},{4,6},{5,7... | collective-permute-start | bytes 393224 | tf_op jit(solution)/shard_map/ppermute | solution.py:351
  106.0 2.4 %collective-permute-start.6 = (bf16[512,128]{1,0:T(8,128)(2,1)}, bf16[512,128]{1,0:T(8,128)(2,1)S(1)}, u32[]{:S(2)}, u32[]{:S(2)}) collective-permute-start(bf16[512,128]{1,0:T(8,128)(2,1)} %get-tuple-element.21), channel_id=1, source_target_pairs={{0,3},{1,2},{2,1},{3,0},{16,19},{17,18},{18,17},{19,16},{4,7},{5,6... | collective-permute-start | bytes 393224 | tf_op jit(solution)/shard_map/ppermute | solution.py:351
  108.5 5.4 %collective-permute-start.7 = (bf16[512,128]{1,0:T(8,128)(2,1)}, bf16[512,128]{1,0:T(8,128)(2,1)S(1)}, u32[]{:S(2)}, u32[]{:S(2)}) collective-permute-start(bf16[512,128]{1,0:T(8,128)(2,1)} %get-tuple-element.22), channel_id=1, source_target_pairs={{0,16},{1,17},{2,18},{3,19},{16,0},{17,1},{18,2},{19,3},{4,20},{5,... | collective-permute-start | bytes 393224 | tf_op jit(solution)/shard_map/ppermute | solution.py:351
  113.8 2.2 %collective-permute-start.8 = (bf16[512,128]{1,0:T(8,128)(2,1)}, bf16[512,128]{1,0:T(8,128)(2,1)S(1)}, u32[]{:S(2)}, u32[]{:S(2)}) collective-permute-start(bf16[512,128]{1,0:T(8,128)(2,1)} %get-tuple-element.23), channel_id=1, source_target_pairs={{0,17},{1,16},{2,19},{3,18},{16,1},{17,0},{18,3},{19,2},{4,21},{5,... | collective-permute-start | bytes 393224 | tf_op jit(solution)/shard_map/ppermute | solution.py:351
  116.0 0.0 collective-permute-done.4.refs_1_
  116.0 4.4 %collective-permute-start.9 = (bf16[512,128]{1,0:T(8,128)(2,1)}, bf16[512,128]{1,0:T(8,128)(2,1)S(1)}, u32[]{:S(2)}, u32[]{:S(2)}) collective-permute-start(bf16[512,128]{1,0:T(8,128)(2,1)} %get-tuple-element.24), channel_id=1, source_target_pairs={{0,18},{1,19},{2,16},{3,17},{16,2},{17,3},{18,0},{19,1},{4,22},{5,... | collective-permute-start | bytes 393224 | tf_op jit(solution)/shard_map/ppermute | solution.py:351
  120.5 0.0 collective-permute-done.5.refs_2_
  120.5 2.3 %collective-permute-start.10 = (bf16[512,128]{1,0:T(8,128)(2,1)}, bf16[512,128]{1,0:T(8,128)(2,1)S(1)}, u32[]{:S(2)}, u32[]{:S(2)}) collective-permute-start(bf16[512,128]{1,0:T(8,128)(2,1)} %get-tuple-element.25), channel_id=1, source_target_pairs={{0,19},{1,18},{2,17},{3,16},{16,3},{17,2},{18,1},{19,0},{4,23},{5,... | collective-permute-start | bytes 393224 | tf_op jit(solution)/shard_map/ppermute | solution.py:351
  122.8 0.0 all-to-all-done.1.got_ref
  122.8 0.4 shard_map.116
  123.2 0.0 collective-permute-done.6.refs_3_
  123.2 7.1 %collective-permute-start.11 = (f32[64,128]{1,0:T(8,128)S(1)}, f32[64,128]{1,0:T(8,128)S(1)}, u32[]{:S(2)}, u32[]{:S(2)}) collective-permute-start(f32[64,128]{1,0:T(8,128)S(1)} %shard_map.116), channel_id=1, source_target_pairs={{0,0},{1,8},{2,4},{3,12},{4,1},{5,9},{6,5},{7,13},{8,16},{9,24},{1... | collective-permute-start | bytes 98312 | tf_op jit(solution)/shard_map/ppermute | solution.py:353
  130.3 0.0 collective-permute-done.7.refs_4_
  130.3 0.0 collective-permute-done.8.refs_5_
  130.3 0.0 collective-permute-done.9.refs_6_
  130.3 0.0 collective-permute-done.10.refs_7_
  130.4 0.0 copy-done.1
  130.4 0.0 copy-done.2
  130.4 1.8 %shard_map.114 = (bf16[1,128,2048]{2,1,0:T(8,128)(2,1)}, bf16[1,128,1024]{2,1,0:T(8,128)(2,1)}, bf16[1,128,1024]{2,1,0:T(8,128)(2,1)}) custom-call(s32[3]{0:T(128)S(1)} %copy-done.2, bf16[512,128]{1,0:T(8,128)(2,1)S(1)} %copy-done.1, bf16[512,128]{1,0:T(8,128)(2,1)S(1)} %collective-permute-done.4.refs_1_, ...), custom_call_target="tpu_custom_call" | custom-call | bytes 2097152 | tf_op jit(solution)/shard_map/pallas_call | solution.py:325
  132.2 0.0 collective-permute-done.11
  132.2 0.6 copy.13
  (1 shorter events, 0.0 us)
Async XLA Ops:
  7.2 14.6 %copy-start = (bf16[128,2048]{1,0:T(8,128)(2,1)S(1)}, bf16[128,2048]{1,0:T(8,128)(2,1)}, u32[]{:S(2)}) copy-start(bf16[128,2048]{1,0:T(8,128)(2,1)} %param.12) | copy-start | bytes 1572868
  7.2 61.9 %all-gather.3.cloned.1.call-start = ((), (), s32[]{:S(2)}) async-start(), calls=%async_computation.2 | async-start | bytes 4718592 | tf_op jit(solution)/shard_map/all_gather | solution.py:339
  11.4 47.2 %all-to-all-start = ((bf16[8,528,128]{2,1,0:T(8,128)(2,1)}), bf16[8,528,128]{2,1,0:T(8,128)(2,1)S(1)}, u32[]{:S(2)}, u32[]{:S(2)}) async-start(bf16[8,528,128]{2,1,0:T(8,128)(2,1)} %bitcast.6), calls=%async_computation | async-start | bytes 2162688 | tf_op jit(solution)/shard_map/all_to_all | solution.py:341
  21.8 27.6 %collective-permute-start = (bf16[64,2048]{1,0:T(8,128)(2,1)S(1)}, bf16[64,2048]{1,0:T(8,128)(2,1)S(1)}, u32[]{:S(2)}, u32[]{:S(2)}) collective-permute-start(bf16[64,2048]{1,0:T(8,128)(2,1)S(1)} %constant_dynamic-slice_fusion), channel_id=1, source_target_pairs={{0,0},{8,1},{4,2},{12,3},{16,4},{24,5},{20,6},{28,7},{256,8},{264,... | collective-permute-start | bytes 786440 | tf_op jit(solution)/shard_map/ppermute | solution.py:338
  49.4 15.5 %copy-start.7 = (bf16[64,2048]{1,0:T(8,128)(2,1)}, bf16[64,2048]{1,0:T(8,128)(2,1)S(1)}, u32[]{:S(2)}) copy-start(bf16[64,2048]{1,0:T(8,128)(2,1)S(1)} %collective-permute-done.w0_ref) | copy-start | bytes 786436
  49.4 15.5 %collective-permute-start.3 = (bf16[64,2048]{1,0:T(8,128)(2,1)S(1)}, bf16[64,2048]{1,0:T(8,128)(2,1)S(1)}, u32[]{:S(2)}, u32[]{:S(2)}) collective-permute-start(bf16[64,2048]{1,0:T(8,128)(2,1)S(1)} %collective-permute-done.w0_ref), channel_id=1, source_target_pairs={{0,384},{128,0},{256,128},{384,256},{1,385},{129,1},{257,129},{385... | collective-permute-start | bytes 786440 | tf_op jit(solution)/shard_map/ppermute | solution.py:344
  54.2 11.4 %collective-permute-start.2 = (bf16[64,2048]{1,0:T(8,128)(2,1)S(1)}, bf16[64,2048]{1,0:T(8,128)(2,1)S(1)}, u32[]{:S(2)}, u32[]{:S(2)}) collective-permute-start(bf16[64,2048]{1,0:T(8,128)(2,1)S(1)} %collective-permute-done.w0_ref), channel_id=1, source_target_pairs={{0,256},{128,384},{256,0},{384,128},{1,257},{129,385},{257,1},{385... | collective-permute-start | bytes 786440 | tf_op jit(solution)/shard_map/ppermute | solution.py:344
  56.1 13.0 %collective-permute-start.1 = (bf16[64,2048]{1,0:T(8,128)(2,1)S(1)}, bf16[64,2048]{1,0:T(8,128)(2,1)S(1)}, u32[]{:S(2)}, u32[]{:S(2)}) collective-permute-start(bf16[64,2048]{1,0:T(8,128)(2,1)S(1)} %collective-permute-done.w0_ref), channel_id=1, source_target_pairs={{0,128},{128,256},{256,384},{384,0},{1,129},{129,257},{257,385},{3... | collective-permute-start | bytes 786440 | tf_op jit(solution)/shard_map/ppermute | solution.py:344
  58.6 1.0 copy-start.3
  64.9 4.2 %copy-start.4 = (bf16[64,2048]{1,0:T(8,128)(2,1)}, bf16[64,2048]{1,0:T(8,128)(2,1)S(1)}, u32[]{:S(2)}) copy-start(bf16[64,2048]{1,0:T(8,128)(2,1)S(1)} %collective-permute-done.3.w3_ref.c_ref) | copy-start | bytes 786436
  65.6 3.5 %copy-start.5 = (bf16[64,2048]{1,0:T(8,128)(2,1)}, bf16[64,2048]{1,0:T(8,128)(2,1)S(1)}, u32[]{:S(2)}) copy-start(bf16[64,2048]{1,0:T(8,128)(2,1)S(1)} %collective-permute-done.2.w2_ref.b_ref) | copy-start | bytes 786436
  69.1 0.7 copy-start.6
  73.9 48.9 %all-to-all-start.1 = ((bf16[64,64,128]{2,1,0:T(8,128)(2,1)}), bf16[64,64,128]{2,1,0:T(8,128)(2,1)S(1)}, u32[]{:S(2)}, u32[]{:S(2)}) async-start(bf16[64,64,128]{2,1,0:T(8,128)(2,1)} %shard_map.115), calls=%async_computation.1 | async-start | bytes 2097152 | tf_op jit(solution)/shard_map/all_to_all | solution.py:347
  100.3 30.1 %copy-start.1 = (bf16[512,128]{1,0:T(8,128)(2,1)S(1)}, bf16[512,128]{1,0:T(8,128)(2,1)}, u32[]{:S(2)}) copy-start(bf16[512,128]{1,0:T(8,128)(2,1)} %get-tuple-element.18.refs_0_) | copy-start | bytes 393220
  100.3 30.1 %copy-start.2 = (s32[3]{0:T(128)S(1)}, s32[3]{0:T(128)}, u32[]{:S(2)}) copy-start(s32[3]{0:T(128)} %pad_add_fusion.me_ref) | copy-start | bytes 40
  100.3 15.8 %collective-permute-start.4 = (bf16[512,128]{1,0:T(8,128)(2,1)}, bf16[512,128]{1,0:T(8,128)(2,1)S(1)}, u32[]{:S(2)}, u32[]{:S(2)}) collective-permute-start(bf16[512,128]{1,0:T(8,128)(2,1)} %get-tuple-element.19), channel_id=1, source_target_pairs={{0,1},{1,0},{2,3},{3,2},{16,17},{17,16},{18,19},{19,18},{4,5},{5,4... | collective-permute-start | bytes 393224 | tf_op jit(solution)/shard_map/ppermute | solution.py:351
  103.0 17.5 %collective-permute-start.5 = (bf16[512,128]{1,0:T(8,128)(2,1)}, bf16[512,128]{1,0:T(8,128)(2,1)S(1)}, u32[]{:S(2)}, u32[]{:S(2)}) collective-permute-start(bf16[512,128]{1,0:T(8,128)(2,1)} %get-tuple-element.20), channel_id=1, source_target_pairs={{0,2},{1,3},{2,0},{3,1},{16,18},{17,19},{18,16},{19,17},{4,6},{5,7... | collective-permute-start | bytes 393224 | tf_op jit(solution)/shard_map/ppermute | solution.py:351
  106.0 17.2 %collective-permute-start.6 = (bf16[512,128]{1,0:T(8,128)(2,1)}, bf16[512,128]{1,0:T(8,128)(2,1)S(1)}, u32[]{:S(2)}, u32[]{:S(2)}) collective-permute-start(bf16[512,128]{1,0:T(8,128)(2,1)} %get-tuple-element.21), channel_id=1, source_target_pairs={{0,3},{1,2},{2,1},{3,0},{16,19},{17,18},{18,17},{19,16},{4,7},{5,6... | collective-permute-start | bytes 393224 | tf_op jit(solution)/shard_map/ppermute | solution.py:351
  108.5 21.9 %collective-permute-start.7 = (bf16[512,128]{1,0:T(8,128)(2,1)}, bf16[512,128]{1,0:T(8,128)(2,1)S(1)}, u32[]{:S(2)}, u32[]{:S(2)}) collective-permute-start(bf16[512,128]{1,0:T(8,128)(2,1)} %get-tuple-element.22), channel_id=1, source_target_pairs={{0,16},{1,17},{2,18},{3,19},{16,0},{17,1},{18,2},{19,3},{4,20},{5,... | collective-permute-start | bytes 393224 | tf_op jit(solution)/shard_map/ppermute | solution.py:351
  113.8 16.5 %collective-permute-start.8 = (bf16[512,128]{1,0:T(8,128)(2,1)}, bf16[512,128]{1,0:T(8,128)(2,1)S(1)}, u32[]{:S(2)}, u32[]{:S(2)}) collective-permute-start(bf16[512,128]{1,0:T(8,128)(2,1)} %get-tuple-element.23), channel_id=1, source_target_pairs={{0,17},{1,16},{2,19},{3,18},{16,1},{17,0},{18,3},{19,2},{4,21},{5,... | collective-permute-start | bytes 393224 | tf_op jit(solution)/shard_map/ppermute | solution.py:351
  116.0 14.3 %collective-permute-start.9 = (bf16[512,128]{1,0:T(8,128)(2,1)}, bf16[512,128]{1,0:T(8,128)(2,1)S(1)}, u32[]{:S(2)}, u32[]{:S(2)}) collective-permute-start(bf16[512,128]{1,0:T(8,128)(2,1)} %get-tuple-element.24), channel_id=1, source_target_pairs={{0,18},{1,19},{2,16},{3,17},{16,2},{17,3},{18,0},{19,1},{4,22},{5,... | collective-permute-start | bytes 393224 | tf_op jit(solution)/shard_map/ppermute | solution.py:351
  120.5 9.9 %collective-permute-start.10 = (bf16[512,128]{1,0:T(8,128)(2,1)}, bf16[512,128]{1,0:T(8,128)(2,1)S(1)}, u32[]{:S(2)}, u32[]{:S(2)}) collective-permute-start(bf16[512,128]{1,0:T(8,128)(2,1)} %get-tuple-element.25), channel_id=1, source_target_pairs={{0,19},{1,18},{2,17},{3,16},{16,3},{17,2},{18,1},{19,0},{4,23},{5,... | collective-permute-start | bytes 393224 | tf_op jit(solution)/shard_map/ppermute | solution.py:351
  123.2 9.0 %collective-permute-start.11 = (f32[64,128]{1,0:T(8,128)S(1)}, f32[64,128]{1,0:T(8,128)S(1)}, u32[]{:S(2)}, u32[]{:S(2)}) collective-permute-start(f32[64,128]{1,0:T(8,128)S(1)} %shard_map.116), channel_id=1, source_target_pairs={{0,0},{1,8},{2,4},{3,12},{4,1},{5,9},{6,5},{7,13},{8,16},{9,24},{1... | collective-permute-start | bytes 98312 | tf_op jit(solution)/shard_map/ppermute | solution.py:353
Sparse Core Ops, SparseCore 0:
  10.2 52.3 all-gather.2

commit v11 on v10

--- a/solution.py
+++ b/solution.py
@@ -248,6 +248,20 @@
     )(queries, keys, values, segment, row_type, pair_index).reshape(8, PAY, HD)
 
 
+def hold_kernel(value_ref, after_ref, out_ref):
+    del value_ref, after_ref, out_ref
+
+
+def run_hold(value, after):
+    return call(
+        hold_kernel,
+        shape(value.shape),
+        in_specs=[pl.BlockSpec(memory_space=pl.ANY)] * 2,
+        out_specs=pl.BlockSpec(memory_space=pl.ANY),
+        input_output_aliases={0: 0},
+    )(value, after)
+
+
 def run_forward(arrived):
     return call(
         forward_kernel,
@@ -338,7 +352,7 @@
     quarter = lax.ppermute(share, AXES, weight_moves())
     cot = lax.all_gather(cotangent[0], NEAR, axis=0, tiled=True)
     payload = run_pack(queries, keys, values, segment, row_type, pair_index)
-    arrived = lax.all_to_all(payload, NEAR, 0, 0)
+    arrived = lax.all_to_all(run_hold(payload, quarter), NEAR, 0, 0)
     out, lse = run_forward(arrived)
     quarters = [quarter] + [
         lax.ppermute(quarter, "x", [(i, (i + turn) % 4) for i in range(4)]) for turn in (1, 2, 3)

time: 141 us -> 140 us (level)
    ppermute x1, waiting for transfers between devices: 23.6 us -> 8.62 us  [local(): quarter = lax.ppermute(share, AXES, weight_moves())]
    all_to_all x1, waiting for transfers between devices: 0.01 us -> 14.9 us  [local(): arrived = lax.all_to_all(run_hold(payload, quarter), NEAR, 0, 0)]
    ppermute x1, starting transfers between devices: 3.99 us -> 9.66 us  [local(): quarter = lax.ppermute(share, AXES, weight_moves())]
    all_to_all x1, starting transfers between devices: 10.3 us -> 5.69 us  [local(): arrived = lax.all_to_all(run_hold(payload, quarter), NEAR, 0, 0)]
    ppermute x3, waiting for transfers between devices: 4.2 us -> 0.01 us  [local(): lax.ppermute(quarter, 'x', [(i, (i + turn) % 4) for i in range(4)])]
    ppermute x7, waiting for transfers between devices: 0.03 us -> 3.97 us  [local(): lax.ppermute(other, NEAR, [(i, i ^ k + 1) for i in range(8)])]
    ppermute x7, starting transfers between devices: 22.5 us -> 19.4 us  [local(): lax.ppermute(other, NEAR, [(i, i ^ k + 1) for i in range(8)])]
    ppermute x3, starting transfers between devices: 9.17 us -> 10.7 us  [local(): lax.ppermute(quarter, 'x', [(i, (i + turn) % 4) for i in range(4)])]
  transfers between devices with their start and end apart: 15 -> 15, of which waited for: 3 -> 4; matrix products, arithmetic and copies ran while one was open for 0% -> 0% of each run, Pallas kernels for 16% -> 16%
where the time goes in v11:
time: 140 us
  starting transfers between devices  66.6 us (48%)
  waiting for transfers between devices  28.2 us (20%)
  Pallas kernels  26.4 us (19%)
  between operations  14.3 us (10%)
  local copies, waits for them, and re-layouts  3.47 us (2%)
    ppermute x7, starting transfers between devices, local(): lax.ppermute(other, NEAR, [(i, i ^ k + 1) for i in range(8)])  19.4 us
    all_to_all x1, waiting for transfers between devices, local(): arrived = lax.all_to_all(run_hold(payload, quarter), NEAR, 0, 0)  14.9 us
    all_to_all x1, starting transfers between devices, local(): got = lax.all_to_all(pieces, FAR, 0, 0)  14.2 us
    pallas_call x1, Pallas kernels, run_backward(): call(backward_kernel, (shape((4 * TOK, HD)),) * 8, flops=8 << 30, bytes_a...  11.4 us
    ppermute x3, starting transfers between devices, local(): lax.ppermute(quarter, 'x', [(i, (i + turn) % 4) for i in range(4)])  10.7 us
    ppermute x1, starting transfers between devices, local(): quarter = lax.ppermute(share, AXES, weight_moves())  9.66 us
    ppermute x1, waiting for transfers between devices, local(): quarter = lax.ppermute(share, AXES, weight_moves())  8.62 us
    ppermute x1, starting transfers between devices, local(): weight_grad = lax.ppermute(run_sum(got), AXES, piece_moves()).T  6.92 us
  transfers between devices with their start and end apart: 15, of which 4 were waited for; matrix products, arithmetic and copies ran while one was open for 0% of the time, Pallas kernels for 16%

profile of v11, /device:TPU:1, one launch (start us, length us, event | category | flops | bytes accessed | tf_op | source)
XLA Modules:
  0.0 139.6 jit_solution(7826632325903122603)
XLA Ops:
  7.2 0.0 copy-start
  7.2 0.0 all-gather.3.cloned.1.call-start
  7.2 0.7 all-gather.3.cloned.1.call-update
  7.9 0.3 copy-done
  8.2 9.7 %collective-permute-start = (bf16[64,2048]{1,0:T(8,128)(2,1)S(1)}, bf16[64,2048]{1,0:T(8,128)(2,1)S(1)}, u32[]{:S(2)}, u32[]{:S(2)}) collective-permute-start(bf16[64,2048]{1,0:T(8,128)(2,1)S(1)} %constant_dynamic-slice_fusion), channel_id=1, source_target_pairs={{0,0},{8,1},{4,2},{12,3},{16,4},{24,5},{20,6},{28,7},{256,8},{264,... | collective-permute-start | bytes 786440 | tf_op jit(solution)/shard_map/ppermute | solution.py:352
  17.9 3.5 %shard_map.111 = bf16[2,4,528,128]{3,2,1,0:T(8,128)(2,1)} custom-call(bf16[1,128,2048]{2,1,0:T(8,128)(2,1)} %q_ref.1, bf16[1,128,1024]{2,1,0:T(8,128)(2,1)} %k_ref.1, bf16[1,128,1024]{2,1,0:T(8,128)(2,1)} %v_ref.1, s32[1,128]{1,0:T(1,128)} %seg_ref.1, s32[1,128]{1,0:T(1,128)} %type_ref.1, s32[1,24]{1,0:T(1,128)} %pair_ref.1), custom_call_target="tpu_custom_call" | custom-call | bytes 2097152 | tf_op jit(solution)/shard_map/pallas_call | solution.py:234
  21.4 8.6 %collective-permute-done.after_ref.w0_ref = bf16[64,2048]{1,0:T(8,128)(2,1)S(1)} collective-permute-done((bf16[64,2048]{1,0:T(8,128)(2,1)S(1)}, bf16[64,2048]{1,0:T(8,128)(2,1)S(1)}, u32[]{:S(2)}, u32[]{:S(2)}) %collective-permute-start) | collective-permute-done | bytes 262176 | tf_op jit(solution)/shard_map/ppermute | solution.py:352
  30.0 0.0 copy-start.4
  30.0 0.7 copy-done.4
  30.7 0.0 copy-start.5
  30.7 5.7 %all-to-all-start = ((bf16[8,528,128]{2,1,0:T(8,128)(2,1)}), bf16[8,528,128]{2,1,0:T(8,128)(2,1)S(1)}, u32[]{:S(2)}, u32[]{:S(2)}) async-start(bf16[8,528,128]{2,1,0:T(8,128)(2,1)} %shard_map.112), calls=%async_computation | async-start | bytes 2162688 | tf_op jit(solution)/shard_map/all_to_all | solution.py:355
  36.4 0.0 copy-done.5
  36.4 6.3 %collective-permute-start.3 = (bf16[64,2048]{1,0:T(8,128)(2,1)S(1)}, bf16[64,2048]{1,0:T(8,128)(2,1)S(1)}, u32[]{:S(2)}, u32[]{:S(2)}) collective-permute-start(bf16[64,2048]{1,0:T(8,128)(2,1)S(1)} %copy-done.5), channel_id=1, source_target_pairs={{0,384},{128,0},{256,128},{384,256},{1,385},{129,1},{257,129},{385... | collective-permute-start | bytes 786440 | tf_op jit(solution)/shard_map/ppermute | solution.py:358
  42.8 1.9 %collective-permute-start.2 = (bf16[64,2048]{1,0:T(8,128)(2,1)S(1)}, bf16[64,2048]{1,0:T(8,128)(2,1)S(1)}, u32[]{:S(2)}, u32[]{:S(2)}) collective-permute-start(bf16[64,2048]{1,0:T(8,128)(2,1)S(1)} %copy-done.5), channel_id=1, source_target_pairs={{0,256},{128,384},{256,0},{384,128},{1,257},{129,385},{257,1},{385... | collective-permute-start | bytes 786440 | tf_op jit(solution)/shard_map/ppermute | solution.py:358
  44.7 2.5 %collective-permute-start.1 = (bf16[64,2048]{1,0:T(8,128)(2,1)S(1)}, bf16[64,2048]{1,0:T(8,128)(2,1)S(1)}, u32[]{:S(2)}, u32[]{:S(2)}) collective-permute-start(bf16[64,2048]{1,0:T(8,128)(2,1)S(1)} %copy-done.5), channel_id=1, source_target_pairs={{0,128},{128,256},{256,384},{384,0},{1,129},{129,257},{257,385},{3... | collective-permute-start | bytes 786440 | tf_op jit(solution)/shard_map/ppermute | solution.py:358
  47.2 14.9 %all-to-all-done.pay_ref = bf16[8,528,128]{2,1,0:T(8,128)(2,1)S(1)} async-done(((bf16[8,528,128]{2,1,0:T(8,128)(2,1)}), bf16[8,528,128]{2,1,0:T(8,128)(2,1)S(1)}, u32[]{:S(2)}, u32[]{:S(2)}) %all-to-all-start) | async-done | bytes 1081376 | tf_op jit(solution)/shard_map/all_to_all | solution.py:355
  62.1 0.0 copy-start.3
  62.1 1.0 copy-done.3
  63.1 5.3 %shard_map.113 = (bf16[256,1024]{1,0:T(8,128)(2,1)}, f32[1024,128]{1,0:T(8,128)}) custom-call(bf16[8,528,128]{2,1,0:T(8,128)(2,1)} %copy-done.3), custom_call_target="tpu_custom_call" | custom-call | flops 4294967296 | bytes 2097152 | tf_op jit(solution)/shard_map/pallas_call | solution.py:266
  68.4 0.0 collective-permute-done.3.w3_ref.c_ref
  68.4 0.0 copy-start.6
  68.4 0.0 collective-permute-done.2.w2_ref.b_ref
  68.4 0.0 copy-start.7
  68.4 0.0 collective-permute-done.1.w1_ref.a_ref
  68.4 0.0 copy-start.8
  68.4 0.0 all-gather.3.cloned.1.call-done
  68.5 0.6 copy-done.6
  69.1 0.1 copy-done.7
  69.2 0.1 copy-done.8
  69.3 4.1 %shard_map.116 = bf16[64,64,128]{2,1,0:T(8,128)(2,1)} custom-call(bf16[256,1024]{1,0:T(8,128)(2,1)} %get-tuple-element.29.out_ref, bf16[1024,2048]{1,0:T(8,128)(2,1)} %bitcast.7, bf16[64,2048]{1,0:T(8,128)(2,1)} %copy-done.8, bf16[64,2048]{1,0:T(8,128)(2,1)} %copy-done.7, bf16[64,2048]{1,0:T(8,128)(2,1)} %copy-done.6), custom_call_target="tpu_custom_call" | custom-call | flops 1073741824 | bytes 6291456 | tf_op jit(solution)/shard_map/pallas_call | solution.py:281
  73.3 14.2 %all-to-all-start.1 = ((bf16[64,64,128]{2,1,0:T(8,128)(2,1)}), bf16[64,64,128]{2,1,0:T(8,128)(2,1)S(1)}, u32[]{:S(2)}, u32[]{:S(2)}) async-start(bf16[64,64,128]{2,1,0:T(8,128)(2,1)} %shard_map.116), calls=%async_computation.1 | async-start | bytes 2097152 | tf_op jit(solution)/shard_map/all_to_all | solution.py:361
  87.5 0.6 pad_add_fusion.me_ref
  88.1 11.4 %shard_map.114 = (bf16[512,128]{1,0:T(8,128)(2,1)}, bf16[512,128]{1,0:T(8,128)(2,1)}, bf16[512,128]{1,0:T(8,128)(2,1)}, bf16[512,128]{1,0:T(8,128)(2,1)}, bf16[5...) custom-call(s32[3]{0:T(128)} %pad_add_fusion.me_ref, ...), custom_call_target="tpu_custom_call" | custom-call | flops 8589934592 | bytes 7340032 | tf_op jit(solution)/shard_map/pallas_call | solution.py:318
  99.6 0.0 copy-start.1
  99.6 0.0 copy-start.2
  99.6 3.2 %collective-permute-start.4 = (bf16[512,128]{1,0:T(8,128)(2,1)}, bf16[512,128]{1,0:T(8,128)(2,1)S(1)}, u32[]{:S(2)}, u32[]{:S(2)}) collective-permute-start(bf16[512,128]{1,0:T(8,128)(2,1)} %get-tuple-element.19), channel_id=1, source_target_pairs={{0,1},{1,0},{2,3},{3,2},{16,17},{17,16},{18,19},{19,18},{4,5},{5,4... | collective-permute-start | bytes 393224 | tf_op jit(solution)/shard_map/ppermute | solution.py:365
  102.7 2.4 %collective-permute-start.5 = (bf16[512,128]{1,0:T(8,128)(2,1)}, bf16[512,128]{1,0:T(8,128)(2,1)S(1)}, u32[]{:S(2)}, u32[]{:S(2)}) collective-permute-start(bf16[512,128]{1,0:T(8,128)(2,1)} %get-tuple-element.20), channel_id=1, source_target_pairs={{0,2},{1,3},{2,0},{3,1},{16,18},{17,19},{18,16},{19,17},{4,6},{5,7... | collective-permute-start | bytes 393224 | tf_op jit(solution)/shard_map/ppermute | solution.py:365
  105.1 3.1 %collective-permute-start.6 = (bf16[512,128]{1,0:T(8,128)(2,1)}, bf16[512,128]{1,0:T(8,128)(2,1)S(1)}, u32[]{:S(2)}, u32[]{:S(2)}) collective-permute-start(bf16[512,128]{1,0:T(8,128)(2,1)} %get-tuple-element.21), channel_id=1, source_target_pairs={{0,3},{1,2},{2,1},{3,0},{16,19},{17,18},{18,17},{19,16},{4,7},{5,6... | collective-permute-start | bytes 393224 | tf_op jit(solution)/shard_map/ppermute | solution.py:365
  108.2 2.1 %collective-permute-start.7 = (bf16[512,128]{1,0:T(8,128)(2,1)}, bf16[512,128]{1,0:T(8,128)(2,1)S(1)}, u32[]{:S(2)}, u32[]{:S(2)}) collective-permute-start(bf16[512,128]{1,0:T(8,128)(2,1)} %get-tuple-element.22), channel_id=1, source_target_pairs={{0,16},{1,17},{2,18},{3,19},{16,0},{17,1},{18,2},{19,3},{4,20},{5,... | collective-permute-start | bytes 393224 | tf_op jit(solution)/shard_map/ppermute | solution.py:365
  110.3 3.6 %collective-permute-start.8 = (bf16[512,128]{1,0:T(8,128)(2,1)}, bf16[512,128]{1,0:T(8,128)(2,1)S(1)}, u32[]{:S(2)}, u32[]{:S(2)}) collective-permute-start(bf16[512,128]{1,0:T(8,128)(2,1)} %get-tuple-element.23), channel_id=1, source_target_pairs={{0,17},{1,16},{2,19},{3,18},{16,1},{17,0},{18,3},{19,2},{4,21},{5,... | collective-permute-start | bytes 393224 | tf_op jit(solution)/shard_map/ppermute | solution.py:365
  113.9 0.0 collective-permute-done.4.refs_1_
  113.9 2.6 %collective-permute-start.9 = (bf16[512,128]{1,0:T(8,128)(2,1)}, bf16[512,128]{1,0:T(8,128)(2,1)S(1)}, u32[]{:S(2)}, u32[]{:S(2)}) collective-permute-start(bf16[512,128]{1,0:T(8,128)(2,1)} %get-tuple-element.24), channel_id=1, source_target_pairs={{0,18},{1,19},{2,16},{3,17},{16,2},{17,3},{18,0},{19,1},{4,22},{5,... | collective-permute-start | bytes 393224 | tf_op jit(solution)/shard_map/ppermute | solution.py:365
  116.5 1.3 collective-permute-done.5.refs_2_
  117.7 2.5 %collective-permute-start.10 = (bf16[512,128]{1,0:T(8,128)(2,1)}, bf16[512,128]{1,0:T(8,128)(2,1)S(1)}, u32[]{:S(2)}, u32[]{:S(2)}) collective-permute-start(bf16[512,128]{1,0:T(8,128)(2,1)} %get-tuple-element.25), channel_id=1, source_target_pairs={{0,19},{1,18},{2,17},{3,16},{16,3},{17,2},{18,1},{19,0},{4,23},{5,... | collective-permute-start | bytes 393224 | tf_op jit(solution)/shard_map/ppermute | solution.py:365
  120.3 0.0 all-to-all-done.1.got_ref
  120.3 0.4 shard_map.117
  120.6 2.7 %collective-permute-done.6.refs_3_ = bf16[512,128]{1,0:T(8,128)(2,1)S(1)} collective-permute-done((bf16[512,128]{1,0:T(8,128)(2,1)}, bf16[512,128]{1,0:T(8,128)(2,1)S(1)}, u32[]{:S(2)}, u32[]{:S(2)}) %collective-permute-start.6) | collective-permute-done | bytes 131104 | tf_op jit(solution)/shard_map/ppermute | solution.py:365
  123.3 6.9 %collective-permute-start.11 = (f32[64,128]{1,0:T(8,128)S(1)}, f32[64,128]{1,0:T(8,128)S(1)}, u32[]{:S(2)}, u32[]{:S(2)}) collective-permute-start(f32[64,128]{1,0:T(8,128)S(1)} %shard_map.117), channel_id=1, source_target_pairs={{0,0},{1,8},{2,4},{3,12},{4,1},{5,9},{6,5},{7,13},{8,16},{9,24},{1... | collective-permute-start | bytes 98312 | tf_op jit(solution)/shard_map/ppermute | solution.py:367
  130.3 0.0 collective-permute-done.7.refs_4_
  130.3 0.0 collective-permute-done.8.refs_5_
  130.3 0.0 collective-permute-done.9.refs_6_
  130.3 0.0 collective-permute-done.10.refs_7_
  130.3 0.0 copy-done.1
  130.3 0.0 copy-done.2
  130.3 1.8 %shard_map.115 = (bf16[1,128,2048]{2,1,0:T(8,128)(2,1)}, bf16[1,128,1024]{2,1,0:T(8,128)(2,1)}, bf16[1,128,1024]{2,1,0:T(8,128)(2,1)}) custom-call(s32[3]{0:T(128)S(1)} %copy-done.2, bf16[512,128]{1,0:T(8,128)(2,1)S(1)} %copy-done.1, bf16[512,128]{1,0:T(8,128)(2,1)S(1)} %collective-permute-done.4.refs_1_, ...), custom_call_target="tpu_custom_call" | custom-call | bytes 2097152 | tf_op jit(solution)/shard_map/pallas_call | solution.py:339
  132.2 0.0 collective-permute-done.11
  132.2 0.6 copy.15
  (2 shorter events, 0.0 us)
Async XLA Ops:
  7.2 1.0 copy-start
  7.2 61.3 %all-gather.3.cloned.1.call-start = ((), (), s32[]{:S(2)}) async-start(), calls=%async_computation.2 | async-start | bytes 4718592 | tf_op jit(solution)/shard_map/all_gather | solution.py:353
  8.2 21.8 %collective-permute-start = (bf16[64,2048]{1,0:T(8,128)(2,1)S(1)}, bf16[64,2048]{1,0:T(8,128)(2,1)S(1)}, u32[]{:S(2)}, u32[]{:S(2)}) collective-permute-start(bf16[64,2048]{1,0:T(8,128)(2,1)S(1)} %constant_dynamic-slice_fusion), channel_id=1, source_target_pairs={{0,0},{8,1},{4,2},{12,3},{16,4},{24,5},{20,6},{28,7},{256,8},{264,... | collective-permute-start | bytes 786440 | tf_op jit(solution)/shard_map/ppermute | solution.py:352
  30.0 0.7 copy-start.4
  30.7 5.7 %copy-start.5 = (bf16[64,2048]{1,0:T(8,128)(2,1)S(1)}, bf16[64,2048]{1,0:T(8,128)(2,1)}, u32[]{:S(2)}) copy-start(bf16[64,2048]{1,0:T(8,128)(2,1)} %copy-done.4) | copy-start | bytes 786436
  30.7 31.4 %all-to-all-start = ((bf16[8,528,128]{2,1,0:T(8,128)(2,1)}), bf16[8,528,128]{2,1,0:T(8,128)(2,1)S(1)}, u32[]{:S(2)}, u32[]{:S(2)}) async-start(bf16[8,528,128]{2,1,0:T(8,128)(2,1)} %shard_map.112), calls=%async_computation | async-start | bytes 2162688 | tf_op jit(solution)/shard_map/all_to_all | solution.py:355
  36.4 32.0 %collective-permute-start.3 = (bf16[64,2048]{1,0:T(8,128)(2,1)S(1)}, bf16[64,2048]{1,0:T(8,128)(2,1)S(1)}, u32[]{:S(2)}, u32[]{:S(2)}) collective-permute-start(bf16[64,2048]{1,0:T(8,128)(2,1)S(1)} %copy-done.5), channel_id=1, source_target_pairs={{0,384},{128,0},{256,128},{384,256},{1,385},{129,1},{257,129},{385... | collective-permute-start | bytes 786440 | tf_op jit(solution)/shard_map/ppermute | solution.py:358
  42.8 25.6 %collective-permute-start.2 = (bf16[64,2048]{1,0:T(8,128)(2,1)S(1)}, bf16[64,2048]{1,0:T(8,128)(2,1)S(1)}, u32[]{:S(2)}, u32[]{:S(2)}) collective-permute-start(bf16[64,2048]{1,0:T(8,128)(2,1)S(1)} %copy-done.5), channel_id=1, source_target_pairs={{0,256},{128,384},{256,0},{384,128},{1,257},{129,385},{257,1},{385... | collective-permute-start | bytes 786440 | tf_op jit(solution)/shard_map/ppermute | solution.py:358
  44.7 23.7 %collective-permute-start.1 = (bf16[64,2048]{1,0:T(8,128)(2,1)S(1)}, bf16[64,2048]{1,0:T(8,128)(2,1)S(1)}, u32[]{:S(2)}, u32[]{:S(2)}) collective-permute-start(bf16[64,2048]{1,0:T(8,128)(2,1)S(1)} %copy-done.5), channel_id=1, source_target_pairs={{0,128},{128,256},{256,384},{384,0},{1,129},{129,257},{257,385},{3... | collective-permute-start | bytes 786440 | tf_op jit(solution)/shard_map/ppermute | solution.py:358
  62.1 1.0 copy-start.3
  68.4 0.7 copy-start.6
  68.4 0.8 copy-start.7
  68.4 0.8 copy-start.8
  73.3 47.0 %all-to-all-start.1 = ((bf16[64,64,128]{2,1,0:T(8,128)(2,1)}), bf16[64,64,128]{2,1,0:T(8,128)(2,1)S(1)}, u32[]{:S(2)}, u32[]{:S(2)}) async-start(bf16[64,64,128]{2,1,0:T(8,128)(2,1)} %shard_map.116), calls=%async_computation.1 | async-start | bytes 2097152 | tf_op jit(solution)/shard_map/all_to_all | solution.py:361
  99.6 30.8 %copy-start.1 = (bf16[512,128]{1,0:T(8,128)(2,1)S(1)}, bf16[512,128]{1,0:T(8,128)(2,1)}, u32[]{:S(2)}) copy-start(bf16[512,128]{1,0:T(8,128)(2,1)} %get-tuple-element.18.refs_0_) | copy-start | bytes 393220
  99.6 30.8 %copy-start.2 = (s32[3]{0:T(128)S(1)}, s32[3]{0:T(128)}, u32[]{:S(2)}) copy-start(s32[3]{0:T(128)} %pad_add_fusion.me_ref) | copy-start | bytes 40
  99.6 14.3 %collective-permute-start.4 = (bf16[512,128]{1,0:T(8,128)(2,1)}, bf16[512,128]{1,0:T(8,128)(2,1)S(1)}, u32[]{:S(2)}, u32[]{:S(2)}) collective-permute-start(bf16[512,128]{1,0:T(8,128)(2,1)} %get-tuple-element.19), channel_id=1, source_target_pairs={{0,1},{1,0},{2,3},{3,2},{16,17},{17,16},{18,19},{19,18},{4,5},{5,4... | collective-permute-start | bytes 393224 | tf_op jit(solution)/shard_map/ppermute | solution.py:365
  102.7 15.0 %collective-permute-start.5 = (bf16[512,128]{1,0:T(8,128)(2,1)}, bf16[512,128]{1,0:T(8,128)(2,1)S(1)}, u32[]{:S(2)}, u32[]{:S(2)}) collective-permute-start(bf16[512,128]{1,0:T(8,128)(2,1)} %get-tuple-element.20), channel_id=1, source_target_pairs={{0,2},{1,3},{2,0},{3,1},{16,18},{17,19},{18,16},{19,17},{4,6},{5,7... | collective-permute-start | bytes 393224 | tf_op jit(solution)/shard_map/ppermute | solution.py:365
  105.1 18.2 %collective-permute-start.6 = (bf16[512,128]{1,0:T(8,128)(2,1)}, bf16[512,128]{1,0:T(8,128)(2,1)S(1)}, u32[]{:S(2)}, u32[]{:S(2)}) collective-permute-start(bf16[512,128]{1,0:T(8,128)(2,1)} %get-tuple-element.21), channel_id=1, source_target_pairs={{0,3},{1,2},{2,1},{3,0},{16,19},{17,18},{18,17},{19,16},{4,7},{5,6... | collective-permute-start | bytes 393224 | tf_op jit(solution)/shard_map/ppermute | solution.py:365
  108.2 22.1 %collective-permute-start.7 = (bf16[512,128]{1,0:T(8,128)(2,1)}, bf16[512,128]{1,0:T(8,128)(2,1)S(1)}, u32[]{:S(2)}, u32[]{:S(2)}) collective-permute-start(bf16[512,128]{1,0:T(8,128)(2,1)} %get-tuple-element.22), channel_id=1, source_target_pairs={{0,16},{1,17},{2,18},{3,19},{16,0},{17,1},{18,2},{19,3},{4,20},{5,... | collective-permute-start | bytes 393224 | tf_op jit(solution)/shard_map/ppermute | solution.py:365
  110.3 20.0 %collective-permute-start.8 = (bf16[512,128]{1,0:T(8,128)(2,1)}, bf16[512,128]{1,0:T(8,128)(2,1)S(1)}, u32[]{:S(2)}, u32[]{:S(2)}) collective-permute-start(bf16[512,128]{1,0:T(8,128)(2,1)} %get-tuple-element.23), channel_id=1, source_target_pairs={{0,17},{1,16},{2,19},{3,18},{16,1},{17,0},{18,3},{19,2},{4,21},{5,... | collective-permute-start | bytes 393224 | tf_op jit(solution)/shard_map/ppermute | solution.py:365
  113.9 16.4 %collective-permute-start.9 = (bf16[512,128]{1,0:T(8,128)(2,1)}, bf16[512,128]{1,0:T(8,128)(2,1)S(1)}, u32[]{:S(2)}, u32[]{:S(2)}) collective-permute-start(bf16[512,128]{1,0:T(8,128)(2,1)} %get-tuple-element.24), channel_id=1, source_target_pairs={{0,18},{1,19},{2,16},{3,17},{16,2},{17,3},{18,0},{19,1},{4,22},{5,... | collective-permute-start | bytes 393224 | tf_op jit(solution)/shard_map/ppermute | solution.py:365
  117.7 12.6 %collective-permute-start.10 = (bf16[512,128]{1,0:T(8,128)(2,1)}, bf16[512,128]{1,0:T(8,128)(2,1)S(1)}, u32[]{:S(2)}, u32[]{:S(2)}) collective-permute-start(bf16[512,128]{1,0:T(8,128)(2,1)} %get-tuple-element.25), channel_id=1, source_target_pairs={{0,19},{1,18},{2,17},{3,16},{16,3},{17,2},{18,1},{19,0},{4,23},{5,... | collective-permute-start | bytes 393224 | tf_op jit(solution)/shard_map/ppermute | solution.py:365
  123.3 8.8 %collective-permute-start.11 = (f32[64,128]{1,0:T(8,128)S(1)}, f32[64,128]{1,0:T(8,128)S(1)}, u32[]{:S(2)}, u32[]{:S(2)}) collective-permute-start(f32[64,128]{1,0:T(8,128)S(1)} %shard_map.117), channel_id=1, source_target_pairs={{0,0},{1,8},{2,4},{3,12},{4,1},{5,9},{6,5},{7,13},{8,16},{9,24},{1... | collective-permute-start | bytes 98312 | tf_op jit(solution)/shard_map/ppermute | solution.py:367
Sparse Core Ops, SparseCore 0:
  10.2 54.4 all-gather.2

commit v12 on v11

--- a/solution.py
+++ b/solution.py
@@ -137,29 +137,43 @@
 
 
 def backward_kernel(me_ref, pay_ref, lse_ref, cot_ref, w0_ref, w1_ref, w2_ref, w3_ref, *refs):
-    *out_refs, wbuf, ghbuf, ret_ref = refs
-
-    @pl.when(pl.program_id(0) == 0)
+    *out_refs, wbuf, ghbuf, ret_ref, abuf, cbuf, sem = refs
+    now = pl.program_id(0)
+
+    def fetch(step):
+        first = pl.multiple_of(jnp.bitwise_xor(step, me_ref[1]) * WINDOW, WINDOW)
+        return pltpu.make_async_copy(cot_ref.at[pl.ds(first, WINDOW)], cbuf.at[step], sem.at[step])
+
+    @pl.when(now == 0)
     def _():
+        fetch(0).start()
+        fetch(1).start()
         for turn, quarter in enumerate((w0_ref, w1_ref, w2_ref, w3_ref)):
             first = pl.multiple_of(lax.rem(me_ref[0] + 4 - turn, 4) * 64, 64)
             wbuf[pl.ds(first, 64), :] = quarter[...]
 
-    ghbuf[...] = dot(cot_ref[...], wbuf[...], ((1,), (1,))).astype(BF16)
     key = rows(pay_ref, 2 * TOK)
     value = rows(pay_ref, 3 * TOK)
     want, have = hot(pay_ref)
-    kparts = [[None, None], [None, None]]
-    vparts = [[None, None], [None, None]]
     for block in range(2):
         lo = block * HALF
         ext = lo + HALF
         visible = visible_block(want, have, lo, ext)
         for b in range(2):
             query = rows(pay_ref, b * TOK)[lo:ext]
+            scores = dot(query, key[:ext], ((1,), (1,))) * SCALE - lse_ref[lo:ext, b : b + 1]
+            abuf[b, lo:ext, :ext] = jnp.exp(jnp.where(visible, scores, -jnp.inf))
+    fetch(now).wait()
+    ghbuf[...] = dot(cbuf[now], wbuf[...], ((1,), (1,))).astype(BF16)
+    kparts = [[None, None], [None, None]]
+    vparts = [[None, None], [None, None]]
+    for block in range(2):
+        lo = block * HALF
+        ext = lo + HALF
+        for b in range(2):
+            query = rows(pay_ref, b * TOK)[lo:ext]
             grad = ghbuf[lo:ext, b * HD : (b + 1) * HD]
-            scores = dot(query, key[:ext], ((1,), (1,))) * SCALE - lse_ref[lo:ext, b : b + 1]
-            attend = jnp.exp(jnp.where(visible, scores, -jnp.inf))
+            attend = abuf[b, lo:ext, :ext]
             low = attend.astype(BF16)
             grad_attend = dot(grad, value[:ext], ((1,), (1,)))
             delta = jnp.sum(attend * grad_attend, axis=-1, keepdims=True)
@@ -266,6 +280,7 @@
     return call(
         forward_kernel,
         (shape((2 * HD, 2 * WINDOW)), shape((2 * WINDOW, HD), F32)),
+        room=40,
         flops=4 << 30,
         bytes_accessed=2 << 20,
         grid=(2,),
@@ -305,7 +320,7 @@
         in_specs=[
             pl.BlockSpec((4, PAY, HD), lambda i, me_ref: (row(i, me_ref), 0, 0)),
             pl.BlockSpec((WINDOW, HD), lambda i, me_ref: (row(i, me_ref), 0)),
-            pl.BlockSpec((WINDOW, width), lambda i, me_ref: (row(i, me_ref), 0)),
+            pl.BlockSpec(memory_space=pltpu.HBM),
         ]
         + [whole(64, width)] * 4,
         out_specs=[whole(4 * TOK, HD)] * 8,
@@ -313,6 +328,9 @@
             pltpu.VMEM((2 * HD, width), BF16),
             pltpu.VMEM((WINDOW, 2 * HD), BF16),
             pltpu.VMEM((4, 4 * TOK, HD), BF16),
+            pltpu.VMEM((2, WINDOW, WINDOW), F32),
+            pltpu.VMEM((2, WINDOW, width), BF16),
+            pltpu.SemaphoreType.DMA((2,)),
         ],
     )
     return call(

time: 140 us -> 137 us (0.979)
    ppermute x1, starting transfers between devices: 6.92 us -> 5.09 us  [local(): weight_grad = lax.ppermute(run_sum(got), AXES, piece_moves()).T]
    pallas_call x1, Pallas kernels: 5.25 us -> 3.51 us  [run_forward(): call(forward_kernel, (shape((2 * HD, 2 * WINDOW)), shape((2 * WINDOW, HD)...]
    unnamed x19 -> x23, local copies, waits for them, and re-layouts: 3.45 us -> 3.28 us
where the time goes in v12:
time: 137 us; the launch traced here: 136 us
  starting transfers between devices  65.4 us (48%)
  waiting for transfers between devices  27.1 us (20%)
  Pallas kernels  25.3 us (18%)
  between operations  14.3 us (10%)
  local copies, waits for them, and re-layouts  3.3 us (2%)
    ppermute x7, starting transfers between devices, local(): lax.ppermute(other, NEAR, [(i, i ^ k + 1) for i in range(8)])  20 us
    all_to_all x1, waiting for transfers between devices, local(): arrived = lax.all_to_all(run_hold(payload, quarter), NEAR, 0, 0)  14.9 us
    all_to_all x1, starting transfers between devices, local(): got = lax.all_to_all(pieces, FAR, 0, 0)  14.2 us
    pallas_call x1, Pallas kernels, run_backward(): call(backward_kernel, (shape((4 * TOK, HD)),) * 8, flops=8 << 30, bytes_a...  12 us
    ppermute x3, starting transfers between devices, local(): lax.ppermute(quarter, 'x', [(i, (i + turn) % 4) for i in range(4)])  10.7 us
    ppermute x1, starting transfers between devices, local(): quarter = lax.ppermute(share, AXES, weight_moves())  9.66 us
    ppermute x1, waiting for transfers between devices, local(): quarter = lax.ppermute(share, AXES, weight_moves())  8.57 us
    all_to_all x1, starting transfers between devices, local(): arrived = lax.all_to_all(run_hold(payload, quarter), NEAR, 0, 0)  5.69 us
  transfers between devices with their start and end apart: 15, of which 4 were waited for; matrix products, arithmetic and copies ran while one was open for 0% of the time, Pallas kernels for 16%

profile of v12, /device:TPU:1, one launch (start us, length us, event | category | flops | bytes accessed | tf_op | source)
XLA Modules:
  0.0 135.9 jit_solution(16938840436861987880)
XLA Ops:
  7.2 0.0 copy-start
  7.2 0.0 all-gather.3.cloned.1.call-start
  7.2 0.7 all-gather.3.cloned.1.call-update
  7.9 0.3 copy-done
  8.2 9.7 %collective-permute-start = (bf16[64,2048]{1,0:T(8,128)(2,1)S(1)}, bf16[64,2048]{1,0:T(8,128)(2,1)S(1)}, u32[]{:S(2)}, u32[]{:S(2)}) collective-permute-start(bf16[64,2048]{1,0:T(8,128)(2,1)S(1)} %constant_dynamic-slice_fusion), channel_id=1, source_target_pairs={{0,0},{8,1},{4,2},{12,3},{16,4},{24,5},{20,6},{28,7},{256,8},{264,... | collective-permute-start | bytes 786440 | tf_op jit(solution)/shard_map/ppermute | solution.py:370
  17.9 3.5 %shard_map.111 = bf16[2,4,528,128]{3,2,1,0:T(8,128)(2,1)} custom-call(bf16[1,128,2048]{2,1,0:T(8,128)(2,1)} %q_ref.1, bf16[1,128,1024]{2,1,0:T(8,128)(2,1)} %k_ref.1, bf16[1,128,1024]{2,1,0:T(8,128)(2,1)} %v_ref.1, s32[1,128]{1,0:T(1,128)} %seg_ref.1, s32[1,128]{1,0:T(1,128)} %type_ref.1, s32[1,24]{1,0:T(1,128)} %pair_ref.1), custom_call_target="tpu_custom_call" | custom-call | bytes 2097152 | tf_op jit(solution)/shard_map/pallas_call | solution.py:248
  21.5 8.6 %collective-permute-done.after_ref.w0_ref = bf16[64,2048]{1,0:T(8,128)(2,1)S(1)} collective-permute-done((bf16[64,2048]{1,0:T(8,128)(2,1)S(1)}, bf16[64,2048]{1,0:T(8,128)(2,1)S(1)}, u32[]{:S(2)}, u32[]{:S(2)}) %collective-permute-start) | collective-permute-done | bytes 262176 | tf_op jit(solution)/shard_map/ppermute | solution.py:370
  30.0 0.0 copy-start.6
  30.0 0.7 copy-done.6
  30.7 0.0 copy-start.7
  30.7 5.7 %all-to-all-start = ((bf16[8,528,128]{2,1,0:T(8,128)(2,1)}), bf16[8,528,128]{2,1,0:T(8,128)(2,1)S(1)}, u32[]{:S(2)}, u32[]{:S(2)}) async-start(bf16[8,528,128]{2,1,0:T(8,128)(2,1)} %shard_map.112), calls=%async_computation | async-start | bytes 2162688 | tf_op jit(solution)/shard_map/all_to_all | solution.py:373
  36.4 0.0 copy-done.7
  36.4 6.3 %collective-permute-start.3 = (bf16[64,2048]{1,0:T(8,128)(2,1)S(1)}, bf16[64,2048]{1,0:T(8,128)(2,1)S(1)}, u32[]{:S(2)}, u32[]{:S(2)}) collective-permute-start(bf16[64,2048]{1,0:T(8,128)(2,1)S(1)} %copy-done.7), channel_id=1, source_target_pairs={{0,384},{128,0},{256,128},{384,256},{1,385},{129,1},{257,129},{385... | collective-permute-start | bytes 786440 | tf_op jit(solution)/shard_map/ppermute | solution.py:376
  42.8 1.9 %collective-permute-start.2 = (bf16[64,2048]{1,0:T(8,128)(2,1)S(1)}, bf16[64,2048]{1,0:T(8,128)(2,1)S(1)}, u32[]{:S(2)}, u32[]{:S(2)}) collective-permute-start(bf16[64,2048]{1,0:T(8,128)(2,1)S(1)} %copy-done.7), channel_id=1, source_target_pairs={{0,256},{128,384},{256,0},{384,128},{1,257},{129,385},{257,1},{385... | collective-permute-start | bytes 786440 | tf_op jit(solution)/shard_map/ppermute | solution.py:376
  44.7 2.5 %collective-permute-start.1 = (bf16[64,2048]{1,0:T(8,128)(2,1)S(1)}, bf16[64,2048]{1,0:T(8,128)(2,1)S(1)}, u32[]{:S(2)}, u32[]{:S(2)}) collective-permute-start(bf16[64,2048]{1,0:T(8,128)(2,1)S(1)} %copy-done.7), channel_id=1, source_target_pairs={{0,128},{128,256},{256,384},{384,0},{1,129},{129,257},{257,385},{3... | collective-permute-start | bytes 786440 | tf_op jit(solution)/shard_map/ppermute | solution.py:376
  47.2 14.9 %all-to-all-done.pay_ref = bf16[8,528,128]{2,1,0:T(8,128)(2,1)S(1)} async-done(((bf16[8,528,128]{2,1,0:T(8,128)(2,1)}), bf16[8,528,128]{2,1,0:T(8,128)(2,1)S(1)}, u32[]{:S(2)}, u32[]{:S(2)}) %all-to-all-start) | async-done | bytes 1081376 | tf_op jit(solution)/shard_map/all_to_all | solution.py:373
  62.1 0.0 copy-start.1
  62.1 3.5 %shard_map.113 = (bf16[256,1024]{1,0:T(8,128)(2,1)S(1)}, f32[1024,128]{1,0:T(8,128)S(1)}) custom-call(bf16[8,528,128]{2,1,0:T(8,128)(2,1)S(1)} %all-to-all-done.pay_ref), custom_call_target="tpu_custom_call" | custom-call | flops 4294967296 | bytes 2097152 | tf_op jit(solution)/shard_map/pallas_call | solution.py:280
  65.6 0.0 copy-done.1
  65.6 0.0 copy-start.2
  65.6 0.8 copy-done.2
  66.4 0.0 copy-start.5
  66.4 0.0 collective-permute-done.3.w3_ref.c_ref
  66.4 0.0 copy-start.8
  66.4 0.0 collective-permute-done.2.w2_ref.b_ref
  66.4 0.0 copy-start.9
  66.5 0.0 collective-permute-done.1.w1_ref.a_ref
  66.5 0.0 copy-start.10
  66.5 0.0 all-gather.3.cloned.1.call-done
  66.5 0.7 copy-done.8
  67.2 0.1 copy-done.9
  67.2 0.1 copy-done.10
  67.3 4.1 %shard_map.116 = bf16[64,64,128]{2,1,0:T(8,128)(2,1)} custom-call(bf16[256,1024]{1,0:T(8,128)(2,1)} %copy-done.2, bf16[1024,2048]{1,0:T(8,128)(2,1)} %bitcast.7, bf16[64,2048]{1,0:T(8,128)(2,1)} %copy-done.10, bf16[64,2048]{1,0:T(8,128)(2,1)} %copy-done.9, bf16[64,2048]{1,0:T(8,128)(2,1)} %copy-done.8), custom_call_target="tpu_custom_call" | custom-call | flops 1073741824 | bytes 6291456 | tf_op jit(solution)/shard_map/pallas_call | solution.py:296
  71.4 0.0 copy-done.5
  71.4 14.2 %all-to-all-start.1 = ((bf16[64,64,128]{2,1,0:T(8,128)(2,1)}), bf16[64,64,128]{2,1,0:T(8,128)(2,1)S(1)}, u32[]{:S(2)}, u32[]{:S(2)}) async-start(bf16[64,64,128]{2,1,0:T(8,128)(2,1)} %shard_map.116), calls=%async_computation.1 | async-start | bytes 2097152 | tf_op jit(solution)/shard_map/all_to_all | solution.py:379
  85.6 0.6 pad_add_fusion.me_ref
  86.2 12.0 %shard_map.114 = (bf16[512,128]{1,0:T(8,128)(2,1)}, bf16[512,128]{1,0:T(8,128)(2,1)}, bf16[512,128]{1,0:T(8,128)(2,1)}, bf16[512,128]{1,0:T(8,128)(2,1)}, bf16[5...) custom-call(s32[3]{0:T(128)} %pad_add_fusion.me_ref, ...), custom_call_target="tpu_custom_call" | custom-call | flops 8589934592 | bytes 7340032 | tf_op jit(solution)/shard_map/pallas_call | solution.py:336
  98.3 0.0 copy-start.3
  98.3 0.0 copy-start.4
  98.3 3.1 %collective-permute-start.4 = (bf16[512,128]{1,0:T(8,128)(2,1)}, bf16[512,128]{1,0:T(8,128)(2,1)S(1)}, u32[]{:S(2)}, u32[]{:S(2)}) collective-permute-start(bf16[512,128]{1,0:T(8,128)(2,1)} %get-tuple-element.19), channel_id=1, source_target_pairs={{0,1},{1,0},{2,3},{3,2},{16,17},{17,16},{18,19},{19,18},{4,5},{5,4... | collective-permute-start | bytes 393224 | tf_op jit(solution)/shard_map/ppermute | solution.py:383
  101.4 2.4 %collective-permute-start.5 = (bf16[512,128]{1,0:T(8,128)(2,1)}, bf16[512,128]{1,0:T(8,128)(2,1)S(1)}, u32[]{:S(2)}, u32[]{:S(2)}) collective-permute-start(bf16[512,128]{1,0:T(8,128)(2,1)} %get-tuple-element.20), channel_id=1, source_target_pairs={{0,2},{1,3},{2,0},{3,1},{16,18},{17,19},{18,16},{19,17},{4,6},{5,7... | collective-permute-start | bytes 393224 | tf_op jit(solution)/shard_map/ppermute | solution.py:383
  103.8 3.1 %collective-permute-start.6 = (bf16[512,128]{1,0:T(8,128)(2,1)}, bf16[512,128]{1,0:T(8,128)(2,1)S(1)}, u32[]{:S(2)}, u32[]{:S(2)}) collective-permute-start(bf16[512,128]{1,0:T(8,128)(2,1)} %get-tuple-element.21), channel_id=1, source_target_pairs={{0,3},{1,2},{2,1},{3,0},{16,19},{17,18},{18,17},{19,16},{4,7},{5,6... | collective-permute-start | bytes 393224 | tf_op jit(solution)/shard_map/ppermute | solution.py:383
  106.9 2.1 %collective-permute-start.7 = (bf16[512,128]{1,0:T(8,128)(2,1)}, bf16[512,128]{1,0:T(8,128)(2,1)S(1)}, u32[]{:S(2)}, u32[]{:S(2)}) collective-permute-start(bf16[512,128]{1,0:T(8,128)(2,1)} %get-tuple-element.22), channel_id=1, source_target_pairs={{0,16},{1,17},{2,18},{3,19},{16,0},{17,1},{18,2},{19,3},{4,20},{5,... | collective-permute-start | bytes 393224 | tf_op jit(solution)/shard_map/ppermute | solution.py:383
  109.0 3.6 %collective-permute-start.8 = (bf16[512,128]{1,0:T(8,128)(2,1)}, bf16[512,128]{1,0:T(8,128)(2,1)S(1)}, u32[]{:S(2)}, u32[]{:S(2)}) collective-permute-start(bf16[512,128]{1,0:T(8,128)(2,1)} %get-tuple-element.23), channel_id=1, source_target_pairs={{0,17},{1,16},{2,19},{3,18},{16,1},{17,0},{18,3},{19,2},{4,21},{5,... | collective-permute-start | bytes 393224 | tf_op jit(solution)/shard_map/ppermute | solution.py:383
  112.6 0.0 collective-permute-done.4.refs_1_
  112.6 2.6 %collective-permute-start.9 = (bf16[512,128]{1,0:T(8,128)(2,1)}, bf16[512,128]{1,0:T(8,128)(2,1)S(1)}, u32[]{:S(2)}, u32[]{:S(2)}) collective-permute-start(bf16[512,128]{1,0:T(8,128)(2,1)} %get-tuple-element.24), channel_id=1, source_target_pairs={{0,18},{1,19},{2,16},{3,17},{16,2},{17,3},{18,0},{19,1},{4,22},{5,... | collective-permute-start | bytes 393224 | tf_op jit(solution)/shard_map/ppermute | solution.py:383
  115.2 0.7 collective-permute-done.5.refs_2_
  115.9 3.1 %collective-permute-start.10 = (bf16[512,128]{1,0:T(8,128)(2,1)}, bf16[512,128]{1,0:T(8,128)(2,1)S(1)}, u32[]{:S(2)}, u32[]{:S(2)}) collective-permute-start(bf16[512,128]{1,0:T(8,128)(2,1)} %get-tuple-element.25), channel_id=1, source_target_pairs={{0,19},{1,18},{2,17},{3,16},{16,3},{17,2},{18,1},{19,0},{4,23},{5,... | collective-permute-start | bytes 393224 | tf_op jit(solution)/shard_map/ppermute | solution.py:383
  119.0 0.0 all-to-all-done.1.got_ref
  119.0 0.4 shard_map.117
  119.3 2.1 %collective-permute-done.6.refs_3_ = bf16[512,128]{1,0:T(8,128)(2,1)S(1)} collective-permute-done((bf16[512,128]{1,0:T(8,128)(2,1)}, bf16[512,128]{1,0:T(8,128)(2,1)S(1)}, u32[]{:S(2)}, u32[]{:S(2)}) %collective-permute-start.6) | collective-permute-done | bytes 131104 | tf_op jit(solution)/shard_map/ppermute | solution.py:383
  121.5 5.1 %collective-permute-start.11 = (f32[64,128]{1,0:T(8,128)S(1)}, f32[64,128]{1,0:T(8,128)S(1)}, u32[]{:S(2)}, u32[]{:S(2)}) collective-permute-start(f32[64,128]{1,0:T(8,128)S(1)} %shard_map.117), channel_id=1, source_target_pairs={{0,0},{1,8},{2,4},{3,12},{4,1},{5,9},{6,5},{7,13},{8,16},{9,24},{1... | collective-permute-start | bytes 98312 | tf_op jit(solution)/shard_map/ppermute | solution.py:385
  126.6 0.0 collective-permute-done.7.refs_4_
  126.6 0.0 collective-permute-done.8.refs_5_
  126.6 0.0 collective-permute-done.9.refs_6_
  126.6 0.0 collective-permute-done.10.refs_7_
  126.6 0.0 copy-done.3
  126.6 0.0 copy-done.4
  126.6 1.8 %shard_map.115 = (bf16[1,128,2048]{2,1,0:T(8,128)(2,1)}, bf16[1,128,1024]{2,1,0:T(8,128)(2,1)}, bf16[1,128,1024]{2,1,0:T(8,128)(2,1)}) custom-call(s32[3]{0:T(128)S(1)} %copy-done.4, bf16[512,128]{1,0:T(8,128)(2,1)S(1)} %copy-done.3, bf16[512,128]{1,0:T(8,128)(2,1)S(1)} %collective-permute-done.4.refs_1_, ...), custom_call_target="tpu_custom_call" | custom-call | bytes 2097152 | tf_op jit(solution)/shard_map/pallas_call | solution.py:357
  128.5 0.0 collective-permute-done.11
  128.5 0.6 copy.15
  (2 shorter events, 0.0 us)
Async XLA Ops:
  7.2 1.0 copy-start
  7.2 59.3 %all-gather.3.cloned.1.call-start = ((), (), s32[]{:S(2)}) async-start(), calls=%async_computation.2 | async-start | bytes 4718592 | tf_op jit(solution)/shard_map/all_gather | solution.py:371
  8.2 21.8 %collective-permute-start = (bf16[64,2048]{1,0:T(8,128)(2,1)S(1)}, bf16[64,2048]{1,0:T(8,128)(2,1)S(1)}, u32[]{:S(2)}, u32[]{:S(2)}) collective-permute-start(bf16[64,2048]{1,0:T(8,128)(2,1)S(1)} %constant_dynamic-slice_fusion), channel_id=1, source_target_pairs={{0,0},{8,1},{4,2},{12,3},{16,4},{24,5},{20,6},{28,7},{256,8},{264,... | collective-permute-start | bytes 786440 | tf_op jit(solution)/shard_map/ppermute | solution.py:370
  30.0 0.7 copy-start.6
  30.7 5.7 %copy-start.7 = (bf16[64,2048]{1,0:T(8,128)(2,1)S(1)}, bf16[64,2048]{1,0:T(8,128)(2,1)}, u32[]{:S(2)}) copy-start(bf16[64,2048]{1,0:T(8,128)(2,1)} %copy-done.6) | copy-start | bytes 786436
  30.7 31.4 %all-to-all-start = ((bf16[8,528,128]{2,1,0:T(8,128)(2,1)}), bf16[8,528,128]{2,1,0:T(8,128)(2,1)S(1)}, u32[]{:S(2)}, u32[]{:S(2)}) async-start(bf16[8,528,128]{2,1,0:T(8,128)(2,1)} %shard_map.112), calls=%async_computation | async-start | bytes 2162688 | tf_op jit(solution)/shard_map/all_to_all | solution.py:373
  36.4 30.0 %collective-permute-start.3 = (bf16[64,2048]{1,0:T(8,128)(2,1)S(1)}, bf16[64,2048]{1,0:T(8,128)(2,1)S(1)}, u32[]{:S(2)}, u32[]{:S(2)}) collective-permute-start(bf16[64,2048]{1,0:T(8,128)(2,1)S(1)} %copy-done.7), channel_id=1, source_target_pairs={{0,384},{128,0},{256,128},{384,256},{1,385},{129,1},{257,129},{385... | collective-permute-start | bytes 786440 | tf_op jit(solution)/shard_map/ppermute | solution.py:376
  42.8 23.7 %collective-permute-start.2 = (bf16[64,2048]{1,0:T(8,128)(2,1)S(1)}, bf16[64,2048]{1,0:T(8,128)(2,1)S(1)}, u32[]{:S(2)}, u32[]{:S(2)}) collective-permute-start(bf16[64,2048]{1,0:T(8,128)(2,1)S(1)} %copy-done.7), channel_id=1, source_target_pairs={{0,256},{128,384},{256,0},{384,128},{1,257},{129,385},{257,1},{385... | collective-permute-start | bytes 786440 | tf_op jit(solution)/shard_map/ppermute | solution.py:376
  44.7 21.8 %collective-permute-start.1 = (bf16[64,2048]{1,0:T(8,128)(2,1)S(1)}, bf16[64,2048]{1,0:T(8,128)(2,1)S(1)}, u32[]{:S(2)}, u32[]{:S(2)}) collective-permute-start(bf16[64,2048]{1,0:T(8,128)(2,1)S(1)} %copy-done.7), channel_id=1, source_target_pairs={{0,128},{128,256},{256,384},{384,0},{1,129},{129,257},{257,385},{3... | collective-permute-start | bytes 786440 | tf_op jit(solution)/shard_map/ppermute | solution.py:376
  62.1 3.5 %copy-start.1 = (bf16[8,528,128]{2,1,0:T(8,128)(2,1)}, bf16[8,528,128]{2,1,0:T(8,128)(2,1)S(1)}, u32[]{:S(2)}) copy-start(bf16[8,528,128]{2,1,0:T(8,128)(2,1)S(1)} %all-to-all-done.pay_ref) | copy-start | bytes 3244036
  65.6 0.8 copy-start.2
  66.4 5.0 %copy-start.5 = (f32[1024,128]{1,0:T(8,128)}, f32[1024,128]{1,0:T(8,128)S(1)}, u32[]{:S(2)}) copy-start(f32[1024,128]{1,0:T(8,128)S(1)} %get-tuple-element.17.lse_ref) | copy-start | bytes 1572868
  66.4 0.7 copy-start.8
  66.4 0.8 copy-start.9
  66.5 0.9 copy-start.10
  71.4 47.6 %all-to-all-start.1 = ((bf16[64,64,128]{2,1,0:T(8,128)(2,1)}), bf16[64,64,128]{2,1,0:T(8,128)(2,1)S(1)}, u32[]{:S(2)}, u32[]{:S(2)}) async-start(bf16[64,64,128]{2,1,0:T(8,128)(2,1)} %shard_map.116), calls=%async_computation.1 | async-start | bytes 2097152 | tf_op jit(solution)/shard_map/all_to_all | solution.py:379
  98.3 28.4 %copy-start.3 = (bf16[512,128]{1,0:T(8,128)(2,1)S(1)}, bf16[512,128]{1,0:T(8,128)(2,1)}, u32[]{:S(2)}) copy-start(bf16[512,128]{1,0:T(8,128)(2,1)} %get-tuple-element.18.refs_0_) | copy-start | bytes 393220
  98.3 28.4 %copy-start.4 = (s32[3]{0:T(128)S(1)}, s32[3]{0:T(128)}, u32[]{:S(2)}) copy-start(s32[3]{0:T(128)} %pad_add_fusion.me_ref) | copy-start | bytes 40
  98.3 14.3 %collective-permute-start.4 = (bf16[512,128]{1,0:T(8,128)(2,1)}, bf16[512,128]{1,0:T(8,128)(2,1)S(1)}, u32[]{:S(2)}, u32[]{:S(2)}) collective-permute-start(bf16[512,128]{1,0:T(8,128)(2,1)} %get-tuple-element.19), channel_id=1, source_target_pairs={{0,1},{1,0},{2,3},{3,2},{16,17},{17,16},{18,19},{19,18},{4,5},{5,4... | collective-permute-start | bytes 393224 | tf_op jit(solution)/shard_map/ppermute | solution.py:383
  101.4 14.4 %collective-permute-start.5 = (bf16[512,128]{1,0:T(8,128)(2,1)}, bf16[512,128]{1,0:T(8,128)(2,1)S(1)}, u32[]{:S(2)}, u32[]{:S(2)}) collective-permute-start(bf16[512,128]{1,0:T(8,128)(2,1)} %get-tuple-element.20), channel_id=1, source_target_pairs={{0,2},{1,3},{2,0},{3,1},{16,18},{17,19},{18,16},{19,17},{4,6},{5,7... | collective-permute-start | bytes 393224 | tf_op jit(solution)/shard_map/ppermute | solution.py:383
  103.8 17.6 %collective-permute-start.6 = (bf16[512,128]{1,0:T(8,128)(2,1)}, bf16[512,128]{1,0:T(8,128)(2,1)S(1)}, u32[]{:S(2)}, u32[]{:S(2)}) collective-permute-start(bf16[512,128]{1,0:T(8,128)(2,1)} %get-tuple-element.21), channel_id=1, source_target_pairs={{0,3},{1,2},{2,1},{3,0},{16,19},{17,18},{18,17},{19,16},{4,7},{5,6... | collective-permute-start | bytes 393224 | tf_op jit(solution)/shard_map/ppermute | solution.py:383
  106.9 19.7 %collective-permute-start.7 = (bf16[512,128]{1,0:T(8,128)(2,1)}, bf16[512,128]{1,0:T(8,128)(2,1)S(1)}, u32[]{:S(2)}, u32[]{:S(2)}) collective-permute-start(bf16[512,128]{1,0:T(8,128)(2,1)} %get-tuple-element.22), channel_id=1, source_target_pairs={{0,16},{1,17},{2,18},{3,19},{16,0},{17,1},{18,2},{19,3},{4,20},{5,... | collective-permute-start | bytes 393224 | tf_op jit(solution)/shard_map/ppermute | solution.py:383
  109.0 17.6 %collective-permute-start.8 = (bf16[512,128]{1,0:T(8,128)(2,1)}, bf16[512,128]{1,0:T(8,128)(2,1)S(1)}, u32[]{:S(2)}, u32[]{:S(2)}) collective-permute-start(bf16[512,128]{1,0:T(8,128)(2,1)} %get-tuple-element.23), channel_id=1, source_target_pairs={{0,17},{1,16},{2,19},{3,18},{16,1},{17,0},{18,3},{19,2},{4,21},{5,... | collective-permute-start | bytes 393224 | tf_op jit(solution)/shard_map/ppermute | solution.py:383
  112.6 14.0 %collective-permute-start.9 = (bf16[512,128]{1,0:T(8,128)(2,1)}, bf16[512,128]{1,0:T(8,128)(2,1)S(1)}, u32[]{:S(2)}, u32[]{:S(2)}) collective-permute-start(bf16[512,128]{1,0:T(8,128)(2,1)} %get-tuple-element.24), channel_id=1, source_target_pairs={{0,18},{1,19},{2,16},{3,17},{16,2},{17,3},{18,0},{19,1},{4,22},{5,... | collective-permute-start | bytes 393224 | tf_op jit(solution)/shard_map/ppermute | solution.py:383
  115.9 10.7 %collective-permute-start.10 = (bf16[512,128]{1,0:T(8,128)(2,1)}, bf16[512,128]{1,0:T(8,128)(2,1)S(1)}, u32[]{:S(2)}, u32[]{:S(2)}) collective-permute-start(bf16[512,128]{1,0:T(8,128)(2,1)} %get-tuple-element.25), channel_id=1, source_target_pairs={{0,19},{1,18},{2,17},{3,16},{16,3},{17,2},{18,1},{19,0},{4,23},{5,... | collective-permute-start | bytes 393224 | tf_op jit(solution)/shard_map/ppermute | solution.py:383
  121.5 7.0 %collective-permute-start.11 = (f32[64,128]{1,0:T(8,128)S(1)}, f32[64,128]{1,0:T(8,128)S(1)}, u32[]{:S(2)}, u32[]{:S(2)}) collective-permute-start(f32[64,128]{1,0:T(8,128)S(1)} %shard_map.117), channel_id=1, source_target_pairs={{0,0},{1,8},{2,4},{3,12},{4,1},{5,9},{6,5},{7,13},{8,16},{9,24},{1... | collective-permute-start | bytes 98312 | tf_op jit(solution)/shard_map/ppermute | solution.py:385
Sparse Core Ops, SparseCore 0:
  10.2 54.4 all-gather.2
